TPU v7x, 32 devices: a whole 2x2x4 slice. The times are simulated.
32 devices in a mesh: row: 8 (over y, x, core), col: 4 (over z).
Axes of the slice: x: 2, y: 2, z: 4, core: 2. Of those that a mesh axis runs over, the one named last changes fastest.
Arguments:
- images: float32 [32, 197, 768], P(('row', 'col')), may hold values from -6 to 6
- cotangent: float32 [32, 197, 768], P(('row', 'col')), may hold values from -6 to 6
- counts: int32 [8], replicated, may hold values from 1 to 4, as said below
- w_qkv: float32 [2, 768, 2304], P(None, 'row', 'col'), may hold values from -2 to 2
- w_out: float32 [2, 768, 768], P(None, 'col', 'row'), may hold values from -1.5 to 1.5
- w_up: float32 [2, 768, 3072], P(None, 'row', 'col'), may hold values from -0.21875 to 0.21875
- w_down: float32 [2, 3072, 768], P(None, 'col', 'row'), may hold values from -0.109375 to 0.109375
- norm_gains: float32 [2, 2, 768], replicated, may hold values from 0.5 to 1.5
- res_biases: float32 [2, 2, 768], replicated, may hold values from -1.5 to 1.5
- b_up: float32 [2, 3072], replicated, may hold values from -1.5 to 1.5
- m_qkv: float32 [2, 768, 2304], P(None, 'row', 'col'), may hold values from -60 to 60
- m_out: float32 [2, 768, 768], P(None, 'col', 'row'), may hold values from -60 to 60
- m_up: float32 [2, 768, 3072], P(None, 'row', 'col'), may hold values from -60 to 60
- m_down: float32 [2, 3072, 768], P(None, 'col', 'row'), may hold values from -60 to 60
- m_gains: float32 [2, 2, 768], replicated, may hold values from -60 to 60
- m_biases: float32 [2, 2, 768], replicated, may hold values from -60 to 60
- m_bup: float32 [2, 3072], replicated, may hold values from -60 to 60
- v_qkv: float32 [2, 768, 2304], P(None, 'row', 'col'), may hold values from 0.5 to 20
- v_out: float32 [2, 768, 768], P(None, 'col', 'row'), may hold values from 0.5 to 20
- v_up: float32 [2, 768, 3072], P(None, 'row', 'col'), may hold values from 0.5 to 20
- v_down: float32 [2, 3072, 768], P(None, 'col', 'row'), may hold values from 0.5 to 20
- v_gains: float32 [2, 2, 768], replicated, may hold values from 0.5 to 20
- v_biases: float32 [2, 2, 768], replicated, may hold values from 0.5 to 20
- v_bup: float32 [2, 3072], replicated, may hold values from 0.5 to 20
Outputs:
- layer_out: float32 [32, 197, 768], P(('row', 'col'))
- grad_images: float32 [32, 197, 768], P(('row', 'col'))
- grad_qkv: float32 [2, 768, 2304], P(None, 'row', 'col')
- grad_out: float32 [2, 768, 768], P(None, 'col', 'row')
- grad_up: float32 [2, 768, 3072], P(None, 'row', 'col')
- grad_down: float32 [2, 3072, 768], P(None, 'col', 'row')
- grad_gains: float32 [2, 2, 768], replicated
- grad_biases: float32 [2, 2, 768], replicated
- grad_bup: float32 [2, 3072], replicated
- new_qkv: float32 [2, 768, 2304], P(None, 'row', 'col')
- new_out: float32 [2, 768, 768], P(None, 'col', 'row')
- new_up: float32 [2, 768, 3072], P(None, 'row', 'col')
- new_down: float32 [2, 3072, 768], P(None, 'col', 'row')
- fresh_m_qkv: float32 [2, 768, 2304], P(None, 'row', 'col')
- fresh_m_out: float32 [2, 768, 768], P(None, 'col', 'row')
- fresh_m_up: float32 [2, 768, 3072], P(None, 'row', 'col')
- fresh_m_down: float32 [2, 3072, 768], P(None, 'col', 'row')
- fresh_m_gains: float32 [2, 2, 768], replicated
- fresh_m_biases: float32 [2, 2, 768], replicated
- fresh_m_bup: float32 [2, 3072], replicated
- fresh_v_qkv: float32 [2, 768, 2304], P(None, 'row', 'col')
- fresh_v_out: float32 [2, 768, 768], P(None, 'col', 'row')
- fresh_v_up: float32 [2, 768, 3072], P(None, 'row', 'col')
- fresh_v_down: float32 [2, 3072, 768], P(None, 'col', 'row')
- fresh_v_gains: float32 [2, 2, 768], replicated
- fresh_v_biases: float32 [2, 2, 768], replicated
- fresh_v_bup: float32 [2, 3072], replicated
Inputs may be any that keep to these rules, and one draw needn't show every extreme that they name: Row group g holds counts[g] real images, in slots g * 4 to g * 4 + counts[g] - 1; its other slots are padding. Some group is full in every draw.
All inputs are finite; a program needn't handle non-finite values.
Results may differ from a plain program's by a relative error of at most 0.023.
Values may be sent and summed in bfloat16 or wider, within the bound.
No kernel may reach another device: no remote copies, remote signals or barrier semaphores. Data moves between devices by JAX's collectives and lax.ppermute only.
A program may use at most 192 MiB of HBM per device.

v0:
```python
import jax
import jax.numpy as jnp
from jax import lax
from jax.sharding import PartitionSpec as P

HEADS = 12
LAYERS = 2
STEP = 3


norm_eps = 1e-06
root_half = 0.7071067811865476
inv_root_two_pi = 0.3989422804014327
beta_one = 0.9
beta_two = 0.999
adam_eps = 1e-08
learn_rate = 0.06
decay_rate = 0.05


def normalize(tokens, gain):
    center = jnp.mean(tokens, axis=-1, keepdims=True)
    shifted = tokens - center
    inverse = lax.rsqrt(jnp.mean(shifted * shifted, axis=-1, keepdims=True) + norm_eps)
    scaled = shifted * inverse
    return (scaled, inverse, (scaled * gain).astype(jnp.bfloat16))


def norm_back(upstream, scaled, inverse, gain):
    grad_scaled = upstream * gain
    grad_gain = jnp.sum(upstream * scaled, axis=0)
    mean_one = jnp.mean(grad_scaled, axis=-1, keepdims=True)
    mean_two = jnp.mean(grad_scaled * scaled, axis=-1, keepdims=True)
    return (inverse * (grad_scaled - mean_one - scaled * mean_two), grad_gain)


def gelu_value(pre_act):
    return pre_act * 0.5 * (1.0 + lax.erf(pre_act * root_half))


def gelu_slope(pre_act):
    return 0.5 * (1.0 + lax.erf(pre_act * root_half)) + pre_act * inv_root_two_pi * jnp.exp(
        -0.5 * pre_act * pre_act
    )


def split_heads(packed, head_count):
    seq_len = packed.shape[0]
    model_width = packed.shape[1] // 3
    head_size = model_width // head_count
    query_part = packed[:, :model_width].reshape(seq_len, head_count, head_size)
    key_part = packed[:, model_width : 2 * model_width].reshape(seq_len, head_count, head_size)
    value_part = packed[:, 2 * model_width :].reshape(seq_len, head_count, head_size)
    return (query_part, key_part, value_part)


def attend(packed, head_count):
    query_part, key_part, value_part = split_heads(packed, head_count)
    score_scale = query_part.shape[2] ** (-0.5)
    scores = (
        jnp.einsum("qhd,khd->hqk", query_part, key_part, preferred_element_type=jnp.float32)
        * score_scale
    )
    row_peak = jnp.max(scores, axis=-1, keepdims=True)
    row_total = jnp.sum(jnp.exp(scores - row_peak), axis=-1, keepdims=True)
    logsum = row_peak + jnp.log(row_total)
    attn_probs = jnp.exp(scores - logsum).astype(jnp.bfloat16)
    attn_mixed = jnp.einsum(
        "hqk,khd->qhd", attn_probs, value_part, preferred_element_type=jnp.float32
    )
    return (attn_mixed.reshape(packed.shape[0], -1).astype(jnp.bfloat16), logsum)


def attend_back(packed, logsum, grad_mixed, head_count):
    query_part, key_part, value_part = split_heads(packed, head_count)
    seq_len = packed.shape[0]
    score_scale = query_part.shape[2] ** (-0.5)
    scores = (
        jnp.einsum("qhd,khd->hqk", query_part, key_part, preferred_element_type=jnp.float32)
        * score_scale
    )
    attn_probs = jnp.exp(scores - logsum)
    probs_low = attn_probs.astype(jnp.bfloat16)
    grad_heads = grad_mixed.reshape(seq_len, head_count, -1)
    grad_values = jnp.einsum(
        "hqk,qhd->khd", probs_low, grad_heads, preferred_element_type=jnp.float32
    )
    grad_probs = jnp.einsum(
        "qhd,khd->hqk", grad_heads, value_part, preferred_element_type=jnp.float32
    )
    inner_sum = jnp.sum(attn_probs * grad_probs, axis=-1, keepdims=True)
    grad_scores = (attn_probs * (grad_probs - inner_sum) * score_scale).astype(jnp.bfloat16)
    grad_query = jnp.einsum(
        "hqk,khd->qhd", grad_scores, key_part, preferred_element_type=jnp.float32
    )
    grad_keys = jnp.einsum(
        "hqk,qhd->khd", grad_scores, query_part, preferred_element_type=jnp.float32
    )
    joined = jnp.concatenate(
        [
            grad_query.reshape(seq_len, -1),
            grad_keys.reshape(seq_len, -1),
            grad_values.reshape(seq_len, -1),
        ],
        axis=1,
    )
    return joined.astype(jnp.bfloat16)


def group_rows(tokens_low):
    return lax.all_gather(tokens_low, "col", axis=0, tiled=True)


def summed_rows(left_rows, right_matrix, transposed):
    if transposed:
        partial_term = lax.dot_general(
            left_rows, right_matrix, (((1,), (1,)), ((), ())), preferred_element_type=jnp.float32
        )
    else:
        partial_term = jnp.dot(left_rows, right_matrix, preferred_element_type=jnp.float32)
    return lax.psum_scatter(partial_term, "col", scatter_dimension=0, tiled=True)


def contract_rows(left_rows, right_rows):
    return lax.dot_general(
        left_rows, right_rows, (((0,), (0,)), ((), ())), preferred_element_type=jnp.float32
    )


def contract_cols(left_rows, right_rows):
    return lax.dot_general(
        left_rows, right_rows, (((1,), (1,)), ((), ())), preferred_element_type=jnp.float32
    )


def adamw_step(param, gradient, first_moment, second_moment):
    fresh_first = beta_one * first_moment + (1.0 - beta_one) * gradient
    fresh_second = beta_two * second_moment + (1.0 - beta_two) * gradient * gradient
    first_hat = fresh_first / (1.0 - beta_one**STEP)
    second_hat = fresh_second / (1.0 - beta_two**STEP)
    updated = param - learn_rate * (
        first_hat / (jnp.sqrt(second_hat) + adam_eps) + decay_rate * param
    )
    return (updated, fresh_first, fresh_second)


def per_device(
    images,
    cotangent,
    counts,
    w_qkv,
    w_out,
    w_up,
    w_down,
    norm_gains,
    res_biases,
    b_up,
    m_qkv,
    m_out,
    m_up,
    m_down,
    m_gains,
    m_biases,
    m_bup,
    v_qkv,
    v_out,
    v_up,
    v_down,
    v_gains,
    v_biases,
    v_bup,
):
    row_index = lax.axis_index("row")
    col_index = lax.axis_index("col")
    group_count = jnp.sum(
        jnp.where(jnp.arange(counts.shape[0], dtype=jnp.int32) == row_index, counts, 0)
    )
    live_mask = (col_index < group_count).astype(jnp.float32)
    hidden = images[0]
    hidden_block = w_up.shape[2]
    full_hidden = b_up.shape[1]
    saved = []
    for level in range(LAYERS):
        lowered = (
            w_qkv[level].astype(jnp.bfloat16),
            w_out[level].astype(jnp.bfloat16),
            w_up[level].astype(jnp.bfloat16),
            w_down[level].astype(jnp.bfloat16),
        )
        full_qkv, full_out, full_up, full_down = (
            lax.all_gather(lowered[0], "row", axis=0, tiled=True),
            lax.all_gather(lowered[1], "row", axis=1, tiled=True),
            lax.all_gather(lowered[2], "row", axis=0, tiled=True),
            lax.all_gather(lowered[3], "row", axis=1, tiled=True),
        )
        gain_pair = norm_gains[level]
        bias_pair = res_biases[level]
        scaled_one, inverse_one, normed_one = normalize(hidden, gain_pair[0])
        group_one = group_rows(normed_one)
        packed_cols = jnp.dot(group_one, full_qkv, preferred_element_type=jnp.float32).astype(
            jnp.bfloat16
        )
        packed = lax.all_to_all(packed_cols, "col", split_axis=0, concat_axis=1, tiled=True)
        attn_mixed, logsum = attend(packed, HEADS)
        out_matrix = lax.all_gather(full_out, "col", axis=0, tiled=True)
        mixed_cols = attn_mixed
        attn_term = jnp.dot(attn_mixed, out_matrix, preferred_element_type=jnp.float32)
        middle = hidden + attn_term + bias_pair[0]
        scaled_two, inverse_two, normed_two = normalize(middle, gain_pair[1])
        ffn_up, ffn_down = (full_up, full_down)
        up_bias = lax.dynamic_slice_in_dim(b_up[level], col_index * hidden_block, hidden_block, 0)
        group_two = group_rows(normed_two)
        pre_act = jnp.dot(group_two, full_up, preferred_element_type=jnp.float32) + up_bias
        active = gelu_value(pre_act).astype(jnp.bfloat16)
        hidden = middle + summed_rows(active, full_down, False) + bias_pair[1]
        saved.append(
            (
                full_qkv,
                out_matrix,
                ffn_up,
                ffn_down,
                gain_pair,
                scaled_one,
                inverse_one,
                group_one,
                packed,
                logsum,
                attn_mixed,
                mixed_cols,
                scaled_two,
                inverse_two,
                group_two,
                pre_act,
                active,
            )
        )
    layer_out = (hidden * live_mask)[None]
    upstream = cotangent[0] * live_mask
    collected = []
    for level in reversed(range(LAYERS)):
        (
            full_qkv,
            out_matrix,
            ffn_up,
            ffn_down,
            gain_pair,
            scaled_one,
            inverse_one,
            group_one,
            packed,
            logsum,
            attn_mixed,
            mixed_cols,
            scaled_two,
            inverse_two,
            group_two,
            pre_act,
            active,
        ) = saved[level]
        up_low = upstream.astype(jnp.bfloat16)
        grad_res_two = jnp.sum(upstream, axis=0)
        up_group = group_rows(up_low)
        grad_down = contract_rows(active, up_group)
        grad_pre = contract_cols(up_group, ffn_down) * gelu_slope(pre_act)
        pre_low = grad_pre.astype(jnp.bfloat16)
        bup_part = jnp.sum(grad_pre, axis=0)
        bup_full = lax.dynamic_update_slice_in_dim(
            jnp.zeros((full_hidden,), jnp.float32), bup_part, col_index * hidden_block, 0
        )
        grad_up = contract_rows(group_two, pre_low)
        grad_normed_two = summed_rows(pre_low, ffn_up, True)
        grad_middle, gain_two = norm_back(grad_normed_two, scaled_two, inverse_two, gain_pair[1])
        grad_middle = grad_middle + upstream
        grad_res_one = jnp.sum(grad_middle, axis=0)
        middle_low = grad_middle.astype(jnp.bfloat16)
        grad_square = contract_rows(attn_mixed, middle_low)
        grad_out = lax.psum_scatter(
            grad_square.astype(jnp.bfloat16), "col", scatter_dimension=0, tiled=True
        )
        grad_mixed = contract_cols(middle_low, out_matrix).astype(jnp.bfloat16)
        grad_packed = attend_back(packed, logsum, grad_mixed, HEADS)
        grad_packed_cols = lax.all_to_all(
            grad_packed, "col", split_axis=1, concat_axis=0, tiled=True
        )
        grad_qkv = contract_rows(group_one, grad_packed_cols)
        grad_normed_one = summed_rows(grad_packed_cols, full_qkv, True)
        grad_below, gain_one = norm_back(grad_normed_one, scaled_one, inverse_one, gain_pair[0])
        upstream = grad_middle + grad_below
        reduced = (
            lax.psum_scatter(
                grad_qkv.astype(jnp.bfloat16), "row", scatter_dimension=0, tiled=True
            ).astype(jnp.float32),
            lax.psum_scatter(grad_out, "row", scatter_dimension=1, tiled=True).astype(jnp.float32),
            lax.psum_scatter(
                grad_up.astype(jnp.bfloat16), "row", scatter_dimension=0, tiled=True
            ).astype(jnp.float32),
            lax.psum_scatter(
                grad_down.astype(jnp.bfloat16), "row", scatter_dimension=1, tiled=True
            ).astype(jnp.float32),
        )
        small_sums = lax.psum(
            (jnp.stack([gain_one, gain_two]), jnp.stack([grad_res_one, grad_res_two]), bup_full),
            ("row", "col"),
        )
        collected.insert(
            0,
            (
                reduced[0],
                reduced[1],
                reduced[2],
                reduced[3],
                small_sums[0],
                small_sums[1],
                small_sums[2],
            ),
        )
    grad_list = [jnp.stack([entry[index] for entry in collected]) for index in range(7)]
    params = [w_qkv, w_out, w_up, w_down, norm_gains, res_biases, b_up]
    firsts = [m_qkv, m_out, m_up, m_down, m_gains, m_biases, m_bup]
    seconds = [v_qkv, v_out, v_up, v_down, v_gains, v_biases, v_bup]
    results = [
        adamw_step(params[index], grad_list[index], firsts[index], seconds[index])
        for index in range(7)
    ]
    return (
        layer_out,
        upstream[None],
        grad_list[0],
        grad_list[1],
        grad_list[2],
        grad_list[3],
        grad_list[4],
        grad_list[5],
        grad_list[6],
        results[0][0],
        results[1][0],
        results[2][0],
        results[3][0],
        results[0][1],
        results[1][1],
        results[2][1],
        results[3][1],
        results[4][1],
        results[5][1],
        results[6][1],
        results[0][2],
        results[1][2],
        results[2][2],
        results[3][2],
        results[4][2],
        results[5][2],
        results[6][2],
    )


def solution(mesh):
    in_specs = (
        P(("row", "col"), None, None),
        P(("row", "col"), None, None),
        P(),
        P(None, "row", "col"),
        P(None, "col", "row"),
        P(None, "row", "col"),
        P(None, "col", "row"),
        P(),
        P(),
        P(),
        P(None, "row", "col"),
        P(None, "col", "row"),
        P(None, "row", "col"),
        P(None, "col", "row"),
        P(),
        P(),
        P(),
        P(None, "row", "col"),
        P(None, "col", "row"),
        P(None, "row", "col"),
        P(None, "col", "row"),
        P(),
        P(),
        P(),
    )
    out_specs = (
        P(("row", "col"), None, None),
        P(("row", "col"), None, None),
        P(None, "row", "col"),
        P(None, "col", "row"),
        P(None, "row", "col"),
        P(None, "col", "row"),
        P(),
        P(),
        P(),
        P(None, "row", "col"),
        P(None, "col", "row"),
        P(None, "row", "col"),
        P(None, "col", "row"),
        P(None, "row", "col"),
        P(None, "col", "row"),
        P(None, "row", "col"),
        P(None, "col", "row"),
        P(),
        P(),
        P(),
        P(None, "row", "col"),
        P(None, "col", "row"),
        P(None, "row", "col"),
        P(None, "col", "row"),
        P(),
        P(),
        P(),
    )
    return jax.shard_map(
        per_device, mesh=mesh, in_specs=in_specs, out_specs=out_specs, check_vma=False
    )
```

profile of v0, /device:TPU:0, one launch (start us, length us, event | category | flops | bytes accessed | tf_op | source)
XLA Modules:
  0.0 1059.1 jit_solution(16471304933701530794)
XLA Ops:
  14.2 12.3 %all-gather = bf16[1,768,576]{2,1,0:T(8,128)(2,1)S(1)} all-gather(bf16[1,96,576]{2,1,0:T(8,128)(2,1)S(1)} %get-tuple-element.231), channel_id=2, replica_groups=mesh['row'=8,'col'=4] {'row'}, dimensions={1}, use_global_device_ids=true | all-gather | bytes 995328 | tf_op jit(solution)/shard_map/all_gather | solution.py:191
  26.5 21.2 %all-gather.41.cloned.1.call-done = bf16[4,197,768]{2,1,0:T(8,128)(2,1)} async-done(((bf16[1,197,768]{2,1,0:T(8,128)(2,1)}), bf16[4,197,768]{2,1,0:T(8,128)(2,1)}) %all-gather.41.cloned.1.call-update) | async-done | bytes 1210384 | tf_op jit(solution)/shard_map/all_gather | solution.py:111
  56.5 10.4 all-gather.1
  69.1 11.3 %all-to-all-done = bf16[4,197,576]{2,1,0:T(8,128)(2,1)S(1)} async-done(((bf16[4,197,576]{2,1,0:T(8,128)(2,1)}), bf16[4,197,576]{2,1,0:T(8,128)(2,1)S(1)}, u32[]{:S(2)}, u32[]{:S(2)}) %all-to-all-start) | async-done | bytes 907808 | tf_op jit(solution)/shard_map/all_to_all | solution.py:203
  86.9 12.8 %all-gather.29.cloned.1.call-done = bf16[1,768,768]{2,1,0:T(8,128)(2,1)} async-done(((bf16[1,192,768]{2,1,0:T(8,128)(2,1)}), bf16[1,768,768]{2,1,0:T(8,128)(2,1)}) %all-gather.29.cloned.1.call-update) | async-done | bytes 1179664 | tf_op jit(solution)/shard_map/all_gather | solution.py:205
  107.7 25.7 %all-gather.43.cloned.1.call-done = bf16[4,197,768]{2,1,0:T(8,128)(2,1)} async-done(((bf16[1,197,768]{2,1,0:T(8,128)(2,1)}), bf16[4,197,768]{2,1,0:T(8,128)(2,1)}) %all-gather.43.cloned.1.call-update) | async-done | bytes 1210384 | tf_op jit(solution)/shard_map/all_gather | solution.py:111
  136.1 22.8 %all-gather.31.cloned.1.call-done = bf16[1,768,768]{2,1,0:T(8,128)(2,1)} async-done(((bf16[1,96,768]{2,1,0:T(8,128)(2,1)}), bf16[1,768,768]{2,1,0:T(8,128)(2,1)}) %all-gather.31.cloned.1.call-update) | async-done | bytes 1179664 | tf_op jit(solution)/shard_map/all_gather | solution.py:193
  158.9 4.6 multiply_convert_fusion.3
  163.5 21.8 %all-gather.33.cloned.1.call-done = bf16[1,768,768]{1,2,0:T(8,128)(2,1)} async-done(((bf16[1,768,96]{1,2,0:T(8,128)(2,1)}), bf16[1,768,768]{1,2,0:T(8,128)(2,1)}) %all-gather.33.cloned.1.call-update) | async-done | bytes 1179664 | tf_op jit(solution)/shard_map/all_gather | solution.py:194
  189.5 50.4 %fusion = f32[200,768]{1,0:T(8,128)} fusion(f32[788,768]{1,0:T(8,128)} %fusion.62), kind=kCustom, calls=%all-reduce-scatter | all-reduce-scatter fusion | flops 614401 | bytes 3035648
  252.0 11.3 %all-gather.6 = bf16[1,192,768]{1,0,2:T(2,128)(2,1)} all-gather(bf16[1,192,96]{1,0,2:T(2,128)(2,1)} %get-tuple-element.232), channel_id=8, replica_groups=mesh['row'=8,'col'=4] {'row'}, dimensions={2}, use_global_device_ids=true | all-gather | bytes 331776 | tf_op jit(solution)/shard_map/all_gather | solution.py:192
  266.2 12.5 %all-gather.5 = bf16[1,768,576]{2,1,0:T(8,128)(2,1)} all-gather(bf16[1,96,576]{2,1,0:T(8,128)(2,1)} %get-tuple-element.230), channel_id=7, replica_groups=mesh['row'=8,'col'=4] {'row'}, dimensions={1}, use_global_device_ids=true | all-gather | bytes 995328 | tf_op jit(solution)/shard_map/all_gather | solution.py:191
  299.1 37.1 %all-to-all-done.1 = bf16[4,197,576]{2,1,0:T(8,128)(2,1)} async-done(((bf16[4,197,576]{2,1,0:T(8,128)(2,1)}), bf16[4,197,576]{2,1,0:T(8,128)(2,1)}, u32[]{:S(2)}, u32[]{:S(2)}) %all-to-all-start.1) | async-done | bytes 907808 | tf_op jit(solution)/shard_map/all_to_all | solution.py:203
  359.8 5.3 all-gather.49.cloned.1.call-done
  367.8 29.9 %all-gather.47.cloned.1.call-done = bf16[4,197,768]{2,1,0:T(8,128)(2,1)} async-done(((bf16[1,197,768]{2,1,0:T(8,128)(2,1)}), bf16[4,197,768]{2,1,0:T(8,128)(2,1)}) %all-gather.47.cloned.1.call-update) | async-done | bytes 1210384 | tf_op jit(solution)/shard_map/all_gather | solution.py:111
  400.4 22.8 %all-gather.37.cloned.1.call-done = bf16[1,768,768]{2,1,0:T(8,128)(2,1)} async-done(((bf16[1,96,768]{2,1,0:T(8,128)(2,1)}), bf16[1,768,768]{2,1,0:T(8,128)(2,1)}) %all-gather.37.cloned.1.call-update) | async-done | bytes 1179664 | tf_op jit(solution)/shard_map/all_gather | solution.py:193
  423.2 4.6 multiply_convert_fusion.2
  427.8 21.9 %all-gather.39.cloned.1.call-done = bf16[1,768,768]{1,2,0:T(8,128)(2,1)} async-done(((bf16[1,768,96]{1,2,0:T(8,128)(2,1)}), bf16[1,768,768]{1,2,0:T(8,128)(2,1)}) %all-gather.39.cloned.1.call-update) | async-done | bytes 1179664 | tf_op jit(solution)/shard_map/all_gather | solution.py:194
  449.7 4.8 fusion.148
  458.2 50.3 %fusion.2 = f32[200,768]{1,0:T(8,128)} fusion(f32[788,768]{1,0:T(8,128)} %fusion.55), kind=kCustom, calls=%all-reduce-scatter.2 | all-reduce-scatter fusion | flops 614401 | bytes 3035648
  527.2 6.0 fusion.42
  533.2 6.0 fusion.45
  563.1 38.3 %all-to-all-done.2 = bf16[197,4,576]{2,0,1:T(8,128)(2,1)} async-done(((bf16[197,4,576]{2,0,1:T(8,128)(2,1)}), bf16[197,4,576]{2,0,1:T(8,128)(2,1)}, u32[]{:S(2)}, u32[]{:S(2)}) %all-to-all-start.2) | async-done | bytes 907808 | tf_op jit(solution)/shard_map/all_to_all | solution.py:282
  608.2 43.9 %fusion.3 = f32[200,768]{1,0:T(8,128)} fusion(f32[788,768]{1,0:T(8,128)} %fusion.72), kind=kCustom, calls=%all-reduce-scatter.3 | all-reduce-scatter fusion | flops 614401 | bytes 3035648
  671.4 24.6 %all-gather.51.cloned.1.call-done = bf16[4,197,768]{2,1,0:T(8,128)(2,1)} async-done(((bf16[1,197,768]{2,1,0:T(8,128)(2,1)}), bf16[4,197,768]{2,1,0:T(8,128)(2,1)}) %all-gather.51.cloned.1.call-update) | async-done | bytes 1210384 | tf_op jit(solution)/shard_map/all_gather | solution.py:111
  710.8 48.6 %fusion.4 = f32[200,768]{1,0:T(8,128)} fusion(f32[788,768]{1,0:T(8,128)} %fusion.64), kind=kCustom, calls=%all-reduce-scatter.4 | all-reduce-scatter fusion | flops 614401 | bytes 3035648
  789.6 4.5 fusion.36
  794.1 4.7 fusion.39
  820.8 32.3 %all-to-all-done.3 = bf16[197,4,576]{2,0,1:T(8,128)(2,1)S(1)} async-done(((bf16[197,4,576]{2,0,1:T(8,128)(2,1)}), bf16[197,4,576]{2,0,1:T(8,128)(2,1)S(1)}, u32[]{:S(2)}, u32[]{:S(2)}) %all-to-all-start.3) | async-done | bytes 907808 | tf_op jit(solution)/shard_map/all_to_all | solution.py:282
  858.5 84.0 %fusion.129 = (f32[200,768]{1,0:T(8,128)S(1)}, f32[200,768]{1,0:T(8,128)S(1)}) fusion(f32[788,768]{1,0:T(8,128)} %fusion.53, f32[788,768]{1,0:T(8,128)} %fusion.75), kind=kCustom, calls=%all-reduce-scatter.6 | all-reduce-scatter fusion | flops 1228801 | bytes 6070784
  952.5 41.4 %all-reduce.12 = (f32[1,2,768]{2,1,0:T(2,128)S(1)}, f32[1,2,768]{2,1,0:T(2,128)S(1)}, f32[1,2,768]{2,1,0:T(2,128)S(1)}, f32[1,2,768]{2,1,0:T(2,128)S(1)}, f32[1,3072]{1,0:T(1,128)S(1)}, /*index=5*/f32[1,3072]{1,0:T(1,128)S(1)}) all-reduce(f32[1,2,768]{2,1,0:T(2,128)S(1)} %maximum_bitcast_fusion, ...), channel_id=1, replica_groups=mesh['row'=8,'col'=4] {'row','col'}, use_global_device_ids=true, to_apply=%region_41.42 | all-reduce | flops 12288 | bytes 98304 | tf_op jit(solution)/shard_map/psum | solution.py:301
  1015.3 34.6 %reduce-scatter.43.cloned.1.call-done = bf16[96,192]{1,0:T(8,128)(2,1)} async-done(((bf16[768,192]{1,0:T(8,128)(2,1)}), bf16[96,192]{1,0:T(8,128)(2,1)}) %reduce-scatter.43.cloned.1.call-update) | async-done | bytes 36880
  (355 shorter events, 279.1 us)
Async XLA Ops:
  7.2 40.4 %all-gather.41.cloned.1.call-start = ((), (), s32[]{:S(2)}) async-start(), calls=%async_computation.28 | async-start | bytes 1536000 | tf_op jit(solution)/shard_map/all_gather | solution.py:111
  51.9 28.6 %all-to-all-start = ((bf16[4,197,576]{2,1,0:T(8,128)(2,1)}), bf16[4,197,576]{2,1,0:T(8,128)(2,1)S(1)}, u32[]{:S(2)}, u32[]{:S(2)}) async-start(bf16[4,197,576]{2,1,0:T(8,128)(2,1)} %all_to_all.52), calls=%async_computation | async-start | bytes 2048000 | tf_op jit(solution)/shard_map/all_to_all | solution.py:203
  55.5 44.2 %all-gather.29.cloned.1.call-start = ((), (), s32[]{:S(2)}) async-start(), calls=%async_computation.22 | async-start | bytes 1474560 | tf_op jit(solution)/shard_map/all_gather | solution.py:205
  68.5 65.0 %all-gather.43.cloned.1.call-start = ((), (), s32[]{:S(2)}) async-start(), calls=%async_computation.29 | async-start | bytes 1536000 | tf_op jit(solution)/shard_map/all_gather | solution.py:111
  102.9 56.0 %all-gather.31.cloned.1.call-start = ((), (), s32[]{:S(2)}) async-start(), calls=%async_computation.23 | async-start | bytes 1327104 | tf_op jit(solution)/shard_map/all_gather | solution.py:193
  104.9 80.4 %all-gather.33.cloned.1.call-start = ((), (), s32[]{:S(2)}) async-start(), calls=%async_computation.24 | async-start | bytes 1327104 | tf_op jit(solution)/shard_map/all_gather | solution.py:194
  106.8 175.8 %all-gather.45.cloned.1.call-start = ((), (), s32[]{:S(2)}) async-start(), calls=%async_computation.30 | async-start | bytes 1536000 | tf_op jit(solution)/shard_map/all_gather | solution.py:111
  241.4 3.3 collective-permute-start
  252.0 102.0 %all-gather.35.cloned.1.call-start = ((), (), s32[]{:S(2)}) async-start(), calls=%async_computation.25 | async-start | bytes 1474560 | tf_op jit(solution)/shard_map/all_gather | solution.py:205
  291.6 44.6 %all-to-all-start.1 = ((bf16[4,197,576]{2,1,0:T(8,128)(2,1)}), bf16[4,197,576]{2,1,0:T(8,128)(2,1)}, u32[]{:S(2)}, u32[]{:S(2)}) async-start(bf16[4,197,576]{2,1,0:T(8,128)(2,1)} %all_to_all.56), calls=%async_computation.1 | async-start | bytes 2048000 | tf_op jit(solution)/shard_map/all_to_all | solution.py:203
  295.8 69.3 %all-gather.49.cloned.1.call-start = ((), (), s32[]{:S(2)}) async-start(), calls=%async_computation.32 | async-start | bytes 1536000 | tf_op jit(solution)/shard_map/all_gather | solution.py:111
  299.1 98.6 %all-gather.47.cloned.1.call-start = ((), (), s32[]{:S(2)}) async-start(), calls=%async_computation.31 | async-start | bytes 1536000 | tf_op jit(solution)/shard_map/all_gather | solution.py:111
  357.8 65.3 %all-gather.37.cloned.1.call-start = ((), (), s32[]{:S(2)}) async-start(), calls=%async_computation.26 | async-start | bytes 1327104 | tf_op jit(solution)/shard_map/all_gather | solution.py:193
  358.4 91.3 %all-gather.39.cloned.1.call-start = ((), (), s32[]{:S(2)}) async-start(), calls=%async_computation.27 | async-start | bytes 1327104 | tf_op jit(solution)/shard_map/all_gather | solution.py:194
  509.3 3.0 collective-permute-start.2
  555.9 45.5 %all-to-all-start.2 = ((bf16[197,4,576]{2,0,1:T(8,128)(2,1)}), bf16[197,4,576]{2,0,1:T(8,128)(2,1)}, u32[]{:S(2)}, u32[]{:S(2)}) async-start(bf16[197,4,576]{2,0,1:T(8,128)(2,1)} %copy.167), calls=%async_computation.2 | async-start | bytes 2048000 | tf_op jit(solution)/shard_map/all_to_all | solution.py:282
  560.3 104.9 %reduce-scatter.33.cloned.1.call-start = ((), (), s32[]{:S(2)}) async-start(), calls=%async_computation.17 | async-start | bytes 1474560 | tf_op jit(solution)/shard_map/reduce_scatter | solution.py:277
  563.1 132.9 %all-gather.51.cloned.1.call-start = ((), (), s32[]{:S(2)}) async-start(), calls=%async_computation.33 | async-start | bytes 1536000 | tf_op jit(solution)/shard_map/all_gather | solution.py:111
  652.9 3.0 collective-permute-start.3
  665.2 154.6 %reduce-scatter.45.cloned.1.call-start = ((), (), s32[]{:S(2)}) async-start(), calls=%async_computation.35 | async-start | bytes 442368
  667.2 335.0 %reduce-scatter.41.cloned.1.call-start = ((), (), s32[]{:S(2)}) async-start(), calls=%async_computation.21 | async-start | bytes 1327104 | tf_op jit(solution)/shard_map/reduce_scatter | solution.py:297
  671.4 330.8 %reduce-scatter.39.cloned.1.call-start = ((), (), s32[]{:S(2)}) async-start(), calls=%async_computation.20 | async-start | bytes 1327104 | tf_op jit(solution)/shard_map/reduce_scatter | solution.py:297
  702.8 301.9 %reduce-scatter.31.cloned.1.call-start = ((), (), s32[]{:S(2)}) async-start(), calls=%async_computation.16 | async-start | bytes 1474560 | tf_op jit(solution)/shard_map/reduce_scatter | solution.py:277
  760.2 3.3 collective-permute-start.4
  773.3 233.4 %reduce-scatter.37.cloned.1.call-start = ((), (), s32[]{:S(2)}) async-start(), calls=%async_computation.19 | async-start | bytes 1327104 | tf_op jit(solution)/shard_map/reduce_scatter | solution.py:294
  777.8 229.0 %reduce-scatter.35.cloned.1.call-start = ((), (), s32[]{:S(2)}) async-start(), calls=%async_computation.18 | async-start | bytes 1327104 | tf_op jit(solution)/shard_map/reduce_scatter | solution.py:294
  808.8 44.3 %all-to-all-start.3 = ((bf16[197,4,576]{2,0,1:T(8,128)(2,1)}), bf16[197,4,576]{2,0,1:T(8,128)(2,1)S(1)}, u32[]{:S(2)}, u32[]{:S(2)}) async-start(bf16[197,4,576]{2,0,1:T(8,128)(2,1)} %copy.175), calls=%async_computation.3 | async-start | bytes 2048000 | tf_op jit(solution)/shard_map/all_to_all | solution.py:282
  812.5 197.2 %reduce-scatter.29.cloned.1.call-start = ((), (), s32[]{:S(2)}) async-start(), calls=%async_computation.15 | async-start | bytes 1105920 | tf_op jit(solution)/shard_map/reduce_scatter | solution.py:290
  819.4 193.6 %reduce-scatter.27.cloned.1.call-start = ((), (), s32[]{:S(2)}) async-start(), calls=%async_computation.14 | async-start | bytes 1105920 | tf_op jit(solution)/shard_map/reduce_scatter | solution.py:290
  942.5 7.4 collective-permute-start.5
  947.6 48.1 %collective-permute-start.1 = (f32[9,768]{1,0:T(8,128)S(1)}, f32[9,768]{1,0:T(8,128)S(1)}, u32[]{:S(2)}, u32[]{:S(2)}) collective-permute-start(f32[9,768]{1,0:T(8,128)S(1)} %slice.149), channel_id=1, source_target_pairs={{0,1},{1,2},{2,3},{4,5},{5,6},{6,7},{8,9},{9,10},{10,11},{12,13},{... | collective-permute-start | bytes 82952
  949.9 100.0 %reduce-scatter.43.cloned.1.call-start = ((), (), s32[]{:S(2)}) async-start(), calls=%async_computation.34 | async-start | bytes 442368
  (58 other events, 697.6 us)
Sparse Core Ops, SparseCore 0:
  13.6 33.9 all-gather.40
  68.6 31.0 all-gather.28
  103.1 30.3 all-gather.42
  135.7 23.1 all-gather.30
  161.2 24.0 all-gather.32
  252.1 30.4 all-gather.44
  284.7 48.1 all-gather.34
  335.1 30.0 all-gather.48
  367.3 30.3 all-gather.46
  400.0 23.1 all-gather.36
  425.6 24.0 all-gather.38
  563.2 39.6 reduce-scatter.32
  665.3 30.6 all-gather.50
  699.5 32.9 reduce-scatter.44
  735.6 36.7 reduce-scatter.40
  775.7 36.7 reduce-scatter.38
  814.7 39.4 reduce-scatter.30
  857.3 36.9 reduce-scatter.36
  897.9 36.7 reduce-scatter.34
  937.8 35.8 reduce-scatter.28
  977.2 35.7 reduce-scatter.26
  1016.0 33.8 reduce-scatter.42
where the time goes:
time: 1070 us; the launch traced here: 1060 us
  waiting for transfers between devices  374 us (35%)
  blocking collectives  365 us (34%)
  matrix products  118 us (11%)
  local copies, waits for them, and re-layouts  114 us (11%)
  other arithmetic  41.6 us (4%)
  starting transfers between devices  29.6 us (3%)
  between operations  17.2 us (2%)
    unnamed x5, blocking collectives  277 us
    all_gather x6, waiting for transfers between devices, group_rows(): return lax.all_gather(tokens_low, 'col', axis=0, tiled=True)  111 us
    all_to_all x2, waiting for transfers between devices, per_device(): lax.all_to_all(grad_packed, 'col', split_axis=1, concat_axis=0, tiled=True)  70.6 us
    unnamed x144, local copies, waits for them, and re-layouts  57.2 us
    all_to_all x2, waiting for transfers between devices, per_device(): lax.all_to_all(packed_cols, 'col', split_axis=0, concat_axis=1, tiled=True)  48.4 us
    all_gather x2, waiting for transfers between devices, per_device(): lax.all_gather(lowered[2], 'row', axis=0, tiled=True)  45.6 us
    all_gather x2, waiting for transfers between devices, per_device(): lax.all_gather(lowered[3], 'row', axis=1, tiled=True)  43.7 us
    psum x1, blocking collectives, per_device(): lax.psum((jnp.stack([gain_one, gain_two]), jnp.stack([grad_res_one, grad_...  41.4 us
  transfers between devices with their start and end apart: 32, of which 21 were waited for; matrix products, arithmetic and copies ran while one was open for 33% of the time, Pallas kernels for 0%

commit v1 on v0

v1 whole, which is shorter than its diff:
```python
import functools

import jax
import jax.numpy as jnp
from jax import lax
from jax.experimental import pallas as pl
from jax.experimental.pallas import tpu as pltpu
from jax.sharding import PartitionSpec as P

HEADS = 12
LAYERS = 2
STEP = 3
D = 768
FF = 3072
HD = 64
BLOCKS = 4
ROWS = 208
QKV_W = 3 * D // BLOCKS
OUT_W = D // BLOCKS
UP_W = FF // BLOCKS
PIECE = 96

norm_eps = 1e-06
root_half = 0.7071067811865476
inv_root_two_pi = 0.3989422804014327
beta_one = 0.9
beta_two = 0.999
adam_eps = 1e-08
learn_rate = 0.06
decay_rate = 0.05

BF = jnp.bfloat16
F32 = jnp.float32


def dot_nn(a, b):
    return lax.dot_general(a, b, (((1,), (0,)), ((), ())), preferred_element_type=F32)


def dot_nt(a, b):
    return lax.dot_general(a, b, (((1,), (1,)), ((), ())), preferred_element_type=F32)


def dot_tn(a, b):
    return lax.dot_general(a, b, (((0,), (0,)), ((), ())), preferred_element_type=F32)


def scaled_rows(x):
    center = jnp.mean(x, axis=-1, keepdims=True)
    shifted = x - center
    inverse = lax.rsqrt(jnp.mean(shifted * shifted, axis=-1, keepdims=True) + norm_eps)
    return shifted * inverse, inverse


def norm_back(upstream, scaled, inverse, gain):
    grad_scaled = upstream * gain
    mean_one = jnp.mean(grad_scaled, axis=-1, keepdims=True)
    mean_two = jnp.mean(grad_scaled * scaled, axis=-1, keepdims=True)
    grad_gain = jnp.sum(upstream * scaled, axis=0, keepdims=True)
    return inverse * (grad_scaled - mean_one - scaled * mean_two), grad_gain


def block_of(turn, s):
    return lax.rem(turn - s + 2 * BLOCKS, BLOCKS)


def attend_kernel(seq, turn_ref, x_ref, gain_ref, bias_ref, w_ref, qkv_ref, lse_ref, oext_ref, h1_ref, a2_ref, blk):
    turn = turn_ref[0]
    x = x_ref[...]
    scaled, _ = scaled_rows(x)
    a1 = (scaled * gain_ref[0:1, :]).astype(BF)
    for s in range(BLOCKS):
        t = dot_nn(a1, w_ref[s, :, 0:640])
        blk[block_of(turn, s)] = t.astype(BF)
    for b in range(BLOCKS):
        qkv_ref[:, b * QKV_W : (b + 1) * QKV_W] = blk[b, :, 0:QKV_W]
    low_half = lax.broadcasted_iota(jnp.int32, (ROWS, 128), 1) < HD
    key_live = lax.broadcasted_iota(jnp.int32, (ROWS, ROWS), 0) < seq
    scale = HD ** (-0.5)
    oext_ref[:, :, 0:HD] = jnp.zeros((BLOCKS, ROWS, HD), BF)
    for pair in range(HEADS // 2):
        q2 = qkv_ref[:, pair * 128 : (pair + 1) * 128]
        k2 = qkv_ref[:, D + pair * 128 : D + (pair + 1) * 128]
        v2 = qkv_ref[:, 2 * D + pair * 128 : 2 * D + (pair + 1) * 128]
        mixed = []
        for half in range(2):
            live = low_half if half == 0 else jnp.logical_not(low_half)
            qm = jnp.where(live, q2, jnp.zeros_like(q2))
            st = jnp.where(key_live, dot_nt(k2, qm) * scale, -1e30)
            peak = jnp.max(st, axis=0, keepdims=True)
            grown = jnp.exp(st - peak)
            total = jnp.sum(grown, axis=0, keepdims=True)
            head = 2 * pair + half
            lse_ref[head : head + 1, :] = peak + jnp.log(total)
            probs = (grown * (1.0 / total)).astype(BF)
            mixed.append(dot_tn(probs, v2))
        both = jnp.where(low_half, mixed[0], mixed[1]).astype(BF)
        for half in range(2):
            head = 2 * pair + half
            lane = HD + (head % 3) * HD
            oext_ref[head // 3, :, lane : lane + HD] = both[:, half * HD : (half + 1) * HD]
    total = x + bias_ref[0:1, :]
    for s in range(BLOCKS):
        total = total + dot_nt(oext_ref[block_of(turn, s)], w_ref[s, :, 512:768])
    h1_ref[...] = total
    scaled2, _ = scaled_rows(total)
    a2_ref[...] = (scaled2 * gain_ref[1:2, :]).astype(BF)


def feed_kernel(h1_ref, a2_ref, bias_ref, bup_ref, w_ref, z_ref, slope_ref, y_ref):
    s = pl.program_id(0)

    @pl.when(s == 0)
    def _():
        y_ref[...] = h1_ref[...] + bias_ref[1:2, :]

    u = dot_nn(a2_ref[...], w_ref[0, :, 0:UP_W]) + bup_ref[0]
    bell = 0.5 * (1.0 + lax.erf(u * root_half))
    z = (u * bell).astype(BF)
    z_ref[0] = z
    slope_ref[0] = bell + u * inv_root_two_pi * jnp.exp(-0.5 * u * u)
    y_ref[...] += dot_nt(z, w_ref[0, :, UP_W : 2 * UP_W])


def put_grad(near_ref, far_ref, value):
    for m in range(4):
        near_ref[m, 0] = value[m * PIECE : (m + 1) * PIECE]
        far_ref[m, 0] = value[(4 + m) * PIECE : (5 + m) * PIECE]


def feed_back_kernel(
    g_ref, h1_ref, a2_ref, gain_ref, z_ref, slope_ref, w_ref,
    upn_ref, upf_ref, dnn_ref, dnf_ref, bup_ref, dh1_ref, sums_ref, da2, gb_t, a2_t,
):
    s = pl.program_id(0)

    @pl.when(s == 0)
    def _():
        da2[...] = jnp.zeros_like(da2)
        gb_t[...] = g_ref[...].T.astype(BF)
        a2_t[...] = a2_ref[...].T

    gb = g_ref[...].astype(BF)
    put_grad(dnn_ref, dnf_ref, dot_nn(gb_t[...], z_ref[0]).astype(BF))
    du = dot_nn(gb, w_ref[0, :, UP_W : 2 * UP_W]) * slope_ref[0]
    bup_ref[0] = jnp.sum(du, axis=0, keepdims=True)
    dub = du.astype(BF)
    put_grad(upn_ref, upf_ref, dot_nn(a2_t[...], dub).astype(BF))
    da2[...] += dot_nt(dub, w_ref[0, :, 0:UP_W])

    @pl.when(s == BLOCKS - 1)
    def _():
        g = g_ref[...]
        scaled, inverse = scaled_rows(h1_ref[...])
        below, grad_gain = norm_back(da2[...], scaled, inverse, gain_ref[1:2, :])
        dh1 = below + g
        dh1_ref[...] = dh1
        sums_ref[0:1, :] = grad_gain
        sums_ref[1:2, :] = jnp.sum(g, axis=0, keepdims=True)
        sums_ref[2:3, :] = jnp.sum(dh1, axis=0, keepdims=True)


def attend_back_kernel(
    seq, turn_ref, dh1_ref, x_ref, gain_ref, qkv_ref, lse_ref, oext_ref, w_ref,
    near_ref, far_ref, below_ref, sums_ref, dext, dmix, dqkv, dqx,
):
    turn = turn_ref[0]
    dh1 = dh1_ref[...]
    hb = dh1.astype(BF)
    hb_t = dh1.T.astype(BF)
    for s in range(BLOCKS):
        dext[block_of(turn, s)] = dot_nn(hb, w_ref[s, :, 512:768]).astype(BF)
    for b in range(BLOCKS):
        dmix[:, b * OUT_W : (b + 1) * OUT_W] = dext[b, :, HD : HD + OUT_W]
    low_half = lax.broadcasted_iota(jnp.int32, (ROWS, 128), 1) < HD
    key_live = lax.broadcasted_iota(jnp.int32, (ROWS, ROWS), 0) < seq
    scale = HD ** (-0.5)
    for pair in range(HEADS // 2):
        q2 = qkv_ref[:, pair * 128 : (pair + 1) * 128]
        k2 = qkv_ref[:, D + pair * 128 : D + (pair + 1) * 128]
        v2 = qkv_ref[:, 2 * D + pair * 128 : 2 * D + (pair + 1) * 128]
        d2 = dmix[:, pair * 128 : (pair + 1) * 128]
        dq = jnp.zeros((ROWS, 128), F32)
        dk = jnp.zeros((ROWS, 128), F32)
        dv = jnp.zeros((ROWS, 128), F32)
        for half in range(2):
            head = 2 * pair + half
            live = low_half if half == 0 else jnp.logical_not(low_half)
            none = jnp.zeros_like(q2)
            qm = jnp.where(live, q2, none)
            km = jnp.where(live, k2, none)
            dm = jnp.where(live, d2, none)
            st = jnp.where(key_live, dot_nt(k2, qm) * scale, -1e30)
            probs = jnp.exp(st - lse_ref[head : head + 1, :])
            dprobs = dot_nt(v2, dm)
            inner = jnp.sum(probs * dprobs, axis=0, keepdims=True)
            dst = (probs * (dprobs - inner) * scale).astype(BF)
            dv = dv + dot_nn(probs.astype(BF), dm)
            dk = dk + dot_nn(dst, qm)
            dq = dq + dot_tn(dst, km)
        dqkv[:, pair * 128 : (pair + 1) * 128] = dq.astype(BF)
        dqkv[:, D + pair * 128 : D + (pair + 1) * 128] = dk.astype(BF)
        dqkv[:, 2 * D + pair * 128 : 2 * D + (pair + 1) * 128] = dv.astype(BF)
    for b in range(BLOCKS):
        dqx[b, :, 0:QKV_W] = dqkv[:, b * QKV_W : (b + 1) * QKV_W]
        dqx[b, :, QKV_W:640] = jnp.zeros((ROWS, 640 - QKV_W), BF)
    scaled, inverse = scaled_rows(x_ref[...])
    a1_t = (scaled * gain_ref[0:1, :]).T.astype(BF)
    da1 = jnp.zeros((ROWS, D), F32)
    for s in range(BLOCKS):
        own = block_of(turn, s)
        part = dqx[own]
        da1 = da1 + dot_nt(part, w_ref[s, :, 0:640])
        first = dot_nn(a1_t, part)
        second = dot_nn(hb_t, oext_ref[own])
        for m in range(8):
            ref = near_ref if m < 4 else far_ref
            rows = slice(m * PIECE, (m + 1) * PIECE)
            ref[m % 4, s, :, 0:512] = first[rows, 0:512].astype(BF)
            ref[m % 4, s, :, 512:640] = (first[rows, 512:640] + second[rows, 0:128]).astype(BF)
            ref[m % 4, s, :, 640:768] = second[rows, 128:256].astype(BF)
    below, grad_gain = norm_back(da1, scaled, inverse, gain_ref[0:1, :])
    below_ref[...] = below + dh1
    sums_ref[0:1, :] = grad_gain


VM = pl.BlockSpec(memory_space=pltpu.VMEM)
SM = pl.BlockSpec(memory_space=pltpu.SMEM)
LIMIT = 56 * 1024 * 1024


def sds(shape, dtype):
    return jax.ShapeDtypeStruct(shape, dtype)


def attend(seq, turn, x, gains, biases, w):
    return pl.pallas_call(
        functools.partial(attend_kernel, seq),
        out_shape=(
            sds((ROWS, 3 * D), BF), sds((16, ROWS), F32), sds((BLOCKS, ROWS, 256), BF),
            sds((ROWS, D), F32), sds((ROWS, D), BF),
        ),
        in_specs=[SM] + [VM] * 4,
        out_specs=[VM] * 5,
        scratch_shapes=[pltpu.VMEM((BLOCKS, ROWS, 640), BF)],
        compiler_params=pltpu.CompilerParams(vmem_limit_bytes=LIMIT),
        cost_estimate=pl.CostEstimate(flops=10**10, bytes_accessed=8 * 10**6, transcendentals=10**6),
        name="attend",
    )(turn, x, gains, biases, w)


def whole(shape):
    return pl.BlockSpec(shape, lambda s: (0,) * len(shape))


def feed(h1, a2, biases, bup, w):
    return pl.pallas_call(
        feed_kernel,
        grid=(BLOCKS,),
        out_shape=(sds((BLOCKS, ROWS, UP_W), BF), sds((BLOCKS, ROWS, UP_W), F32), sds((ROWS, D), F32)),
        in_specs=[
            whole((ROWS, D)), whole((ROWS, D)), whole((2, D)),
            pl.BlockSpec((1, 1, UP_W), lambda s: (s, 0, 0)),
            pl.BlockSpec((1, D, 2 * UP_W), lambda s: (s, 0, 0)),
        ],
        out_specs=[
            pl.BlockSpec((1, ROWS, UP_W), lambda s: (s, 0, 0)),
            pl.BlockSpec((1, ROWS, UP_W), lambda s: (s, 0, 0)),
            whole((ROWS, D)),
        ],
        compiler_params=pltpu.CompilerParams(vmem_limit_bytes=LIMIT),
        cost_estimate=pl.CostEstimate(flops=10**10, bytes_accessed=14 * 10**6, transcendentals=10**6),
        name="feed",
    )(h1, a2, biases, bup, w)


def feed_back(g, h1, a2, gains, z, slope, w):
    grad = sds((4, BLOCKS, PIECE, UP_W), BF)
    grad_spec = pl.BlockSpec((4, 1, PIECE, UP_W), lambda s: (0, s, 0, 0))
    step_spec = pl.BlockSpec((1, ROWS, UP_W), lambda s: (s, 0, 0))
    return pl.pallas_call(
        feed_back_kernel,
        grid=(BLOCKS,),
        out_shape=(grad, grad, grad, grad, sds((BLOCKS, 1, UP_W), F32), sds((ROWS, D), F32), sds((8, D), F32)),
        in_specs=[
            whole((ROWS, D)), whole((ROWS, D)), whole((ROWS, D)), whole((2, D)), step_spec, step_spec,
            pl.BlockSpec((1, D, 2 * UP_W), lambda s: (s, 0, 0)),
        ],
        out_specs=[
            grad_spec, grad_spec, grad_spec, grad_spec,
            pl.BlockSpec((1, 1, UP_W), lambda s: (s, 0, 0)), whole((ROWS, D)), whole((8, D)),
        ],
        scratch_shapes=[pltpu.VMEM((ROWS, D), F32), pltpu.VMEM((D, ROWS), BF), pltpu.VMEM((D, ROWS), BF)],
        compiler_params=pltpu.CompilerParams(vmem_limit_bytes=LIMIT),
        cost_estimate=pl.CostEstimate(flops=2 * 10**10, bytes_accessed=28 * 10**6, transcendentals=0),
        name="feed_back",
    )(g, h1, a2, gains, z, slope, w)


def attend_back(seq, turn, dh1, x, gains, qkv, lse, oext, w):
    grad = sds((4, BLOCKS, PIECE, D), BF)
    return pl.pallas_call(
        functools.partial(attend_back_kernel, seq),
        out_shape=(grad, grad, sds((ROWS, D), F32), sds((8, D), F32)),
        in_specs=[SM] + [VM] * 7,
        out_specs=[VM] * 4,
        scratch_shapes=[
            pltpu.VMEM((BLOCKS, ROWS, 256), BF), pltpu.VMEM((ROWS, D), BF),
            pltpu.VMEM((ROWS, 3 * D), BF), pltpu.VMEM((BLOCKS, ROWS, 640), BF),
        ],
        compiler_params=pltpu.CompilerParams(vmem_limit_bytes=LIMIT),
        cost_estimate=pl.CostEstimate(flops=2 * 10**10, bytes_accessed=16 * 10**6, transcendentals=10**6),
        name="attend_back",
    )(turn, dh1, x, gains, qkv, lse, oext, w)


def adamw_step(param, gradient, first_moment, second_moment):
    fresh_first = beta_one * first_moment + (1.0 - beta_one) * gradient
    fresh_second = beta_two * second_moment + (1.0 - beta_two) * gradient * gradient
    first_hat = fresh_first / (1.0 - beta_one**STEP)
    second_hat = fresh_second / (1.0 - beta_two**STEP)
    updated = param - learn_rate * (
        first_hat / (jnp.sqrt(second_hat) + adam_eps) + decay_rate * param
    )
    return (updated, fresh_first, fresh_second)


class PlainPlan:
    def __init__(self, mesh):
        self.n_row = mesh.shape["row"]
        self.n_col = mesh.shape["col"]
        self.turn = jnp.zeros((1,), jnp.int32)

    def features(self, x):
        return x

    features_back = features

    def hidden(self, bias):
        return bias

    hidden_back = hidden

    def gather(self, shard, widths):
        full = lax.all_gather(shard, ("col", "row"), axis=0, tiled=True)
        full = full.reshape(self.n_col, D, sum(widths))
        parts = []
        start = 0
        for width in widths:
            part = full[:, :, start : start + width].transpose(1, 0, 2)
            parts.append(part.reshape(D, BLOCKS, -1).transpose(1, 0, 2))
            start += width
        return jnp.concatenate(parts, axis=2)

    def reduce(self, near, far, widths):
        full = jnp.concatenate([near, far], axis=0).transpose(0, 2, 1, 3)
        full = full.reshape(D, BLOCKS, -1)
        parts = []
        start = 0
        for width in widths:
            wide = width * self.n_col // BLOCKS
            part = full[:, :, start : start + wide].reshape(D, self.n_col, width)
            parts.append(part.transpose(1, 0, 2))
            start += wide
        packed = jnp.concatenate(parts, axis=2).reshape(self.n_col * D, sum(widths))
        return lax.psum_scatter(packed, ("col", "row"), scatter_dimension=0, tiled=True).astype(F32)

    def total(self, values):
        return lax.psum(values, ("row", "col"))


def flip_row(x, mask):
    return lax.ppermute(x, "row", [(i, i ^ mask) for i in range(8)])


def turn_col(x, shift):
    return lax.ppermute(x, "col", [(i, (i + shift) % 4) for i in range(4)])


CORE, NEXT_X, NEXT_Y = 1, 2, 4


class RelativePlan:
    def __init__(self, mesh):
        self.row = lax.axis_index("row")
        self.col = lax.axis_index("col")
        self.turn = self.col.reshape(1).astype(jnp.int32)

    def flip(self, x, bit, size):
        swapped = x.reshape(x.shape[:-1] + (-1, 2, size))
        swapped = jnp.concatenate([swapped[..., 1:2, :], swapped[..., 0:1, :]], axis=-2).reshape(x.shape)
        return jnp.where((self.row >> bit) & 1 == 1, swapped, x)

    def features(self, x):
        for bit in range(3):
            x = self.flip(x, bit, PIECE << bit)
        blocks = [x[..., i * PIECE : (i + 1) * PIECE] for i in range(8)]
        return jnp.concatenate([blocks[(p >> 2) | ((p & 3) << 1)] for p in range(8)], axis=-1)

    def features_back(self, x):
        blocks = [x[..., i * PIECE : (i + 1) * PIECE] for i in range(8)]
        x = jnp.concatenate([blocks[((i & 1) << 2) | (i >> 1)] for i in range(8)], axis=-1)
        for bit in range(3):
            x = self.flip(x, bit, PIECE << bit)
        return x

    def order(self):
        return lax.rem(self.col - jnp.arange(BLOCKS) + BLOCKS, BLOCKS)

    def hidden(self, bias):
        return bias[self.order()]

    hidden_back = hidden

    def gather(self, shard, widths):
        own = jnp.stack([shard] + [turn_col(shard, s) for s in range(1, BLOCKS)])
        from_x = flip_row(own, NEXT_X)
        from_y = flip_row(own, NEXT_Y)
        diag_low = flip_row(from_y[0:2], NEXT_X)
        diag_high = flip_row(from_x[2:4], NEXT_Y)
        near = [own, from_x, from_y, jnp.concatenate([diag_low, diag_high], axis=0)]
        far = [flip_row(part, CORE) for part in near]
        return jnp.concatenate(near + far, axis=1)

    def reduce(self, near, far, widths):
        other = flip_row(far, CORE)

        def joined(m, blocks):
            return near[m, blocks].astype(F32) + other[m, blocks].astype(F32)

        low, high, every = slice(0, 2), slice(2, 4), slice(0, 4)
        diag_low = flip_row(joined(3, low).astype(BF), NEXT_X)
        diag_high = flip_row(joined(3, high).astype(BF), NEXT_Y)
        to_x = jnp.concatenate([joined(1, low), joined(1, high) + diag_high.astype(F32)], axis=0)
        to_y = jnp.concatenate([joined(2, low) + diag_low.astype(F32), joined(2, high)], axis=0)
        from_x = flip_row(to_x.astype(BF), NEXT_X)
        from_y = flip_row(to_y.astype(BF), NEXT_Y)
        plane = joined(0, every) + from_x.astype(F32) + from_y.astype(F32)
        out = plane[0]
        for s in range(1, BLOCKS):
            out = out + turn_col(plane[s].astype(BF), -s).astype(F32)
        return out

    def total(self, values):
        for mask in (CORE, NEXT_X, NEXT_Y):
            values = values + flip_row(values, mask)
        for mask in (1, 2):
            values = values + lax.ppermute(values, "col", [(i, i ^ mask) for i in range(4)])
        return values


def per_device(
    mesh,
    images, cotangent, counts, w_qkv, w_out, w_up, w_down, norm_gains, res_biases, b_up,
    m_qkv, m_out, m_up, m_down, m_gains, m_biases, m_bup,
    v_qkv, v_out, v_up, v_down, v_gains, v_biases, v_bup,
):
    seq = images.shape[1]
    relative = mesh.shape["row"] == 8 and mesh.shape["col"] == 4
    plan = RelativePlan(mesh) if relative else PlainPlan(mesh)
    row_index = lax.axis_index("row")
    col_index = lax.axis_index("col")
    group_count = jnp.sum(
        jnp.where(jnp.arange(counts.shape[0], dtype=jnp.int32) == row_index, counts, 0)
    )
    live_mask = (col_index < group_count).astype(F32)
    att_widths = (w_qkv.shape[2], w_out.shape[1])
    ffn_widths = (w_up.shape[2], w_down.shape[1])
    att_full, ffn_full = [], []
    for level in range(LAYERS):
        att_shard = jnp.concatenate([w_qkv[level].astype(BF), w_out[level].T.astype(BF)], axis=1)
        ffn_shard = jnp.concatenate([w_up[level].astype(BF), w_down[level].T.astype(BF)], axis=1)
        att_full.append(plan.gather(att_shard, att_widths))
        ffn_full.append(plan.gather(ffn_shard, ffn_widths))

    pad = ((0, ROWS - seq), (0, 0))
    hidden = jnp.pad(plan.features(images[0]), pad)
    gains = plan.features(norm_gains)
    biases = plan.features(res_biases)
    saved = []
    for level in range(LAYERS):
        bup = plan.hidden(b_up[level].reshape(BLOCKS, UP_W))[:, None]
        qkv, lse, oext, h1, a2 = attend(seq, plan.turn, hidden, gains[level], biases[level], att_full[level])
        z, slope, y = feed(h1, a2, biases[level], bup, ffn_full[level])
        saved.append((hidden, qkv, lse, oext, h1, a2, z, slope))
        hidden = y
    layer_out = (plan.features_back(hidden[:seq]) * live_mask)[None]
    upstream = jnp.pad(plan.features(cotangent[0] * live_mask), pad)
    grads = [None] * LAYERS
    smalls = [None] * LAYERS
    for level in reversed(range(LAYERS)):
        below, qkv, lse, oext, h1, a2, z, slope = saved[level]
        upn, upf, dnn, dnf, bup_sum, dh1, sums_two = feed_back(
            upstream, h1, a2, gains[level], z, slope, ffn_full[level]
        )
        down = plan.reduce(dnn, dnf, ffn_widths[1:])
        up = plan.reduce(upn, upf, ffn_widths[:1])
        atn, atf, upstream, sums_one = attend_back(
            seq, plan.turn, dh1, below, gains[level], qkv, lse, oext, att_full[level]
        )
        att = plan.reduce(atn, atf, att_widths)
        grads[level] = (att[:, : att_widths[0]], att[:, att_widths[0] :].T, up, down.T)
        features = plan.features_back(
            jnp.concatenate([sums_one[0:1], sums_two[0:1], sums_two[2:3], sums_two[1:2]], axis=0)
        )
        bup_row = plan.hidden_back(bup_sum[:, 0]).reshape(4, D)
        smalls[level] = plan.total(jnp.concatenate([features, bup_row], axis=0))
    grad_images = plan.features_back(upstream[:seq])[None]
    grad_list = [jnp.stack([grads[level][index] for level in range(LAYERS)]) for index in range(4)]
    grad_list.append(jnp.stack([small[0:2] for small in smalls]))
    grad_list.append(jnp.stack([small[2:4] for small in smalls]))
    grad_list.append(jnp.stack([small[4:8].reshape(FF) for small in smalls]))
    params = [w_qkv, w_out, w_up, w_down, norm_gains, res_biases, b_up]
    firsts = [m_qkv, m_out, m_up, m_down, m_gains, m_biases, m_bup]
    seconds = [v_qkv, v_out, v_up, v_down, v_gains, v_biases, v_bup]
    results = [
        adamw_step(params[index], grad_list[index], firsts[index], seconds[index])
        for index in range(7)
    ]
    return (
        (layer_out, grad_images)
        + tuple(grad_list)
        + tuple(result[0] for result in results[:4])
        + tuple(result[1] for result in results)
        + tuple(result[2] for result in results)
    )


def solution(mesh):
    tokens = P(("row", "col"), None, None)
    matrices = (P(None, "row", "col"), P(None, "col", "row"), P(None, "row", "col"), P(None, "col", "row"))
    vectors = (P(), P(), P())
    in_specs = (tokens, tokens, P()) + (matrices + vectors) * 3
    out_specs = (tokens, tokens) + matrices + vectors + matrices + (matrices + vectors) * 2
    return jax.shard_map(
        functools.partial(per_device, mesh), mesh=mesh, in_specs=in_specs, out_specs=out_specs, check_vma=False
    )
```

time: 1070 us -> 591 us (0.55)
  blocking collectives: 365 us -> 0 us
  waiting for transfers between devices: 374 us -> 207 us
  matrix products: 118 us -> 0 us
  starting transfers between devices: 29.6 us -> 122 us
  Pallas kernels: 0 us -> 81.7 us
  between operations: 17.2 us -> 4.02 us
    unnamed x5 -> x0, blocking collectives: 277 us -> none
    all_gather x12 -> x0, waiting for transfers between devices: 213 us -> none  [the longest x6 111 us: group_rows(): return lax.all_gather(tokens_low, 'col', axis=0, tiled=True)]
    ppermute x0 -> x102, waiting for transfers between devices: none -> 207 us  [the longest x68 158 us: flip_row(): return lax.ppermute(x, 'row', [(i, i ^ mask) for i in range(8)])]
    ppermute x0 -> x102, starting transfers between devices: none -> 122 us  [the longest x30 65.4 us: turn_col(): return lax.ppermute(x, 'col', [(i, (i + shift) % 4) for i in range(4)])]
    all_to_all x4 -> x0, waiting for transfers between devices: 119 us -> none  [the longest x2 70.6 us: per_device(): lax.all_to_all(grad_packed, 'col', split_axis=1, concat_axis=0, tiled=True)]
    dot_general x36 -> x0, matrix products: 118 us -> none  [the longest x8 26.9 us: contract_rows(): lax.dot_general(left_rows, right_rows, (((0,), (0,)), ((), ())), preferre...]
    pallas_call x0 -> x8, Pallas kernels: none -> 81.7 us  [the longest x2 26.6 us: feed_back(): pl.pallas_call(feed_back_kernel, grid=(BLOCKS,), out_shape=(grad, grad, g...]
    all_gather x4 -> x0, blocking collectives: 46.5 us -> none  [the longest x2 24.8 us: per_device(): lax.all_gather(lowered[0], 'row', axis=0, tiled=True)]
  transfers between devices with their start and end apart: 32 -> 102, of which waited for: 21 -> 46; matrix products, arithmetic and copies ran while one was open for 33% -> 19% of each run, Pallas kernels for 0% -> 4%
where the time goes in v1:
time: 591 us; the launch traced here: 582 us
  waiting for transfers between devices  207 us (35%)
  starting transfers between devices  122 us (21%)
  local copies, waits for them, and re-layouts  115 us (19%)
  Pallas kernels  81.7 us (14%)
  other arithmetic  51 us (9%)
    ppermute x68, waiting for transfers between devices, flip_row(): return lax.ppermute(x, 'row', [(i, i ^ mask) for i in range(8)])  158 us
    ppermute x30, starting transfers between devices, turn_col(): return lax.ppermute(x, 'col', [(i, (i + shift) % 4) for i in range(4)])  65.4 us
    ppermute x68, starting transfers between devices, flip_row(): return lax.ppermute(x, 'row', [(i, i ^ mask) for i in range(8)])  53 us
    ppermute x30, waiting for transfers between devices, turn_col(): return lax.ppermute(x, 'col', [(i, (i + shift) % 4) for i in range(4)])  45 us
    unnamed x193, local copies, waits for them, and re-layouts  32.3 us
    reshape x34, local copies, waits for them, and re-layouts, flip(): jnp.concatenate([swapped[..., 1:2, :], swapped[..., 0:1, :]], axis=-2)  27.2 us
    pallas_call x2, Pallas kernels, feed_back(): pl.pallas_call(feed_back_kernel, grid=(BLOCKS,), out_shape=(grad, grad, g...  26.6 us
    pallas_call x2, Pallas kernels, attend_back(): pl.pallas_call(functools.partial(attend_back_kernel, seq), out_shape=(gra...  24.6 us
  transfers between devices with their start and end apart: 102, of which 46 were waited for; matrix products, arithmetic and copies ran while one was open for 19% of the time, Pallas kernels for 4%

profile of v1, /device:TPU:0, one launch (start us, length us, event | category | flops | bytes accessed | tf_op | source)
XLA Modules:
  0.0 581.6 jit_solution(11767184523702049278)
XLA Ops:
  3.8 5.0 collective-permute-start.2
  53.4 3.9 collective-permute-start.13
  62.1 12.6 %collective-permute-start.34 = (bf16[96,1536]{1,0:T(8,128)(2,1)}, bf16[96,1536]{1,0:T(8,128)(2,1)}, u32[]{:S(2)}, u32[]{:S(2)}) collective-permute-start(bf16[96,1536]{1,0:T(8,128)(2,1)} %get-tuple-element.354), channel_id=1, source_target_pairs={{0,2},{1,3},{2,0},{3,1},{4,6},{5,7},{6,4},{7,5},{8,10},{9,11},{10,... | collective-permute-start | bytes 884744 | tf_op jit(solution)/shard_map/ppermute | solution.py:377
  91.3 20.0 %collective-permute-done.34 = bf16[96,1536]{1,0:T(8,128)(2,1)} collective-permute-done((bf16[96,1536]{1,0:T(8,128)(2,1)}, bf16[96,1536]{1,0:T(8,128)(2,1)}, u32[]{:S(2)}, u32[]{:S(2)}) %collective-permute-start.34) | collective-permute-done | bytes 294944 | tf_op jit(solution)/shard_map/ppermute | solution.py:377
  118.1 9.4 %collective-permute-done.26 = bf16[4,96,768]{2,1,0:T(8,128)(2,1)S(1)} collective-permute-done((bf16[4,96,768]{2,1,0:T(8,128)(2,1)S(1)}, bf16[4,96,768]{2,1,0:T(8,128)(2,1)S(1)}, u32[]{:S(2)}, u32[]{:S(2)}) %collective-permute-start.26) | collective-permute-done | bytes 589856 | tf_op jit(solution)/shard_map/ppermute | solution.py:373
  146.5 21.6 %collective-permute-done.14 = bf16[4,96,1536]{2,1,0:T(8,128)(2,1)S(1)} collective-permute-done((bf16[4,96,1536]{2,1,0:T(8,128)(2,1)S(1)}, bf16[4,96,1536]{2,1,0:T(8,128)(2,1)S(1)}, u32[]{:S(2)}, u32[]{:S(2)}) %collective-permute-start.14) | collective-permute-done | bytes 1179680 | tf_op jit(solution)/shard_map/ppermute | solution.py:373
  173.1 20.9 %collective-permute-done.37 = bf16[4,96,1536]{2,1,0:T(8,128)(2,1)S(1)} collective-permute-done((bf16[4,96,1536]{2,1,0:T(8,128)(2,1)S(1)}, bf16[4,96,1536]{2,1,0:T(8,128)(2,1)S(1)}, u32[]{:S(2)}, u32[]{:S(2)}) %collective-permute-start.37) | collective-permute-done | bytes 1179680 | tf_op jit(solution)/shard_map/ppermute | solution.py:373
  202.4 7.5 %attend.2 = (bf16[208,2304]{1,0:T(8,128)(2,1)}, f32[16,208]{1,0:T(8,128)}, bf16[4,208,256]{2,1,0:T(8,128)(2,1)}, f32[208,768]{1,0:T(8,128)}, bf16[208,768]{1,0:T(8,128)(2,1)}) custom-call(s32[1]{0:T(128)} %bitcast.turn_ref, f32[208,768]{1,0:T(8,128)} %pad.7.x_ref, f32[2,768]{1,0:T(2,128)} %get-tuple-element.415.gain_ref, ...), custom_call_target="tpu_custom_call" | custom-call | flops 10000000000 | bytes 8000000 | tf_op jit(solution)/shard_map/attend/pallas_call | solution.py:237
  219.6 6.0 %collective-permute-done.38 = bf16[2,96,1536]{2,1,0:T(8,128)(2,1)S(1)} collective-permute-done((bf16[2,96,1536]{2,1,0:T(8,128)(2,1)}, bf16[2,96,1536]{2,1,0:T(8,128)(2,1)S(1)}, u32[]{:S(2)}, u32[]{:S(2)}) %collective-permute-start.38) | collective-permute-done | bytes 589856 | tf_op jit(solution)/shard_map/ppermute | solution.py:373
  239.0 7.8 %feed.2 = (bf16[4,208,768]{2,1,0:T(8,128)(2,1)}, f32[4,208,768]{2,1,0:T(8,128)}, f32[208,768]{1,0:T(8,128)}) custom-call(f32[208,768]{1,0:T(8,128)} %get-tuple-element.65.h1_ref, bf16[208,768]{1,0:T(8,128)(2,1)} %get-tuple-element.66.a2_ref, f32[2,768]{1,0:T(2,128)} %get-tuple-element.413.bias_ref, f32[4,1,768]{2,1,0:T(1,128)} %broadcast_in_dim.8.bup_ref, ...), custom_call_target="tpu_custom_call" | custom-call | flops 10000000000 | bytes 14000000 | tf_op jit(solution)/shard_map/feed/pallas_call | solution.py:257
  246.8 7.5 %attend.3 = (bf16[208,2304]{1,0:T(8,128)(2,1)}, f32[16,208]{1,0:T(8,128)}, bf16[4,208,256]{2,1,0:T(8,128)(2,1)}, f32[208,768]{1,0:T(8,128)}, bf16[208,768]{1,0:T(8,128)(2,1)}) custom-call(s32[1]{0:T(128)} %bitcast.turn_ref, f32[208,768]{1,0:T(8,128)} %get-tuple-element.67.x_ref, f32[2,768]{1,0:T(2,128)} %get-tuple-element.414.gain_ref, ...), custom_call_target="tpu_custom_call" | custom-call | flops 10000000000 | bytes 8000000 | tf_op jit(solution)/shard_map/attend/pallas_call | solution.py:237
  255.5 7.7 %feed.3 = (bf16[4,208,768]{2,1,0:T(8,128)(2,1)}, f32[4,208,768]{2,1,0:T(8,128)}, f32[208,768]{1,0:T(8,128)}) custom-call(f32[208,768]{1,0:T(8,128)} %get-tuple-element.68.h1_ref, bf16[208,768]{1,0:T(8,128)(2,1)} %get-tuple-element.69.a2_ref, f32[2,768]{1,0:T(2,128)} %get-tuple-element.412.bias_ref, f32[4,1,768]{2,1,0:T(1,128)} %broadcast_in_dim.9.bup_ref, ...), custom_call_target="tpu_custom_call" | custom-call | flops 10000000000 | bytes 14000000 | tf_op jit(solution)/shard_map/feed/pallas_call | solution.py:257
  274.4 13.4 %feed_back.2 = (bf16[4,4,96,768]{3,2,1,0:T(8,128)(2,1)}, bf16[4,4,96,768]{3,2,1,0:T(8,128)(2,1)}, bf16[4,4,96,768]{3,2,1,0:T(8,128)(2,1)}, bf16[4,4,96,768]{3,2,...) custom-call(f32[208,768]{1,0:T(8,128)} %pad.8.g_ref, ...), custom_call_target="tpu_custom_call" | custom-call | flops 20000000000 | bytes 28000000 | tf_op jit(solution)/shard_map/feed_back/pallas_call | solution.py:281
  287.8 12.2 %attend_back.2 = (bf16[4,4,96,768]{3,2,1,0:T(8,128)(2,1)}, bf16[4,4,96,768]{3,2,1,0:T(8,128)(2,1)}, f32[208,768]{1,0:T(8,128)}, f32[8,768]{1,0:T(8,128)}) custom-call(s32[1]{0:T(128)} %bitcast.turn_ref, f32[208,768]{1,0:T(8,128)} %get-tuple-element.73.dh1_ref, f32[208,768]{1,0:T(8,128)} %get-tuple-element.67.x_ref, f32[2,768]{1,0:T(2,128)} %get-tuple-element.414.gain_ref, ...), custom_call_target="tpu_custom_call" | custom-call | flops 20000000000 | bytes 16000000 | tf_op jit(solution)/shard_map/attend_back/pallas_call | solution.py:302
  300.1 13.1 %feed_back.3 = (bf16[4,4,96,768]{3,2,1,0:T(8,128)(2,1)}, bf16[4,4,96,768]{3,2,1,0:T(8,128)(2,1)}, bf16[4,4,96,768]{3,2,1,0:T(8,128)(2,1)}, bf16[4,4,96,768]{3,2,...) custom-call(f32[208,768]{1,0:T(8,128)} %get-tuple-element.77.g_ref, ...), custom_call_target="tpu_custom_call" | custom-call | flops 20000000000 | bytes 28000000 | tf_op jit(solution)/shard_map/feed_back/pallas_call | solution.py:281
  313.2 12.3 %attend_back.3 = (bf16[4,4,96,768]{3,2,1,0:T(8,128)(2,1)}, bf16[4,4,96,768]{3,2,1,0:T(8,128)(2,1)}, f32[208,768]{1,0:T(8,128)}, f32[8,768]{1,0:T(8,128)}) custom-call(s32[1]{0:T(128)} %bitcast.turn_ref, f32[208,768]{1,0:T(8,128)} %get-tuple-element.80.dh1_ref, f32[208,768]{1,0:T(8,128)} %pad.7.x_ref, f32[2,768]{1,0:T(2,128)} %get-tuple-element.415.gain_ref, ...), custom_call_target="tpu_custom_call" | custom-call | flops 20000000000 | bytes 16000000 | tf_op jit(solution)/shard_map/attend_back/pallas_call | solution.py:302
  416.3 3.4 collective-permute-done.69
  422.4 3.6 collective-permute-done.61
  428.9 3.4 collective-permute-done.85
  441.5 9.8 %collective-permute-done.56 = bf16[4,96,768]{2,1,0:T(8,128)(2,1)S(1)} collective-permute-done((bf16[4,96,768]{2,1,0:T(8,128)(2,1)S(1)}, bf16[4,96,768]{2,1,0:T(8,128)(2,1)S(1)}, u32[]{:S(2)}, u32[]{:S(2)}) %collective-permute-start.56) | collective-permute-done | bytes 589856 | tf_op jit(solution)/shard_map/ppermute | solution.py:373
  455.2 8.8 %collective-permute-done.48 = bf16[4,96,768]{2,1,0:T(8,128)(2,1)S(1)} collective-permute-done((bf16[4,96,768]{2,1,0:T(8,128)(2,1)S(1)}, bf16[4,96,768]{2,1,0:T(8,128)(2,1)S(1)}, u32[]{:S(2)}, u32[]{:S(2)}) %collective-permute-start.48) | collective-permute-done | bytes 589856 | tf_op jit(solution)/shard_map/ppermute | solution.py:373
  466.8 9.8 %collective-permute-done.72 = bf16[4,96,768]{2,1,0:T(8,128)(2,1)S(1)} collective-permute-done((bf16[4,96,768]{2,1,0:T(8,128)(2,1)S(1)}, bf16[4,96,768]{2,1,0:T(8,128)(2,1)S(1)}, u32[]{:S(2)}, u32[]{:S(2)}) %collective-permute-start.72) | collective-permute-done | bytes 589856 | tf_op jit(solution)/shard_map/ppermute | solution.py:373
  479.4 9.8 %collective-permute-done.64 = bf16[4,96,768]{2,1,0:T(8,128)(2,1)S(1)} collective-permute-done((bf16[4,96,768]{2,1,0:T(8,128)(2,1)S(1)}, bf16[4,96,768]{2,1,0:T(8,128)(2,1)S(1)}, u32[]{:S(2)}, u32[]{:S(2)}) %collective-permute-start.64) | collective-permute-done | bytes 589856 | tf_op jit(solution)/shard_map/ppermute | solution.py:373
  490.8 11.1 %collective-permute-done.88 = bf16[4,96,768]{2,1,0:T(8,128)(2,1)S(1)} collective-permute-done((bf16[4,96,768]{2,1,0:T(8,128)(2,1)S(1)}, bf16[4,96,768]{2,1,0:T(8,128)(2,1)S(1)}, u32[]{:S(2)}, u32[]{:S(2)}) %collective-permute-start.88) | collective-permute-done | bytes 589856 | tf_op jit(solution)/shard_map/ppermute | solution.py:373
  505.6 8.0 %collective-permute-done.80 = bf16[4,96,768]{2,1,0:T(8,128)(2,1)S(1)} collective-permute-done((bf16[4,96,768]{2,1,0:T(8,128)(2,1)S(1)}, bf16[4,96,768]{2,1,0:T(8,128)(2,1)S(1)}, u32[]{:S(2)}, u32[]{:S(2)}) %collective-permute-start.80) | collective-permute-done | bytes 589856 | tf_op jit(solution)/shard_map/ppermute | solution.py:373
  523.6 7.7 %collective-permute-done.50 = bf16[96,768]{1,0:T(8,128)(2,1)S(1)} collective-permute-done((bf16[96,768]{1,0:T(8,128)(2,1)S(1)}, bf16[96,768]{1,0:T(8,128)(2,1)S(1)}, u32[]{:S(2)}, u32[]{:S(2)}) %collective-permute-start.50) | collective-permute-done | bytes 147488 | tf_op jit(solution)/shard_map/ppermute | solution.py:377
  531.4 4.5 collective-permute-start.67
  544.9 3.5 collective-permute-start.91
  548.4 3.5 collective-permute-start.90
  553.6 4.8 collective-permute-done.66
  561.2 3.5 collective-permute-start.82
  573.9 3.6 collective-permute-done.82
  (655 shorter events, 297.4 us)
Async XLA Ops:
  3.8 49.5 %collective-permute-start.2 = (bf16[96,768]{1,0:T(8,128)(2,1)}, bf16[96,768]{1,0:T(8,128)(2,1)}, u32[]{:S(2)}, u32[]{:S(2)}) collective-permute-start(bf16[96,768]{1,0:T(8,128)(2,1)} %pad_maximum_fusion.38), channel_id=1, source_target_pairs={{0,3},{1,0},{2,1},{3,2},{4,7},{5,4},{6,5},{7,6},{8,11},{9,8},{10,9... | collective-permute-start | bytes 442376 | tf_op jit(solution)/shard_map/ppermute | solution.py:377
  8.8 44.6 %collective-permute-start.1 = (bf16[96,768]{1,0:T(8,128)(2,1)}, bf16[96,768]{1,0:T(8,128)(2,1)}, u32[]{:S(2)}, u32[]{:S(2)}) collective-permute-start(bf16[96,768]{1,0:T(8,128)(2,1)} %pad_maximum_fusion.38), channel_id=1, source_target_pairs={{0,2},{1,3},{2,0},{3,1},{4,6},{5,7},{6,4},{7,5},{8,10},{9,11},{10,... | collective-permute-start | bytes 442376 | tf_op jit(solution)/shard_map/ppermute | solution.py:377
  8.8 48.5 %collective-permute-start = (bf16[96,768]{1,0:T(8,128)(2,1)}, bf16[96,768]{1,0:T(8,128)(2,1)}, u32[]{:S(2)}, u32[]{:S(2)}) collective-permute-start(bf16[96,768]{1,0:T(8,128)(2,1)} %pad_maximum_fusion.38), channel_id=1, source_target_pairs={{0,1},{1,2},{2,3},{3,0},{4,5},{5,6},{6,7},{7,4},{8,9},{9,10},{10,1... | collective-permute-start | bytes 442376 | tf_op jit(solution)/shard_map/ppermute | solution.py:377
  10.6 46.7 %collective-permute-start.24 = (bf16[96,768]{1,0:T(8,128)(2,1)}, bf16[96,768]{1,0:T(8,128)(2,1)}, u32[]{:S(2)}, u32[]{:S(2)}) collective-permute-start(bf16[96,768]{1,0:T(8,128)(2,1)} %pad_maximum_fusion.39), channel_id=1, source_target_pairs={{0,3},{1,0},{2,1},{3,2},{4,7},{5,4},{6,5},{7,6},{8,11},{9,8},{10,9... | collective-permute-start | bytes 442376 | tf_op jit(solution)/shard_map/ppermute | solution.py:377
  13.4 44.6 %collective-permute-start.23 = (bf16[96,768]{1,0:T(8,128)(2,1)}, bf16[96,768]{1,0:T(8,128)(2,1)}, u32[]{:S(2)}, u32[]{:S(2)}) collective-permute-start(bf16[96,768]{1,0:T(8,128)(2,1)} %pad_maximum_fusion.39), channel_id=1, source_target_pairs={{0,2},{1,3},{2,0},{3,1},{4,6},{5,7},{6,4},{7,5},{8,10},{9,11},{10,... | collective-permute-start | bytes 442376 | tf_op jit(solution)/shard_map/ppermute | solution.py:377
  53.4 30.8 %collective-permute-start.13 = (bf16[96,1536]{1,0:T(8,128)(2,1)}, bf16[96,1536]{1,0:T(8,128)(2,1)}, u32[]{:S(2)}, u32[]{:S(2)}) collective-permute-start(bf16[96,1536]{1,0:T(8,128)(2,1)} %get-tuple-element.360), channel_id=1, source_target_pairs={{0,3},{1,0},{2,1},{3,2},{4,7},{5,4},{6,5},{7,6},{8,11},{9,8},{10,9... | collective-permute-start | bytes 884744 | tf_op jit(solution)/shard_map/ppermute | solution.py:377
  57.3 30.3 %collective-permute-start.12 = (bf16[96,1536]{1,0:T(8,128)(2,1)}, bf16[96,1536]{1,0:T(8,128)(2,1)}, u32[]{:S(2)}, u32[]{:S(2)}) collective-permute-start(bf16[96,1536]{1,0:T(8,128)(2,1)} %get-tuple-element.360), channel_id=1, source_target_pairs={{0,2},{1,3},{2,0},{3,1},{4,6},{5,7},{6,4},{7,5},{8,10},{9,11},{10,... | collective-permute-start | bytes 884744 | tf_op jit(solution)/shard_map/ppermute | solution.py:377
  57.3 32.1 %collective-permute-start.11 = (bf16[96,1536]{1,0:T(8,128)(2,1)}, bf16[96,1536]{1,0:T(8,128)(2,1)}, u32[]{:S(2)}, u32[]{:S(2)}) collective-permute-start(bf16[96,1536]{1,0:T(8,128)(2,1)} %get-tuple-element.360), channel_id=1, source_target_pairs={{0,1},{1,2},{2,3},{3,0},{4,5},{5,6},{6,7},{7,4},{8,9},{9,10},{10,1... | collective-permute-start | bytes 884744 | tf_op jit(solution)/shard_map/ppermute | solution.py:377
  58.0 33.2 %collective-permute-start.35 = (bf16[96,1536]{1,0:T(8,128)(2,1)}, bf16[96,1536]{1,0:T(8,128)(2,1)}, u32[]{:S(2)}, u32[]{:S(2)}) collective-permute-start(bf16[96,1536]{1,0:T(8,128)(2,1)} %get-tuple-element.354), channel_id=1, source_target_pairs={{0,3},{1,0},{2,1},{3,2},{4,7},{5,4},{6,5},{7,6},{8,11},{9,8},{10,9... | collective-permute-start | bytes 884744 | tf_op jit(solution)/shard_map/ppermute | solution.py:377
  62.1 49.2 %collective-permute-start.34 = (bf16[96,1536]{1,0:T(8,128)(2,1)}, bf16[96,1536]{1,0:T(8,128)(2,1)}, u32[]{:S(2)}, u32[]{:S(2)}) collective-permute-start(bf16[96,1536]{1,0:T(8,128)(2,1)} %get-tuple-element.354), channel_id=1, source_target_pairs={{0,2},{1,3},{2,0},{3,1},{4,6},{5,7},{6,4},{7,5},{8,10},{9,11},{10,... | collective-permute-start | bytes 884744 | tf_op jit(solution)/shard_map/ppermute | solution.py:377
  84.3 30.0 %collective-permute-start.33 = (bf16[96,1536]{1,0:T(8,128)(2,1)}, bf16[96,1536]{1,0:T(8,128)(2,1)S(1)}, u32[]{:S(2)}, u32[]{:S(2)}) collective-permute-start(bf16[96,1536]{1,0:T(8,128)(2,1)} %get-tuple-element.354), channel_id=1, source_target_pairs={{0,1},{1,2},{2,3},{3,0},{4,5},{5,6},{6,7},{7,4},{8,9},{9,10},{10,1... | collective-permute-start | bytes 884744 | tf_op jit(solution)/shard_map/ppermute | solution.py:377
  87.6 30.0 %collective-permute-start.3 = (bf16[4,96,768]{2,1,0:T(8,128)(2,1)S(1)}, bf16[4,96,768]{2,1,0:T(8,128)(2,1)S(1)}, u32[]{:S(2)}, u32[]{:S(2)}) collective-permute-start(bf16[4,96,768]{2,1,0:T(8,128)(2,1)S(1)} %get-tuple-element.351), channel_id=1, source_target_pairs={{0,8},{4,12},{8,0},{12,4},{16,24},{20,28},{24,16},{28,20},{1,9},{5... | collective-permute-start | bytes 1769480 | tf_op jit(solution)/shard_map/ppermute | solution.py:373
  89.4 26.2 %collective-permute-start.4 = (bf16[4,96,768]{2,1,0:T(8,128)(2,1)S(1)}, bf16[4,96,768]{2,1,0:T(8,128)(2,1)S(1)}, u32[]{:S(2)}, u32[]{:S(2)}) collective-permute-start(bf16[4,96,768]{2,1,0:T(8,128)(2,1)S(1)} %get-tuple-element.351), channel_id=1, source_target_pairs={{0,16},{4,20},{8,24},{12,28},{16,0},{20,4},{24,8},{28,12},{1,17},{... | collective-permute-start | bytes 1769480 | tf_op jit(solution)/shard_map/ppermute | solution.py:373
  91.1 36.4 %collective-permute-start.25 = (bf16[4,96,768]{2,1,0:T(8,128)(2,1)S(1)}, bf16[4,96,768]{2,1,0:T(8,128)(2,1)S(1)}, u32[]{:S(2)}, u32[]{:S(2)}) collective-permute-start(bf16[4,96,768]{2,1,0:T(8,128)(2,1)S(1)} %get-tuple-element.349), channel_id=1, source_target_pairs={{0,8},{4,12},{8,0},{12,4},{16,24},{20,28},{24,16},{28,20},{1,9},{5... | collective-permute-start | bytes 1769480 | tf_op jit(solution)/shard_map/ppermute | solution.py:373
  139.2 28.9 %collective-permute-start.14 = (bf16[4,96,1536]{2,1,0:T(8,128)(2,1)S(1)}, bf16[4,96,1536]{2,1,0:T(8,128)(2,1)S(1)}, u32[]{:S(2)}, u32[]{:S(2)}) collective-permute-start(bf16[4,96,1536]{2,1,0:T(8,128)(2,1)S(1)} %get-tuple-element.257), channel_id=1, source_target_pairs={{0,8},{4,12},{8,0},{12,4},{16,24},{20,28},{24,16},{28,20},{1,9},{5... | collective-permute-start | bytes 3538952 | tf_op jit(solution)/shard_map/ppermute | solution.py:373
  141.9 28.9 %collective-permute-start.15 = (bf16[4,96,1536]{2,1,0:T(8,128)(2,1)S(1)}, bf16[4,96,1536]{2,1,0:T(8,128)(2,1)S(1)}, u32[]{:S(2)}, u32[]{:S(2)}) collective-permute-start(bf16[4,96,1536]{2,1,0:T(8,128)(2,1)S(1)} %get-tuple-element.257), channel_id=1, source_target_pairs={{0,16},{4,20},{8,24},{12,28},{16,0},{20,4},{24,8},{28,12},{1,17},{... | collective-permute-start | bytes 3538952 | tf_op jit(solution)/shard_map/ppermute | solution.py:373
  143.7 51.1 %collective-permute-start.36 = (bf16[4,96,1536]{2,1,0:T(8,128)(2,1)S(1)}, bf16[4,96,1536]{2,1,0:T(8,128)(2,1)S(1)}, u32[]{:S(2)}, u32[]{:S(2)}) collective-permute-start(bf16[4,96,1536]{2,1,0:T(8,128)(2,1)S(1)} %get-tuple-element.255), channel_id=1, source_target_pairs={{0,8},{4,12},{8,0},{12,4},{16,24},{20,28},{24,16},{28,20},{1,9},{5... | collective-permute-start | bytes 3538952 | tf_op jit(solution)/shard_map/ppermute | solution.py:373
  144.0 50.0 %collective-permute-start.37 = (bf16[4,96,1536]{2,1,0:T(8,128)(2,1)S(1)}, bf16[4,96,1536]{2,1,0:T(8,128)(2,1)S(1)}, u32[]{:S(2)}, u32[]{:S(2)}) collective-permute-start(bf16[4,96,1536]{2,1,0:T(8,128)(2,1)S(1)} %get-tuple-element.255), channel_id=1, source_target_pairs={{0,16},{4,20},{8,24},{12,28},{16,0},{20,4},{24,8},{28,12},{1,17},{... | collective-permute-start | bytes 3538952 | tf_op jit(solution)/shard_map/ppermute | solution.py:373
  146.3 70.5 %collective-permute-start.18 = (bf16[4,96,1536]{2,1,0:T(8,128)(2,1)S(1)}, bf16[4,96,1536]{2,1,0:T(8,128)(2,1)}, u32[]{:S(2)}, u32[]{:S(2)}) collective-permute-start(bf16[4,96,1536]{2,1,0:T(8,128)(2,1)S(1)} %get-tuple-element.257), channel_id=1, source_target_pairs={{0,4},{4,0},{8,12},{12,8},{16,20},{20,16},{24,28},{28,24},{1,5},{5... | collective-permute-start | bytes 3538952 | tf_op jit(solution)/shard_map/ppermute | solution.py:373
  168.1 62.4 %collective-permute-start.40 = (bf16[4,96,1536]{2,1,0:T(8,128)(2,1)S(1)}, bf16[4,96,1536]{2,1,0:T(8,128)(2,1)}, u32[]{:S(2)}, u32[]{:S(2)}) collective-permute-start(bf16[4,96,1536]{2,1,0:T(8,128)(2,1)S(1)} %get-tuple-element.255), channel_id=1, source_target_pairs={{0,4},{4,0},{8,12},{12,8},{16,20},{20,16},{24,28},{28,24},{1,5},{5... | collective-permute-start | bytes 3538952 | tf_op jit(solution)/shard_map/ppermute | solution.py:373
  433.6 30.4 %collective-permute-start.48 = (bf16[4,96,768]{2,1,0:T(8,128)(2,1)S(1)}, bf16[4,96,768]{2,1,0:T(8,128)(2,1)S(1)}, u32[]{:S(2)}, u32[]{:S(2)}) collective-permute-start(bf16[4,96,768]{2,1,0:T(8,128)(2,1)S(1)} %pad_maximum_fusion.21), channel_id=1, source_target_pairs={{0,16},{4,20},{8,24},{12,28},{16,0},{20,4},{24,8},{28,12},{1,17},{... | collective-permute-start | bytes 1769480 | tf_op jit(solution)/shard_map/ppermute | solution.py:373
  438.7 26.5 %collective-permute-start.46 = (bf16[4,96,768]{2,1,0:T(8,128)(2,1)S(1)}, bf16[4,96,768]{2,1,0:T(8,128)(2,1)S(1)}, u32[]{:S(2)}, u32[]{:S(2)}) collective-permute-start(bf16[4,96,768]{2,1,0:T(8,128)(2,1)S(1)} %pad_maximum_fusion.20), channel_id=1, source_target_pairs={{0,8},{4,12},{8,0},{12,4},{16,24},{20,28},{24,16},{28,20},{1,9},{5... | collective-permute-start | bytes 1769480 | tf_op jit(solution)/shard_map/ppermute | solution.py:373
  439.9 36.7 %collective-permute-start.72 = (bf16[4,96,768]{2,1,0:T(8,128)(2,1)S(1)}, bf16[4,96,768]{2,1,0:T(8,128)(2,1)S(1)}, u32[]{:S(2)}, u32[]{:S(2)}) collective-permute-start(bf16[4,96,768]{2,1,0:T(8,128)(2,1)S(1)} %pad_maximum_fusion.27), channel_id=1, source_target_pairs={{0,16},{4,20},{8,24},{12,28},{16,0},{20,4},{24,8},{28,12},{1,17},{... | collective-permute-start | bytes 1769480 | tf_op jit(solution)/shard_map/ppermute | solution.py:373
  451.3 26.5 %collective-permute-start.70 = (bf16[4,96,768]{2,1,0:T(8,128)(2,1)S(1)}, bf16[4,96,768]{2,1,0:T(8,128)(2,1)S(1)}, u32[]{:S(2)}, u32[]{:S(2)}) collective-permute-start(bf16[4,96,768]{2,1,0:T(8,128)(2,1)S(1)} %pad_maximum_fusion.26), channel_id=1, source_target_pairs={{0,8},{4,12},{8,0},{12,4},{16,24},{20,28},{24,16},{28,20},{1,9},{5... | collective-permute-start | bytes 1769480 | tf_op jit(solution)/shard_map/ppermute | solution.py:373
  452.6 36.7 %collective-permute-start.64 = (bf16[4,96,768]{2,1,0:T(8,128)(2,1)S(1)}, bf16[4,96,768]{2,1,0:T(8,128)(2,1)S(1)}, u32[]{:S(2)}, u32[]{:S(2)}) collective-permute-start(bf16[4,96,768]{2,1,0:T(8,128)(2,1)S(1)} %pad_maximum_fusion.25), channel_id=1, source_target_pairs={{0,16},{4,20},{8,24},{12,28},{16,0},{20,4},{24,8},{28,12},{1,17},{... | collective-permute-start | bytes 1769480 | tf_op jit(solution)/shard_map/ppermute | solution.py:373
  464.0 26.5 %collective-permute-start.62 = (bf16[4,96,768]{2,1,0:T(8,128)(2,1)S(1)}, bf16[4,96,768]{2,1,0:T(8,128)(2,1)S(1)}, u32[]{:S(2)}, u32[]{:S(2)}) collective-permute-start(bf16[4,96,768]{2,1,0:T(8,128)(2,1)S(1)} %pad_maximum_fusion.24), channel_id=1, source_target_pairs={{0,8},{4,12},{8,0},{12,4},{16,24},{20,28},{24,16},{28,20},{1,9},{5... | collective-permute-start | bytes 1769480 | tf_op jit(solution)/shard_map/ppermute | solution.py:373
  465.2 36.7 %collective-permute-start.88 = (bf16[4,96,768]{2,1,0:T(8,128)(2,1)S(1)}, bf16[4,96,768]{2,1,0:T(8,128)(2,1)S(1)}, u32[]{:S(2)}, u32[]{:S(2)}) collective-permute-start(bf16[4,96,768]{2,1,0:T(8,128)(2,1)S(1)} %pad_maximum_fusion.32), channel_id=1, source_target_pairs={{0,16},{4,20},{8,24},{12,28},{16,0},{20,4},{24,8},{28,12},{1,17},{... | collective-permute-start | bytes 1769480 | tf_op jit(solution)/shard_map/ppermute | solution.py:373
  476.6 27.2 %collective-permute-start.86 = (bf16[4,96,768]{2,1,0:T(8,128)(2,1)S(1)}, bf16[4,96,768]{2,1,0:T(8,128)(2,1)S(1)}, u32[]{:S(2)}, u32[]{:S(2)}) collective-permute-start(bf16[4,96,768]{2,1,0:T(8,128)(2,1)S(1)} %pad_maximum_fusion.31), channel_id=1, source_target_pairs={{0,8},{4,12},{8,0},{12,4},{16,24},{20,28},{24,16},{28,20},{1,9},{5... | collective-permute-start | bytes 1769480 | tf_op jit(solution)/shard_map/ppermute | solution.py:373
  477.9 35.7 %collective-permute-start.80 = (bf16[4,96,768]{2,1,0:T(8,128)(2,1)S(1)}, bf16[4,96,768]{2,1,0:T(8,128)(2,1)S(1)}, u32[]{:S(2)}, u32[]{:S(2)}) collective-permute-start(bf16[4,96,768]{2,1,0:T(8,128)(2,1)S(1)} %pad_maximum_fusion.30), channel_id=1, source_target_pairs={{0,16},{4,20},{8,24},{12,28},{16,0},{20,4},{24,8},{28,12},{1,17},{... | collective-permute-start | bytes 1769480 | tf_op jit(solution)/shard_map/ppermute | solution.py:373
  490.5 27.0 %collective-permute-start.59 = (bf16[96,768]{1,0:T(8,128)(2,1)S(1)}, bf16[96,768]{1,0:T(8,128)(2,1)S(1)}, u32[]{:S(2)}, u32[]{:S(2)}) collective-permute-start(bf16[96,768]{1,0:T(8,128)(2,1)S(1)} %get-tuple-element.347), channel_id=1, source_target_pairs={{0,1},{1,2},{2,3},{3,0},{4,5},{5,6},{6,7},{7,4},{8,9},{9,10},{10,1... | collective-permute-start | bytes 442376 | tf_op jit(solution)/shard_map/ppermute | solution.py:377
  522.2 26.2 %collective-permute-start.73 = (bf16[96,768]{1,0:T(8,128)(2,1)S(1)}, bf16[96,768]{1,0:T(8,128)(2,1)S(1)}, u32[]{:S(2)}, u32[]{:S(2)}) collective-permute-start(bf16[96,768]{1,0:T(8,128)(2,1)S(1)} %get-tuple-element.340), channel_id=1, source_target_pairs={{0,3},{1,0},{2,1},{3,2},{4,7},{5,4},{6,5},{7,6},{8,11},{9,8},{10,9... | collective-permute-start | bytes 442376 | tf_op jit(solution)/shard_map/ppermute | solution.py:377
  544.9 26.5 %collective-permute-start.91 = (bf16[96,768]{1,0:T(8,128)(2,1)}, bf16[96,768]{1,0:T(8,128)(2,1)}, u32[]{:S(2)}, u32[]{:S(2)}) collective-permute-start(bf16[96,768]{1,0:T(8,128)(2,1)} %get-tuple-element.335), channel_id=1, source_target_pairs={{0,1},{1,2},{2,3},{3,0},{4,5},{5,6},{6,7},{7,4},{8,9},{9,10},{10,1... | collective-permute-start | bytes 442376 | tf_op jit(solution)/shard_map/ppermute | solution.py:377
  (142 other events, 1585.6 us)

commit v2 on v1

v2 whole, which is shorter than its diff:
```python
import functools

import jax
import jax.numpy as jnp
from jax import lax
from jax.experimental import pallas as pl
from jax.experimental.pallas import tpu as pltpu
from jax.sharding import PartitionSpec as P

HEADS = 12
LAYERS = 2
STEP = 3
D = 768
FF = 3072
HD = 64
BLOCKS = 4
ROWS = 208
QKV_W = 3 * D // BLOCKS
OUT_W = D // BLOCKS
UP_W = FF // BLOCKS
PIECE = 96

norm_eps = 1e-06
root_half = 0.7071067811865476
inv_root_two_pi = 0.3989422804014327
beta_one = 0.9
beta_two = 0.999
adam_eps = 1e-08
learn_rate = 0.06
decay_rate = 0.05

BF = jnp.bfloat16
F32 = jnp.float32


def dot_nn(a, b):
    return lax.dot_general(a, b, (((1,), (0,)), ((), ())), preferred_element_type=F32)


def dot_nt(a, b):
    return lax.dot_general(a, b, (((1,), (1,)), ((), ())), preferred_element_type=F32)


def dot_tn(a, b):
    return lax.dot_general(a, b, (((0,), (0,)), ((), ())), preferred_element_type=F32)


def scaled_rows(x):
    center = jnp.mean(x, axis=-1, keepdims=True)
    shifted = x - center
    inverse = lax.rsqrt(jnp.mean(shifted * shifted, axis=-1, keepdims=True) + norm_eps)
    return shifted * inverse, inverse


def norm_back(upstream, scaled, inverse, gain):
    grad_scaled = upstream * gain
    mean_one = jnp.mean(grad_scaled, axis=-1, keepdims=True)
    mean_two = jnp.mean(grad_scaled * scaled, axis=-1, keepdims=True)
    grad_gain = jnp.sum(upstream * scaled, axis=0, keepdims=True)
    return inverse * (grad_scaled - mean_one - scaled * mean_two), grad_gain


def block_of(turn, s):
    return jnp.bitwise_xor(turn, s)


FFN_W = 2 * UP_W


def piece_copies(info_ref, refs, column, w, sems):
    copies = []
    for s in range(BLOCKS):
        row = []
        for index, ref in enumerate(refs):
            for part in range(8 if ref.shape[1] == 8 else 4):
                if ref.shape[1] == 8:
                    block = part
                    lanes = slice(0, w.shape[2])
                    source = ref.at[
                        block_of(info_ref[0], s), jnp.bitwise_xor(info_ref[1], part), :,
                        column : column + w.shape[2],
                    ]
                else:
                    block = 2 * part + index % 2
                    lanes = slice(index // 2 * D, (index // 2 + 1) * D)
                    source = ref.at[part, s]
                target = w.at[s, block * PIECE : (block + 1) * PIECE, lanes]
                row.append(pltpu.make_async_copy(source, target, sems.at[s, len(row)]))
        copies.append(row)
    return copies


def start_all(copies):
    for row in copies:
        for copy in row:
            copy.start()


def wait_row(row):
    for copy in row:
        copy.wait()


def flip_features(x, mask):
    place = lax.broadcasted_iota(jnp.int32, x.shape, 1)
    block = jnp.zeros(x.shape, jnp.int32)
    for edge in range(1, D // PIECE):
        block = block + (place >= edge * PIECE).astype(jnp.int32)
    for bit in range(3):
        size = PIECE << bit
        even = ((block >> bit) & 1) == 0
        swapped = jnp.where(even, pltpu.roll(x, D - size, axis=1), pltpu.roll(x, size, axis=1))
        x = jnp.where(jnp.full(x.shape, (mask >> bit) & 1, jnp.int32) == 1, swapped, x)
    return x


def prepare_kernel(
    seq, info_ref, counts_ref, images_ref, cot_ref, gains_ref, biases_ref, bup_ref,
    x_ref, g_ref, gains_out, biases_out, bup_out,
):
    mask = info_ref[1]
    live = (info_ref[2] < counts_ref[info_ref[3]]).astype(F32)
    x_ref[ROWS - 16 : ROWS, :] = jnp.zeros((16, D), F32)
    g_ref[ROWS - 16 : ROWS, :] = jnp.zeros((16, D), F32)
    x_ref[0:seq, :] = flip_features(images_ref[0], mask)
    g_ref[0:seq, :] = flip_features(cot_ref[0], mask) * live
    gains_out[...] = flip_features(gains_ref[...], mask)
    biases_out[...] = flip_features(biases_ref[...], mask)
    for level in range(LAYERS):
        for s in range(BLOCKS):
            bup_out[level, s] = bup_ref[level * BLOCKS + block_of(info_ref[0], s)]


def finish_kernel(seq, extra, info_ref, counts_ref, y_ref, *rest):
    out_ref = rest[extra]
    live = (info_ref[2] < counts_ref[info_ref[3]]).astype(F32)
    out_ref[0] = flip_features(y_ref[...], info_ref[1])[0:seq] * live


def attend_kernel(seq, level, n_pieces, info_ref, x_ref, gain_ref, bias_ref, *rest):
    pieces = rest[:n_pieces]
    qkv_ref, lse_ref, oext_ref, h1_ref, a2_ref, blk, w, sems = rest[n_pieces:]
    copies = piece_copies(info_ref, pieces, 0, w, sems)
    start_all(copies)
    turn = info_ref[0]
    x = x_ref[...]
    scaled, _ = scaled_rows(x)
    a1 = (scaled * gain_ref[2 * level : 2 * level + 1, :]).astype(BF)
    for s in range(BLOCKS):
        wait_row(copies[s])
        t = dot_nn(a1, w[s, :, 0:640])
        blk[block_of(turn, s)] = t.astype(BF)
    for b in range(BLOCKS):
        qkv_ref[:, b * QKV_W : (b + 1) * QKV_W] = blk[b, :, 0:QKV_W]
    low_half = lax.broadcasted_iota(jnp.int32, (ROWS, 128), 1) < HD
    key_live = lax.broadcasted_iota(jnp.int32, (ROWS, ROWS), 0) < seq
    scale = HD ** (-0.5)
    oext_ref[:, :, 0:HD] = jnp.zeros((BLOCKS, ROWS, HD), BF)
    for pair in range(HEADS // 2):
        q2 = qkv_ref[:, pair * 128 : (pair + 1) * 128]
        k2 = qkv_ref[:, D + pair * 128 : D + (pair + 1) * 128]
        v2 = qkv_ref[:, 2 * D + pair * 128 : 2 * D + (pair + 1) * 128]
        mixed = []
        for half in range(2):
            live = low_half if half == 0 else jnp.logical_not(low_half)
            qm = jnp.where(live, q2, jnp.zeros_like(q2))
            st = jnp.where(key_live, dot_nt(k2, qm) * scale, -1e30)
            peak = jnp.max(st, axis=0, keepdims=True)
            grown = jnp.exp(st - peak)
            total = jnp.sum(grown, axis=0, keepdims=True)
            head = 2 * pair + half
            lse_ref[head : head + 1, :] = peak + jnp.log(total)
            probs = (grown * (1.0 / total)).astype(BF)
            mixed.append(dot_tn(probs, v2))
        both = jnp.where(low_half, mixed[0], mixed[1]).astype(BF)
        for half in range(2):
            head = 2 * pair + half
            lane = HD + (head % 3) * HD
            oext_ref[head // 3, :, lane : lane + HD] = both[:, half * HD : (half + 1) * HD]
    total = x + bias_ref[2 * level : 2 * level + 1, :]
    for s in range(BLOCKS):
        total = total + dot_nt(oext_ref[block_of(turn, s)], w[s, :, 512:768])
    h1_ref[...] = total
    scaled2, _ = scaled_rows(total)
    a2_ref[...] = (scaled2 * gain_ref[2 * level + 1 : 2 * level + 2, :]).astype(BF)


def feed_kernel(level, n_pieces, info_ref, h1_ref, a2_ref, bias_ref, bup_ref, *rest):
    pieces = rest[:n_pieces]
    z_ref, slope_ref, y_ref, w, sems = rest[n_pieces:]
    s = pl.program_id(0)
    copies = piece_copies(info_ref, pieces, D, w, sems)

    @pl.when(s == 0)
    def _():
        start_all(copies)
        y_ref[...] = h1_ref[...] + bias_ref[2 * level + 1 : 2 * level + 2, :]

    for step in range(BLOCKS):

        @pl.when(s == step)
        def _():
            wait_row(copies[step])

    u = dot_nn(a2_ref[...], w[s, :, 0:UP_W]) + bup_ref[0, 0]
    bell = 0.5 * (1.0 + lax.erf(u * root_half))
    z = (u * bell).astype(BF)
    z_ref[0] = z
    slope_ref[0] = bell + u * inv_root_two_pi * jnp.exp(-0.5 * u * u)
    y_ref[...] += dot_nt(z, w[s, :, UP_W:FFN_W])


def put_grad(near_ref, far_ref, value, first, width):
    for j in range(8):
        ref = near_ref if j % 2 == 0 else far_ref
        ref[j // 2, 0, :, first : first + width] = value[j * PIECE : (j + 1) * PIECE]


def feed_back_kernel(level, n_pieces, n_after, info_ref, g_ref, h1_ref, a2_ref, gain_ref, z_ref, slope_ref, *rest):
    pieces = rest[:n_pieces]
    near_ref, far_ref, bup_ref, dh1_ref, sums_ref, da2, gb_t, a2_t, w, sems = rest[n_pieces + n_after :]
    s = pl.program_id(0)
    copies = piece_copies(info_ref, pieces, D, w, sems)

    @pl.when(s == 0)
    def _():
        start_all(copies)
        da2[...] = jnp.zeros_like(da2)
        gb_t[...] = g_ref[...].T.astype(BF)
        a2_t[...] = a2_ref[...].T

    for step in range(BLOCKS):

        @pl.when(s == step)
        def _():
            wait_row(copies[step])

    gb = g_ref[...].astype(BF)
    put_grad(near_ref, far_ref, dot_nn(gb_t[...], z_ref[0]).astype(BF), UP_W, UP_W)
    du = dot_nn(gb, w[s, :, UP_W:FFN_W]) * slope_ref[0]
    bup_ref[0] = jnp.sum(du, axis=0, keepdims=True)
    dub = du.astype(BF)
    put_grad(near_ref, far_ref, dot_nn(a2_t[...], dub).astype(BF), 0, UP_W)
    da2[...] += dot_nt(dub, w[s, :, 0:UP_W])

    @pl.when(s == BLOCKS - 1)
    def _():
        g = g_ref[...]
        scaled, inverse = scaled_rows(h1_ref[...])
        below, grad_gain = norm_back(da2[...], scaled, inverse, gain_ref[2 * level + 1 : 2 * level + 2, :])
        dh1 = below + g
        dh1_ref[...] = dh1
        sums_ref[0:1, :] = grad_gain
        sums_ref[1:2, :] = jnp.sum(dh1, axis=0, keepdims=True)
        sums_ref[2:3, :] = jnp.sum(g, axis=0, keepdims=True)


def attend_back_kernel(
    seq, level, n_pieces, n_after,
    info_ref, dh1_ref, x_ref, gain_ref, qkv_ref, lse_ref, oext_ref, sums_in, bup_in, *rest,
):
    pieces = rest[:n_pieces]
    near_ref, far_ref, below_ref, small_ref, dext, dmix, dqkv, dqx, w, sems = rest[n_pieces + n_after :]
    copies = piece_copies(info_ref, pieces, 0, w, sems)
    start_all(copies)
    turn = info_ref[0]
    dh1 = dh1_ref[...]
    hb = dh1.astype(BF)
    hb_t = dh1.T.astype(BF)
    for s in range(BLOCKS):
        wait_row(copies[s])
        dext[block_of(turn, s)] = dot_nn(hb, w[s, :, 512:768]).astype(BF)
    for b in range(BLOCKS):
        dmix[:, b * OUT_W : (b + 1) * OUT_W] = dext[b, :, HD : HD + OUT_W]
    low_half = lax.broadcasted_iota(jnp.int32, (ROWS, 128), 1) < HD
    key_live = lax.broadcasted_iota(jnp.int32, (ROWS, ROWS), 0) < seq
    scale = HD ** (-0.5)
    for pair in range(HEADS // 2):
        q2 = qkv_ref[:, pair * 128 : (pair + 1) * 128]
        k2 = qkv_ref[:, D + pair * 128 : D + (pair + 1) * 128]
        v2 = qkv_ref[:, 2 * D + pair * 128 : 2 * D + (pair + 1) * 128]
        d2 = dmix[:, pair * 128 : (pair + 1) * 128]
        dq = jnp.zeros((ROWS, 128), F32)
        dk = jnp.zeros((ROWS, 128), F32)
        dv = jnp.zeros((ROWS, 128), F32)
        for half in range(2):
            head = 2 * pair + half
            live = low_half if half == 0 else jnp.logical_not(low_half)
            none = jnp.zeros_like(q2)
            qm = jnp.where(live, q2, none)
            km = jnp.where(live, k2, none)
            dm = jnp.where(live, d2, none)
            st = jnp.where(key_live, dot_nt(k2, qm) * scale, -1e30)
            probs = jnp.exp(st - lse_ref[head : head + 1, :])
            dprobs = dot_nt(v2, dm)
            inner = jnp.sum(probs * dprobs, axis=0, keepdims=True)
            dst = (probs * (dprobs - inner) * scale).astype(BF)
            dv = dv + dot_nn(probs.astype(BF), dm)
            dk = dk + dot_nn(dst, qm)
            dq = dq + dot_tn(dst, km)
        dqkv[:, pair * 128 : (pair + 1) * 128] = dq.astype(BF)
        dqkv[:, D + pair * 128 : D + (pair + 1) * 128] = dk.astype(BF)
        dqkv[:, 2 * D + pair * 128 : 2 * D + (pair + 1) * 128] = dv.astype(BF)
    for b in range(BLOCKS):
        dqx[b, :, 0:QKV_W] = dqkv[:, b * QKV_W : (b + 1) * QKV_W]
        dqx[b, :, QKV_W:640] = jnp.zeros((ROWS, 640 - QKV_W), BF)
    gain = gain_ref[2 * level : 2 * level + 1, :]
    scaled, inverse = scaled_rows(x_ref[...])
    a1_t = (scaled * gain).T.astype(BF)
    da1 = jnp.zeros((ROWS, D), F32)
    for s in range(BLOCKS):
        own = block_of(turn, s)
        part = dqx[own]
        da1 = da1 + dot_nt(part, w[s, :, 0:640])
        first = dot_nn(a1_t, part)
        second = dot_nn(hb_t, oext_ref[own])
        for j in range(8):
            ref = near_ref if j % 2 == 0 else far_ref
            rows = slice(j * PIECE, (j + 1) * PIECE)
            ref[j // 2, s, :, 0:512] = first[rows, 0:512].astype(BF)
            ref[j // 2, s, :, 512:640] = (first[rows, 512:640] + second[rows, 0:128]).astype(BF)
            ref[j // 2, s, :, 640:768] = second[rows, 128:256].astype(BF)
    below, grad_gain = norm_back(da1, scaled, inverse, gain)
    below = below + dh1
    if level == 0:
        below_ref[0] = flip_features(below, info_ref[1])[0:seq]
    else:
        below_ref[...] = below
    small_ref[0:1, :] = grad_gain
    small_ref[1:4, :] = sums_in[0:3, :]
    small_ref[4:8, :] = jnp.zeros((4, D), F32)
    small_ref[...] = flip_features(small_ref[...], info_ref[1])
    for s in range(BLOCKS):
        small_ref[pl.ds(4 + block_of(turn, s), 1), :] = bup_in[s]


VM = pl.BlockSpec(memory_space=pltpu.VMEM)
SM = pl.BlockSpec(memory_space=pltpu.SMEM)
HB = pl.BlockSpec(memory_space=pl.ANY)
LIMIT = 60 * 1024 * 1024


def sds(shape, dtype):
    return jax.ShapeDtypeStruct(shape, dtype)


def params():
    return pltpu.CompilerParams(vmem_limit_bytes=LIMIT)


def cost(flops, traffic):
    return pl.CostEstimate(flops=flops, bytes_accessed=traffic, transcendentals=0)


def weight_scratch(width):
    return [pltpu.VMEM((BLOCKS, D, width), BF), pltpu.SemaphoreType.DMA((BLOCKS, 16))]


def prepare(seq, info, counts, images, cotangent, gains, biases, bup):
    return pl.pallas_call(
        functools.partial(prepare_kernel, seq),
        out_shape=(
            sds((ROWS, D), F32), sds((ROWS, D), F32), sds(gains.shape, F32), sds(biases.shape, F32),
            sds((LAYERS, BLOCKS, 1, UP_W), F32),
        ),
        in_specs=[SM, SM] + [VM] * 5,
        out_specs=[VM] * 5,
        compiler_params=params(),
        cost_estimate=cost(10**7, 10**5),
        name="prepare",
    )(info, counts, images, cotangent, gains, biases, bup)


def finish(seq, info, counts, y, after):
    return pl.pallas_call(
        functools.partial(finish_kernel, seq, len(after)),
        out_shape=sds((1, seq, D), F32),
        in_specs=[SM, SM, VM] + [HB] * len(after),
        out_specs=VM,
        compiler_params=params(),
        cost_estimate=cost(10**7, 10**5),
        name="finish",
    )(info, counts, y, *after)


def attend(seq, level, info, x, gains, biases, pieces):
    return pl.pallas_call(
        functools.partial(attend_kernel, seq, level, len(pieces)),
        out_shape=(
            sds((ROWS, 3 * D), BF), sds((16, ROWS), F32), sds((BLOCKS, ROWS, 256), BF),
            sds((ROWS, D), F32), sds((ROWS, D), BF),
        ),
        in_specs=[SM] + [VM] * 3 + [HB] * len(pieces),
        out_specs=[VM] * 5,
        scratch_shapes=[pltpu.VMEM((BLOCKS, ROWS, 640), BF)] + weight_scratch(D),
        compiler_params=params(),
        cost_estimate=cost(10**7, 10**5),
        name="attend",
    )(info, x, gains, biases, *pieces)


def whole(shape):
    return pl.BlockSpec(shape, lambda s: (0,) * len(shape))


def feed(level, info, h1, a2, biases, bup, pieces):
    return pl.pallas_call(
        functools.partial(feed_kernel, level, len(pieces)),
        grid=(BLOCKS,),
        out_shape=(sds((BLOCKS, ROWS, UP_W), BF), sds((BLOCKS, ROWS, UP_W), F32), sds((ROWS, D), F32)),
        in_specs=[
            SM, whole((ROWS, D)), whole((ROWS, D)), whole(biases.shape),
            pl.BlockSpec((1, 1, 1, UP_W), lambda s: (level, s, 0, 0)),
        ]
        + [HB] * len(pieces),
        out_specs=[
            pl.BlockSpec((1, ROWS, UP_W), lambda s: (s, 0, 0)),
            pl.BlockSpec((1, ROWS, UP_W), lambda s: (s, 0, 0)),
            whole((ROWS, D)),
        ],
        scratch_shapes=weight_scratch(FFN_W),
        compiler_params=params(),
        cost_estimate=cost(10**7, 10**5),
        name="feed",
    )(info, h1, a2, biases, bup, *pieces)


def feed_back(level, info, g, h1, a2, gains, z, slope, pieces, after):
    grad = sds((4, BLOCKS, PIECE, FFN_W), BF)
    grad_spec = pl.BlockSpec((4, 1, PIECE, FFN_W), lambda s: (0, s, 0, 0))
    step_spec = pl.BlockSpec((1, ROWS, UP_W), lambda s: (s, 0, 0))
    return pl.pallas_call(
        functools.partial(feed_back_kernel, level, len(pieces), len(after)),
        grid=(BLOCKS,),
        out_shape=(grad, grad, sds((BLOCKS, 1, UP_W), F32), sds((ROWS, D), F32), sds((8, D), F32)),
        in_specs=[SM, whole((ROWS, D)), whole((ROWS, D)), whole((ROWS, D)), whole(gains.shape), step_spec, step_spec]
        + [HB] * (len(pieces) + len(after)),
        out_specs=[
            grad_spec, grad_spec,
            pl.BlockSpec((1, 1, UP_W), lambda s: (s, 0, 0)), whole((ROWS, D)), whole((8, D)),
        ],
        scratch_shapes=[pltpu.VMEM((ROWS, D), F32), pltpu.VMEM((D, ROWS), BF), pltpu.VMEM((D, ROWS), BF)]
        + weight_scratch(FFN_W),
        compiler_params=params(),
        cost_estimate=cost(10**7, 10**5),
        name="feed_back",
    )(info, g, h1, a2, gains, z, slope, *pieces, *after)


def attend_back(seq, level, info, dh1, x, gains, qkv, lse, oext, sums, bup, pieces, after):
    grad = sds((4, BLOCKS, PIECE, D), BF)
    below = sds((1, seq, D), F32) if level == 0 else sds((ROWS, D), F32)
    return pl.pallas_call(
        functools.partial(attend_back_kernel, seq, level, len(pieces), len(after)),
        out_shape=(grad, grad, below, sds((8, D), F32)),
        in_specs=[SM] + [VM] * 8 + [HB] * (len(pieces) + len(after)),
        out_specs=[VM] * 4,
        scratch_shapes=[
            pltpu.VMEM((BLOCKS, ROWS, 256), BF), pltpu.VMEM((ROWS, D), BF),
            pltpu.VMEM((ROWS, 3 * D), BF), pltpu.VMEM((BLOCKS, ROWS, 640), BF),
        ]
        + weight_scratch(D),
        compiler_params=params(),
        cost_estimate=cost(10**7, 10**5),
        name="attend_back",
    )(info, dh1, x, gains, qkv, lse, oext, sums, bup, *pieces, *after)


def adamw_step(param, gradient, first_moment, second_moment):
    fresh_first = beta_one * first_moment + (1.0 - beta_one) * gradient
    fresh_second = beta_two * second_moment + (1.0 - beta_two) * gradient * gradient
    first_hat = fresh_first / (1.0 - beta_one**STEP)
    second_hat = fresh_second / (1.0 - beta_two**STEP)
    updated = param - learn_rate * (
        first_hat / (jnp.sqrt(second_hat) + adam_eps) + decay_rate * param
    )
    return (updated, fresh_first, fresh_second)


def after(value, *earlier):
    return lax.optimization_barrier((value,) + earlier)[0]


class PlainPlan:
    def __init__(self, mesh):
        self.n_row = mesh.shape["row"]
        self.n_col = mesh.shape["col"]
        self.turn = jnp.int32(0)
        self.mask = jnp.int32(0)

    def gather(self, shard, widths):
        full = lax.all_gather(shard, ("col", "row"), axis=0, tiled=True)
        full = full.reshape(self.n_col, D, sum(widths))
        parts = []
        start = 0
        for width in widths:
            part = full[:, :, start : start + width].transpose(1, 0, 2)
            parts.append(part.reshape(D, BLOCKS, -1).transpose(1, 0, 2))
            start += width
        return jnp.concatenate(parts, axis=2).reshape(BLOCKS, 8, PIECE, -1)

    def reduce(self, near, far, widths, *earlier):
        full = jnp.stack([near, far], axis=1).transpose(0, 1, 3, 2, 4)
        full = full.reshape(D, BLOCKS, -1)
        parts = []
        start = 0
        for width in widths:
            wide = width * self.n_col // BLOCKS
            part = full[:, :, start : start + wide].reshape(D, self.n_col, width)
            parts.append(part.transpose(1, 0, 2))
            start += wide
        packed = jnp.concatenate(parts, axis=2).reshape(self.n_col * D, sum(widths))
        done = lax.psum_scatter(packed, ("col", "row"), scatter_dimension=0, tiled=True).astype(F32)
        for _ in range(2):
            yield done
        yield done, done
        yield done
        yield done

    def total(self, values, stages):
        return lax.psum(values, ("row", "col"))


def flip_row(x, mask):
    return lax.ppermute(x, "row", [(i, i ^ mask) for i in range(8)])


def flip_col(x, mask):
    return lax.ppermute(x, "col", [(i, i ^ mask) for i in range(4)])


CORE, NEXT_X, NEXT_Y = 1, 2, 4


class RelativeFetch:
    def __init__(self, shard):
        self.shard = shard

    def turn_one(self, *hold):
        shard = after(self.shard, *hold)
        self.pair = jnp.stack([shard, flip_col(shard, 1)])
        return self.pair[1]

    def turn_two(self, *hold):
        self.others = flip_col(after(self.pair, *hold), 2)
        return self.others

    def plane(self, *hold):
        self.own = after(jnp.concatenate([self.pair, self.others], axis=0), *hold)
        self.from_x = flip_row(self.own, NEXT_X)
        self.from_y = flip_row(self.own, NEXT_Y)
        return self.from_x

    def rest(self, *hold):
        from_x, from_y = after(self.from_x, self.from_y, *hold), after(self.from_y, self.from_x, *hold)
        diag_low = flip_row(from_y[0:2], NEXT_X)
        diag_high = flip_row(from_x[2:4], NEXT_Y)
        near = jnp.concatenate([self.own, from_x, from_y, diag_low, diag_high], axis=0)
        near = near.reshape((4, BLOCKS) + self.shard.shape)
        return [near, flip_row(near, CORE)]


class RelativePlan:
    def __init__(self, mesh):
        self.turn = lax.axis_index("col").astype(jnp.int32)
        self.mask = lax.axis_index("row").astype(jnp.int32)

    def gather(self, shard, widths):
        full = lax.all_gather(shard, ("col", "row"), axis=0, tiled=True)
        return full.reshape(BLOCKS, 8, PIECE, -1)

    def reduce(self, near, far, widths, *earlier):
        far = after(far, *earlier)
        other = flip_row(far, CORE)
        hold = yield other

        def joined(m, blocks):
            return near[m, blocks].astype(F32) + other[m, blocks].astype(F32)

        low, high, every = slice(0, 2), slice(2, 4), slice(0, 4)
        diag_low = flip_row(after(joined(3, low).astype(BF), *hold), NEXT_X)
        diag_high = flip_row(after(joined(3, high).astype(BF), *hold), NEXT_Y)
        hold = yield diag_low, diag_high
        to_x = jnp.concatenate([joined(1, low), joined(1, high) + diag_high.astype(F32)], axis=0)
        to_y = jnp.concatenate([joined(2, low) + diag_low.astype(F32), joined(2, high)], axis=0)
        from_x = flip_row(after(to_x.astype(BF), *hold), NEXT_X)
        from_y = flip_row(after(to_y.astype(BF), *hold), NEXT_Y)
        hold = yield from_x, from_y
        plane = joined(0, every) + from_x.astype(F32) + from_y.astype(F32)
        others = flip_col(after(plane[2:4].astype(BF), *hold), 2)
        hold = yield others
        pair = plane[0:2] + after(others, *hold).astype(F32)
        yield pair[0] + flip_col(pair[1].astype(BF), 1).astype(F32)

    def total(self, values, stages):
        hops = [(flip_row, CORE), (flip_row, NEXT_X), (flip_row, NEXT_Y), (flip_col, 1), (flip_col, 2)]
        for (flip, mask), stage in zip(hops, stages):
            values = values + after(flip(values, mask), *stage)
        return values


def per_device(
    mesh,
    images, cotangent, counts, w_qkv, w_out, w_up, w_down, norm_gains, res_biases, b_up,
    m_qkv, m_out, m_up, m_down, m_gains, m_biases, m_bup,
    v_qkv, v_out, v_up, v_down, v_gains, v_biases, v_bup,
):
    seq = images.shape[1]
    relative = mesh.shape["row"] == 8 and mesh.shape["col"] == 4
    plan = RelativePlan(mesh) if relative else PlainPlan(mesh)
    info = jnp.stack([plan.turn, plan.mask, lax.axis_index("col"), lax.axis_index("row")]).astype(jnp.int32)
    att_widths = (w_qkv.shape[2], w_out.shape[1])
    ffn_widths = (w_up.shape[2], w_down.shape[1])
    shards = []
    for level in range(LAYERS):
        shards.append([
            jnp.concatenate([w_qkv[level].astype(BF), w_out[level].T.astype(BF)], axis=1),
            w_up[level].astype(BF),
            w_down[level].T.astype(BF),
        ])

    hidden, upstream, gains, biases, bup = prepare(
        seq, info, counts, images, cotangent,
        norm_gains.reshape(2 * LAYERS, D), res_biases.reshape(2 * LAYERS, D),
        b_up.reshape(LAYERS * BLOCKS, 1, UP_W),
    )
    saved, att_full, ffn_full = [], [], []

    def forward_attend(level, hidden, pieces):
        att_full.append(pieces)
        return attend(seq, level, info, hidden, gains, biases, pieces)

    def forward_feed(level, hidden, state, pieces):
        qkv, lse, oext, h1, a2 = state
        ffn_full.append(pieces)
        z, slope, y = feed(level, info, h1, a2, biases, bup, pieces)
        saved.append((hidden, qkv, lse, oext, h1, a2, z, slope))
        return y

    def gathered(level):
        return [plan.gather(jnp.concatenate(shards[level], axis=1), att_widths + ffn_widths)]

    later = gathered(1)
    if relative:
        fetches = [RelativeFetch(shard) for shard in shards[0]]
        one = fetches[0].turn_one()
        two = fetches[0].turn_two()
        plane, arrived = (), []
        for index, fetch in enumerate(fetches):
            plane = (fetch.plane(*plane),)
            if index + 1 < len(fetches):
                one = fetches[index + 1].turn_one(one)
                two = fetches[index + 1].turn_two(two)
            arrived.append(fetch.rest(two))
        sooner = arrived[0], arrived[1] + arrived[2]
    else:
        sooner = (gathered(0),) * 2
    state = forward_attend(0, hidden, sooner[0])
    middle = forward_feed(0, hidden, state, sooner[1])
    state = forward_attend(1, middle, later)
    hidden = forward_feed(1, middle, state, later)
    smalls = [None] * LAYERS

    def backward_feed(level, upstream, landed):
        below, qkv, lse, oext, h1, a2, z, slope = saved[level]
        return feed_back(level, info, upstream, h1, a2, gains, z, slope, ffn_full[level], landed)

    def backward_attend(level, dh1, sums, bup_sum, landed):
        below, qkv, lse, oext, h1, a2, z, slope = saved[level]
        return attend_back(
            seq, level, info, dh1, below, gains, qkv, lse, oext, sums, bup_sum, att_full[level], landed
        )

    near, far, bup_sum, dh1, sums = backward_feed(1, upstream, [])
    ffn_one = plan.reduce(near, far, ffn_widths)
    core_ffn_one = next(ffn_one)
    near, far, upstream, smalls[1] = backward_attend(1, dh1, sums, bup_sum, [])
    one_near, one_far = near, far
    near, far, bup_sum, dh1, sums = backward_feed(0, upstream, [core_ffn_one])
    diag_ffn_one = ffn_one.send(())
    zero_near, zero_far = near, far
    near, far, upstream, smalls[0] = backward_attend(0, dh1, sums, bup_sum, [*diag_ffn_one])
    plane_ffn_one = ffn_one.send(())
    att_one = plan.reduce(one_near, one_far, att_widths, smalls[0])
    core_att_one = next(att_one)
    ffn_zero = plan.reduce(zero_near, zero_far, ffn_widths, smalls[0], core_att_one)
    core_ffn_zero = next(ffn_zero)
    att_zero = plan.reduce(near, far, att_widths, core_ffn_zero)
    core_att_zero = next(att_zero)
    diag_att_one = att_one.send(diag_ffn_one)
    plane_att_one = att_one.send(())
    diag_ffn_zero = ffn_zero.send(plane_ffn_one)
    plane_ffn_zero = ffn_zero.send(())
    diag_att_zero = att_zero.send(plane_att_one)
    plane_att_zero = att_zero.send(())
    turn_ffn_one, turn_att_one = ffn_one.send((smalls[0],)), att_one.send(())
    turn_ffn_zero, turn_att_zero = ffn_zero.send(()), att_zero.send(())
    done = {}
    done["ffn", 1], done["att", 1] = ffn_one.send(diag_ffn_zero), att_one.send(plane_ffn_zero)
    done["ffn", 0], done["att", 0] = ffn_zero.send(plane_att_zero), att_zero.send(())
    layer_out = finish(seq, info, counts, hidden, [upstream])
    grads = []
    for level in range(LAYERS):
        ffn, att = done["ffn", level], done["att", level]
        grads.append((
            att[:, : att_widths[0]], att[:, att_widths[0] :].T, ffn[:, : ffn_widths[0]], ffn[:, ffn_widths[0] :].T
        ))
    stages = [plane_ffn_one, diag_att_one, plane_att_one, diag_ffn_zero, plane_ffn_zero]
    small = plan.total(jnp.concatenate(smalls, axis=0), stages).reshape(LAYERS, 8, D)
    grad_list = [jnp.stack([grads[level][index] for level in range(LAYERS)]) for index in range(4)]
    grad_list += [small[:, 0:2], small[:, 2:4], small[:, 4:8].reshape(LAYERS, FF)]
    params_in = [w_qkv, w_out, w_up, w_down, norm_gains, res_biases, b_up]
    firsts = [m_qkv, m_out, m_up, m_down, m_gains, m_biases, m_bup]
    seconds = [v_qkv, v_out, v_up, v_down, v_gains, v_biases, v_bup]
    results = [
        adamw_step(params_in[index], grad_list[index], firsts[index], seconds[index])
        for index in range(7)
    ]
    return (
        (layer_out, upstream)
        + tuple(grad_list)
        + tuple(result[0] for result in results[:4])
        + tuple(result[1] for result in results)
        + tuple(result[2] for result in results)
    )


def solution(mesh):
    tokens = P(("row", "col"), None, None)
    matrices = (P(None, "row", "col"), P(None, "col", "row"), P(None, "row", "col"), P(None, "col", "row"))
    vectors = (P(), P(), P())
    in_specs = (tokens, tokens, P()) + (matrices + vectors) * 3
    out_specs = (tokens, tokens) + matrices + vectors + matrices + (matrices + vectors) * 2
    return jax.shard_map(
        functools.partial(per_device, mesh), mesh=mesh, in_specs=in_specs, out_specs=out_specs, check_vma=False
    )
```

time: 591 us -> 451 us (0.76)
  local copies, waits for them, and re-layouts: 115 us -> 28.6 us
  starting transfers between devices: 122 us -> 75.7 us
  other arithmetic: 51 us -> 36.5 us
  waiting for transfers between devices: 207 us -> 194 us
  Pallas kernels: 81.7 us -> 93.3 us
  between operations: 4.02 us -> 15.3 us
    ppermute x68 -> x38, waiting for transfers between devices: 158 us -> 98.2 us  [flip_row(): return lax.ppermute(x, 'row', [(i, i ^ mask) for i in range(8)])]
    ppermute x34 -> x16, waiting for transfers between devices: 48.9 us -> 96 us  [flip_col(): return lax.ppermute(x, 'col', [(i, i ^ mask) for i in range(4)])]
    ppermute x34 -> x16, starting transfers between devices: 69.3 us -> 42.4 us  [flip_col(): return lax.ppermute(x, 'col', [(i, i ^ mask) for i in range(4)])]
    reshape x44 -> x3, local copies, waits for them, and re-layouts: 30.2 us -> 3.32 us  [the longest x1 1.38 us: per_device(): b_up.reshape(LAYERS * BLOCKS, 1, UP_W)]
    concatenate x32 -> x5, local copies, waits for them, and re-layouts: 26 us -> 2.35 us  [the longest x3 1.48 us: rest(): jnp.concatenate([self.own, from_x, from_y, diag_low, diag_high], axis=0)]
    ppermute x68 -> x38, starting transfers between devices: 53 us -> 33.2 us  [flip_row(): return lax.ppermute(x, 'row', [(i, i ^ mask) for i in range(8)])]
    pallas_call x8 -> x10, Pallas kernels: 81.7 us -> 93.3 us  [the longest x2 27.3 us: attend_back(): pl.pallas_call(functools.partial(attend_back_kernel, seq, level, len(piec...]
    slice x43 -> x10, local copies, waits for them, and re-layouts: 11.7 us -> 0.31 us  [the longest x4 0.19 us: reduce(): others = flip_col(after(plane[2:4].astype(BF), *hold), 2)]
  transfers between devices with their start and end apart: 102 -> 55, of which waited for: 46 -> 23; matrix products, arithmetic and copies ran while one was open for 19% -> 11% of each run, Pallas kernels for 4% -> 11%
where the time goes in v2:
time: 451 us; the launch traced here: 444 us
  waiting for transfers between devices  194 us (43%)
  Pallas kernels  93.3 us (21%)
  starting transfers between devices  75.7 us (17%)
  other arithmetic  36.5 us (8%)
  local copies, waits for them, and re-layouts  28.6 us (6%)
  between operations  15.3 us (3%)
    ppermute x38, waiting for transfers between devices, flip_row(): return lax.ppermute(x, 'row', [(i, i ^ mask) for i in range(8)])  98.2 us
    ppermute x16, waiting for transfers between devices, flip_col(): return lax.ppermute(x, 'col', [(i, i ^ mask) for i in range(4)])  96 us
    ppermute x16, starting transfers between devices, flip_col(): return lax.ppermute(x, 'col', [(i, i ^ mask) for i in range(4)])  42.4 us
    ppermute x38, starting transfers between devices, flip_row(): return lax.ppermute(x, 'row', [(i, i ^ mask) for i in range(8)])  33.2 us
    pallas_call x2, Pallas kernels, attend_back(): pl.pallas_call(functools.partial(attend_back_kernel, seq, level, len(piec...  27.3 us
    pallas_call x2, Pallas kernels, feed_back(): pl.pallas_call(functools.partial(feed_back_kernel, level, len(pieces), le...  25.8 us
    unnamed x110, local copies, waits for them, and re-layouts  22.2 us
    pallas_call x2, Pallas kernels, feed(): pl.pallas_call(functools.partial(feed_kernel, level, len(pieces)), grid=(...  17.7 us
  transfers between devices with their start and end apart: 55, of which 23 were waited for; matrix products, arithmetic and copies ran while one was open for 11% of the time, Pallas kernels for 11%

profile of v2, /device:TPU:0, one launch (start us, length us, event | category | flops | bytes accessed | tf_op | source)
XLA Modules:
  0.0 443.6 jit_solution(4842869028621578789)
XLA Ops:
  13.8 3.8 collective-permute-done
  22.1 20.6 %collective-permute-done.1 = bf16[2,96,768]{2,1,0:T(8,128)(2,1)S(1)} collective-permute-done((bf16[2,96,768]{2,1,0:T(8,128)(2,1)S(1)}, bf16[2,96,768]{2,1,0:T(8,128)(2,1)S(1)}, u32[]{:S(2)}, u32[]{:S(2)}) %collective-permute-start.1) | collective-permute-done | bytes 294944 | tf_op jit(solution)/shard_map/ppermute | solution.py:529
  46.4 3.4 collective-permute-start.5
  50.7 24.5 %collective-permute-done.5 = bf16[2,96,768]{2,1,0:T(8,128)(2,1)S(1)} collective-permute-done((bf16[2,96,768]{2,1,0:T(8,128)(2,1)S(1)}, bf16[2,96,768]{2,1,0:T(8,128)(2,1)S(1)}, u32[]{:S(2)}, u32[]{:S(2)}) %collective-permute-start.5) | collective-permute-done | bytes 294944 | tf_op jit(solution)/shard_map/ppermute | solution.py:529
  83.3 10.8 %collective-permute-done.12 = bf16[2,96,768]{2,1,0:T(8,128)(2,1)S(1)} collective-permute-done((bf16[2,96,768]{2,1,0:T(8,128)(2,1)S(1)}, bf16[2,96,768]{2,1,0:T(8,128)(2,1)S(1)}, u32[]{:S(2)}, u32[]{:S(2)}) %collective-permute-start.12) | collective-permute-done | bytes 294944 | tf_op jit(solution)/shard_map/ppermute | solution.py:529
  100.9 34.9 %collective-permute-done.13 = bf16[2,96,768]{2,1,0:T(8,128)(2,1)S(1)} collective-permute-done((bf16[2,96,768]{2,1,0:T(8,128)(2,1)S(1)}, bf16[2,96,768]{2,1,0:T(8,128)(2,1)S(1)}, u32[]{:S(2)}, u32[]{:S(2)}) %collective-permute-start.13) | collective-permute-done | bytes 294944 | tf_op jit(solution)/shard_map/ppermute | solution.py:525
  138.9 8.5 %collective-permute-done.18 = bf16[2,96,768]{2,1,0:T(8,128)(2,1)S(1)} collective-permute-done((bf16[2,96,768]{2,1,0:T(8,128)(2,1)S(1)}, bf16[2,96,768]{2,1,0:T(8,128)(2,1)S(1)}, u32[]{:S(2)}, u32[]{:S(2)}) %collective-permute-start.18) | collective-permute-done | bytes 294944 | tf_op jit(solution)/shard_map/ppermute | solution.py:525
  160.0 8.6 %attend.2 = (bf16[208,2304]{1,0:T(8,128)(2,1)}, f32[16,208]{1,0:T(8,128)}, bf16[4,208,256]{2,1,0:T(8,128)(2,1)}, f32[208,768]{1,0:T(8,128)}, bf16[208,768]{1,0:T(8,128)(2,1)}) custom-call(s32[4]{0:T(128)} %pad_add_fusion.info_ref, f32[208,768]{1,0:T(8,128)} %get-tuple-element.96.x_ref, f32[4,768]{1,0:T(4,128)} %get-tuple-element.97.gain_ref, ...), custom_call_target="tpu_custom_call" | custom-call | flops 10000000 | bytes 100000 | tf_op jit(solution)/shard_map/attend/pallas_call | solution.py:387
  168.6 9.0 %feed.2 = (bf16[4,208,768]{2,1,0:T(8,128)(2,1)}, f32[4,208,768]{2,1,0:T(8,128)}, f32[208,768]{1,0:T(8,128)}) custom-call(s32[4]{0:T(128)} %pad_add_fusion.info_ref, f32[208,768]{1,0:T(8,128)} %get-tuple-element.103.h1_ref, bf16[208,768]{1,0:T(8,128)(2,1)} %get-tuple-element.104.a2_ref, f32[4,768]{1,0:T(4,128)} %get-tuple-element.98.bias_ref, ...), custom_call_target="tpu_custom_call" | custom-call | flops 10000000 | bytes 100000 | tf_op jit(solution)/shard_map/feed/pallas_call | solution.py:407
  177.7 7.9 %attend.3 = (bf16[208,2304]{1,0:T(8,128)(2,1)}, f32[16,208]{1,0:T(8,128)}, bf16[4,208,256]{2,1,0:T(8,128)(2,1)}, f32[208,768]{1,0:T(8,128)}, bf16[208,768]{1,0:T(8,128)(2,1)}) custom-call(s32[4]{0:T(128)} %pad_add_fusion.info_ref, f32[208,768]{1,0:T(8,128)} %get-tuple-element.114.x_ref, f32[4,768]{1,0:T(4,128)} %get-tuple-element.97.gain_ref, ...), custom_call_target="tpu_custom_call" | custom-call | flops 10000000 | bytes 100000 | tf_op jit(solution)/shard_map/attend/pallas_call | solution.py:387
  185.7 8.6 %feed.3 = (bf16[4,208,768]{2,1,0:T(8,128)(2,1)}, f32[4,208,768]{2,1,0:T(8,128)}, f32[208,768]{1,0:T(8,128)}) custom-call(s32[4]{0:T(128)} %pad_add_fusion.info_ref, f32[208,768]{1,0:T(8,128)} %get-tuple-element.115.h1_ref, bf16[208,768]{1,0:T(8,128)(2,1)} %get-tuple-element.116.a2_ref, f32[4,768]{1,0:T(4,128)} %get-tuple-element.98.bias_ref, ...), custom_call_target="tpu_custom_call" | custom-call | flops 10000000 | bytes 100000 | tf_op jit(solution)/shard_map/feed/pallas_call | solution.py:407
  194.3 13.1 %feed_back.2 = (bf16[4,4,96,1536]{3,2,1,0:T(8,128)(2,1)}, bf16[4,4,96,1536]{3,2,1,0:T(8,128)(2,1)}, f32[4,1,768]{2,1,0:T(1,128)}, f32[208,768]{1,0:T(8,128)}, f32[8,768]{1,0:T(8,128)}) custom-call(s32[4]{0:T(128)} %pad_add_fusion.info_ref, f32[208,768]{1,0:T(8,128)} %get-tuple-element.118.g_ref, f32[208,768]{1,0:T(8,128)} %get-tuple-element.115.h1_ref, ...), custom_call_target="tpu_custom_call" | custom-call | flops 10000000 | bytes 100000 | tf_op jit(solution)/shard_map/feed_back/pallas_call | solution.py:432
  207.9 7.7 %collective-permute-done.21.rest_4_ = bf16[4,4,96,1536]{3,2,1,0:T(8,128)(2,1)S(1)} collective-permute-done((bf16[4,4,96,1536]{3,2,1,0:T(8,128)(2,1)}, bf16[4,4,96,1536]{3,2,1,0:T(8,128)(2,1)S(1)}, u32[]{:S(2)}, u32[]{:S(2)}) %collective-permute-start.21) | collective-permute-done | bytes 4718624 | tf_op jit(solution)/shard_map/ppermute | solution.py:525
  215.7 5.0 %fusion.15 = (bf16[2,96,1536]{2,1,0:T(8,128)(2,1)S(1)}, bf16[2,96,1536]{2,1,0:T(8,128)(2,1)S(1)}, bf16[2,96,1536]{2,1,0:T(8,128)(2,1)}, bf16[2,96,1536]{2,1,0:T(8,128)(2,1)}) fusion(bf16[4,4,96,1536]{3,2,1,0:T(8,128)(2,1)S(1)} %collective-permute-done.21.rest_4_, bf16[4,4,96,1536]{3,2,1,0:T(8,128)(2,1)} %get-tuple-element.137), kind=kLoop, calls=%fused_computation.42 | loop fusion | flops 4718592 | bytes 7077888 | tf_op jit(solution)/shard_map/add | solution.py:578
  221.8 13.7 %attend_back.2 = (bf16[4,4,96,768]{3,2,1,0:T(8,128)(2,1)}, bf16[4,4,96,768]{3,2,1,0:T(8,128)(2,1)}, f32[208,768]{1,0:T(8,128)}, f32[8,768]{1,0:T(8,128)}) custom-call(s32[4]{0:T(128)} %pad_add_fusion.info_ref, f32[208,768]{1,0:T(8,128)} %get-tuple-element.121.dh1_ref, f32[208,768]{1,0:T(8,128)} %get-tuple-element.114.x_ref, ...), custom_call_target="tpu_custom_call" | custom-call | flops 10000000 | bytes 100000 | tf_op jit(solution)/shard_map/attend_back/pallas_call | solution.py:453
  235.5 12.7 %feed_back.3 = (bf16[4,4,96,1536]{3,2,1,0:T(8,128)(2,1)}, bf16[4,4,96,1536]{3,2,1,0:T(8,128)(2,1)}, f32[4,1,768]{2,1,0:T(1,128)}, f32[208,768]{1,0:T(8,128)}, f32[8,768]{1,0:T(8,128)}) custom-call(s32[4]{0:T(128)} %pad_add_fusion.info_ref, f32[208,768]{1,0:T(8,128)} %get-tuple-element.127.g_ref, f32[208,768]{1,0:T(8,128)} %get-tuple-element.103.h1_ref, ...), custom_call_target="tpu_custom_call" | custom-call | flops 10000000 | bytes 100000 | tf_op jit(solution)/shard_map/feed_back/pallas_call | solution.py:432
  249.3 13.5 %attend_back.3 = (bf16[4,4,96,768]{3,2,1,0:T(8,128)(2,1)}, bf16[4,4,96,768]{3,2,1,0:T(8,128)(2,1)}, f32[1,197,768]{2,1,0:T(8,128)}, f32[8,768]{1,0:T(8,128)}) custom-call(s32[4]{0:T(128)} %pad_add_fusion.info_ref, f32[208,768]{1,0:T(8,128)} %get-tuple-element.131.dh1_ref, f32[208,768]{1,0:T(8,128)} %get-tuple-element.96.x_ref, ...), custom_call_target="tpu_custom_call" | custom-call | flops 10000000 | bytes 100000 | tf_op jit(solution)/shard_map/attend_back/pallas_call | solution.py:453
  263.0 4.7 %collective-permute-done.24 = bf16[4,4,96,768]{3,2,1,0:T(8,128)(2,1)S(1)} collective-permute-done((bf16[4,4,96,768]{3,2,1,0:T(8,128)(2,1)}, bf16[4,4,96,768]{3,2,1,0:T(8,128)(2,1)S(1)}, u32[]{:S(2)}, u32[]{:S(2)}) %collective-permute-start.24) | collective-permute-done | bytes 2359328 | tf_op jit(solution)/shard_map/ppermute | solution.py:525
  286.8 14.4 %collective-permute-done.38 = bf16[4,96,1536]{2,1,0:T(8,128)(2,1)} collective-permute-done((bf16[4,96,1536]{2,1,0:T(8,128)(2,1)}, bf16[4,96,1536]{2,1,0:T(8,128)(2,1)}, u32[]{:S(2)}, u32[]{:S(2)}) %collective-permute-start.38) | collective-permute-done | bytes 1179680 | tf_op jit(solution)/shard_map/ppermute | solution.py:525
  305.3 3.5 collective-permute-done.27
  322.7 4.9 %collective-permute-done.51 = f32[16,768]{1,0:T(8,128)S(1)} collective-permute-done((f32[16,768]{1,0:T(8,128)S(1)}, f32[16,768]{1,0:T(8,128)S(1)}, u32[]{:S(2)}, u32[]{:S(2)}) %collective-permute-start.51) | collective-permute-done | bytes 49184 | tf_op jit(solution)/shard_map/ppermute | solution.py:525
  328.5 13.1 %collective-permute-start.52 = (f32[16,768]{1,0:T(8,128)S(1)}, f32[16,768]{1,0:T(8,128)S(1)}, u32[]{:S(2)}, u32[]{:S(2)}) collective-permute-start(f32[16,768]{1,0:T(8,128)S(1)} %add.391), channel_id=1, source_target_pairs={{0,1},{1,0},{2,3},{3,2},{4,5},{5,4},{6,7},{7,6},{8,9},{9,8},{10,11... | collective-permute-start | bytes 147464 | tf_op jit(solution)/shard_map/ppermute | solution.py:529
  346.6 6.3 %collective-permute-done.47 = bf16[2,96,1536]{2,1,0:T(8,128)(2,1)S(1)} collective-permute-done((bf16[2,96,1536]{2,1,0:T(8,128)(2,1)S(1)}, bf16[2,96,1536]{2,1,0:T(8,128)(2,1)S(1)}, u32[]{:S(2)}, u32[]{:S(2)}) %collective-permute-start.47) | collective-permute-done | bytes 589856 | tf_op jit(solution)/shard_map/ppermute | solution.py:529
  353.1 4.0 collective-permute-start.48
  358.8 5.7 %collective-permute-done.48 = bf16[96,1536]{1,0:T(8,128)(2,1)S(1)} collective-permute-done((bf16[96,1536]{1,0:T(8,128)(2,1)S(1)}, bf16[96,1536]{1,0:T(8,128)(2,1)S(1)}, u32[]{:S(2)}, u32[]{:S(2)}) %collective-permute-start.48) | collective-permute-done | bytes 294944 | tf_op jit(solution)/shard_map/ppermute | solution.py:529
  367.2 6.2 %collective-permute-done.37 = bf16[2,96,768]{2,1,0:T(8,128)(2,1)S(1)} collective-permute-done((bf16[2,96,768]{2,1,0:T(8,128)(2,1)S(1)}, bf16[2,96,768]{2,1,0:T(8,128)(2,1)S(1)}, u32[]{:S(2)}, u32[]{:S(2)}) %collective-permute-start.37) | collective-permute-done | bytes 294944 | tf_op jit(solution)/shard_map/ppermute | solution.py:529
  373.5 7.6 %collective-permute-start.44 = (bf16[96,768]{1,0:T(8,128)(2,1)S(1)}, bf16[96,768]{1,0:T(8,128)(2,1)S(1)}, u32[]{:S(2)}, u32[]{:S(2)}) collective-permute-start(bf16[96,768]{1,0:T(8,128)(2,1)S(1)} %fusion.39), channel_id=1, source_target_pairs={{0,1},{1,0},{2,3},{3,2},{4,5},{5,4},{6,7},{7,6},{8,9},{9,8},{10,11... | collective-permute-start | bytes 442376 | tf_op jit(solution)/shard_map/ppermute | solution.py:529
  387.9 4.3 collective-permute-done.31
  395.9 9.2 %collective-permute-done.34 = bf16[4,96,768]{2,1,0:T(8,128)(2,1)S(1)} collective-permute-done((bf16[4,96,768]{2,1,0:T(8,128)(2,1)S(1)}, bf16[4,96,768]{2,1,0:T(8,128)(2,1)S(1)}, u32[]{:S(2)}, u32[]{:S(2)}) %collective-permute-start.34) | collective-permute-done | bytes 589856 | tf_op jit(solution)/shard_map/ppermute | solution.py:525
  408.6 7.2 %collective-permute-done.45 = bf16[2,96,1536]{2,1,0:T(8,128)(2,1)S(1)} collective-permute-done((bf16[2,96,1536]{2,1,0:T(8,128)(2,1)S(1)}, bf16[2,96,1536]{2,1,0:T(8,128)(2,1)S(1)}, u32[]{:S(2)}, u32[]{:S(2)}) %collective-permute-start.45) | collective-permute-done | bytes 589856 | tf_op jit(solution)/shard_map/ppermute | solution.py:529
  416.0 4.9 %collective-permute-done.35 = bf16[2,96,768]{2,1,0:T(8,128)(2,1)S(1)} collective-permute-done((bf16[2,96,768]{2,1,0:T(8,128)(2,1)S(1)}, bf16[2,96,768]{2,1,0:T(8,128)(2,1)S(1)}, u32[]{:S(2)}, u32[]{:S(2)}) %collective-permute-start.35) | collective-permute-done | bytes 294944 | tf_op jit(solution)/shard_map/ppermute | solution.py:529
  421.1 6.1 %collective-permute-done.46 = bf16[96,1536]{1,0:T(8,128)(2,1)S(1)} collective-permute-done((bf16[96,1536]{1,0:T(8,128)(2,1)S(1)}, bf16[96,1536]{1,0:T(8,128)(2,1)S(1)}, u32[]{:S(2)}, u32[]{:S(2)}) %collective-permute-start.46) | collective-permute-done | bytes 294944 | tf_op jit(solution)/shard_map/ppermute | solution.py:529
  (284 shorter events, 119.8 us)
Async XLA Ops:
  7.2 170.5 %all-gather.2.cloned.1.call-start = ((), (), s32[]{:S(2)}) async-start(), calls=%async_computation | async-start | bytes 14598144 | tf_op jit(solution)/shard_map/all_gather | solution.py:569
  17.7 25.0 %collective-permute-start.1 = (bf16[2,96,768]{2,1,0:T(8,128)(2,1)S(1)}, bf16[2,96,768]{2,1,0:T(8,128)(2,1)S(1)}, u32[]{:S(2)}, u32[]{:S(2)}) collective-permute-start(bf16[2,96,768]{2,1,0:T(8,128)(2,1)S(1)} %pad_maximum_fusion.14), channel_id=1, source_target_pairs={{0,2},{1,3},{2,0},{3,1},{4,6},{5,7},{6,4},{7,5},{8,10},{9,11},{10,... | collective-permute-start | bytes 884744 | tf_op jit(solution)/shard_map/ppermute | solution.py:529
  20.5 23.6 %collective-permute-start.4 = (bf16[96,768]{1,0:T(8,128)(2,1)S(1)}, bf16[96,768]{1,0:T(8,128)(2,1)S(1)}, u32[]{:S(2)}, u32[]{:S(2)}) collective-permute-start(bf16[96,768]{1,0:T(8,128)(2,1)S(1)} %get-tuple-element.99), channel_id=1, source_target_pairs={{0,1},{1,0},{2,3},{3,2},{4,5},{5,4},{6,7},{7,6},{8,9},{9,8},{10,11... | collective-permute-start | bytes 442376 | tf_op jit(solution)/shard_map/ppermute | solution.py:529
  42.7 32.5 %collective-permute-start.2 = (bf16[4,96,768]{2,1,0:T(8,128)(2,1)S(1)}, bf16[4,96,768]{2,1,0:T(8,128)(2,1)S(1)}, u32[]{:S(2)}, u32[]{:S(2)}) collective-permute-start(bf16[4,96,768]{2,1,0:T(8,128)(2,1)S(1)} %pad_maximum_fusion.4), channel_id=1, source_target_pairs={{0,8},{4,12},{8,0},{12,4},{16,24},{20,28},{24,16},{28,20},{1,9},{5... | collective-permute-start | bytes 1769480 | tf_op jit(solution)/shard_map/ppermute | solution.py:525
  44.8 34.6 %collective-permute-start.3 = (bf16[4,96,768]{2,1,0:T(8,128)(2,1)S(1)}, bf16[4,96,768]{2,1,0:T(8,128)(2,1)S(1)}, u32[]{:S(2)}, u32[]{:S(2)}) collective-permute-start(bf16[4,96,768]{2,1,0:T(8,128)(2,1)S(1)} %pad_maximum_fusion.4), channel_id=1, source_target_pairs={{0,16},{4,20},{8,24},{12,28},{16,0},{20,4},{24,8},{28,12},{1,17},{... | collective-permute-start | bytes 1769480 | tf_op jit(solution)/shard_map/ppermute | solution.py:525
  46.4 28.8 %collective-permute-start.5 = (bf16[2,96,768]{2,1,0:T(8,128)(2,1)S(1)}, bf16[2,96,768]{2,1,0:T(8,128)(2,1)S(1)}, u32[]{:S(2)}, u32[]{:S(2)}) collective-permute-start(bf16[2,96,768]{2,1,0:T(8,128)(2,1)S(1)} %pad_maximum_fusion.15), channel_id=1, source_target_pairs={{0,2},{1,3},{2,0},{3,1},{4,6},{5,7},{6,4},{7,5},{8,10},{9,11},{10,... | collective-permute-start | bytes 884744 | tf_op jit(solution)/shard_map/ppermute | solution.py:529
  75.2 18.9 %collective-permute-start.12 = (bf16[2,96,768]{2,1,0:T(8,128)(2,1)S(1)}, bf16[2,96,768]{2,1,0:T(8,128)(2,1)S(1)}, u32[]{:S(2)}, u32[]{:S(2)}) collective-permute-start(bf16[2,96,768]{2,1,0:T(8,128)(2,1)S(1)} %pad_maximum_fusion.16), channel_id=1, source_target_pairs={{0,2},{1,3},{2,0},{3,1},{4,6},{5,7},{6,4},{7,5},{8,10},{9,11},{10,... | collective-permute-start | bytes 884744 | tf_op jit(solution)/shard_map/ppermute | solution.py:529
  75.3 19.7 %collective-permute-start.9 = (bf16[4,96,768]{2,1,0:T(8,128)(2,1)S(1)}, bf16[4,96,768]{2,1,0:T(8,128)(2,1)S(1)}, u32[]{:S(2)}, u32[]{:S(2)}) collective-permute-start(bf16[4,96,768]{2,1,0:T(8,128)(2,1)S(1)} %pad_maximum_fusion.5), channel_id=1, source_target_pairs={{0,8},{4,12},{8,0},{12,4},{16,24},{20,28},{24,16},{28,20},{1,9},{5... | collective-permute-start | bytes 1769480 | tf_op jit(solution)/shard_map/ppermute | solution.py:525
  94.9 40.8 %collective-permute-start.16 = (bf16[4,96,768]{2,1,0:T(8,128)(2,1)S(1)}, bf16[4,96,768]{2,1,0:T(8,128)(2,1)S(1)}, u32[]{:S(2)}, u32[]{:S(2)}) collective-permute-start(bf16[4,96,768]{2,1,0:T(8,128)(2,1)S(1)} %pad_maximum_fusion.6), channel_id=1, source_target_pairs={{0,8},{4,12},{8,0},{12,4},{16,24},{20,28},{24,16},{28,20},{1,9},{5... | collective-permute-start | bytes 1769480 | tf_op jit(solution)/shard_map/ppermute | solution.py:525
  95.5 40.3 %collective-permute-start.17 = (bf16[4,96,768]{2,1,0:T(8,128)(2,1)S(1)}, bf16[4,96,768]{2,1,0:T(8,128)(2,1)S(1)}, u32[]{:S(2)}, u32[]{:S(2)}) collective-permute-start(bf16[4,96,768]{2,1,0:T(8,128)(2,1)S(1)} %pad_maximum_fusion.6), channel_id=1, source_target_pairs={{0,16},{4,20},{8,24},{12,28},{16,0},{20,4},{24,8},{28,12},{1,17},{... | collective-permute-start | bytes 1769480 | tf_op jit(solution)/shard_map/ppermute | solution.py:525
  96.8 63.3 %collective-permute-start.8 = (bf16[4,4,96,768]{3,2,1,0:T(8,128)(2,1)}, bf16[4,4,96,768]{3,2,1,0:T(8,128)(2,1)}, u32[]{:S(2)}, u32[]{:S(2)}) collective-permute-start(bf16[4,4,96,768]{3,2,1,0:T(8,128)(2,1)} %bitcast.10.rest_0_), channel_id=1, source_target_pairs={{0,4},{4,0},{8,12},{12,8},{16,20},{20,16},{24,28},{28,24},{1,5},{5... | collective-permute-start | bytes 7077896 | tf_op jit(solution)/shard_map/ppermute | solution.py:525
  96.8 38.9 %collective-permute-start.13 = (bf16[2,96,768]{2,1,0:T(8,128)(2,1)S(1)}, bf16[2,96,768]{2,1,0:T(8,128)(2,1)S(1)}, u32[]{:S(2)}, u32[]{:S(2)}) collective-permute-start(bf16[2,96,768]{2,1,0:T(8,128)(2,1)S(1)} %slice.313), channel_id=1, source_target_pairs={{0,8},{4,12},{8,0},{12,4},{16,24},{20,28},{24,16},{28,20},{1,9},{5... | collective-permute-start | bytes 884744 | tf_op jit(solution)/shard_map/ppermute | solution.py:525
  99.3 37.2 %collective-permute-start.14 = (bf16[2,96,768]{2,1,0:T(8,128)(2,1)S(1)}, bf16[2,96,768]{2,1,0:T(8,128)(2,1)S(1)}, u32[]{:S(2)}, u32[]{:S(2)}) collective-permute-start(bf16[2,96,768]{2,1,0:T(8,128)(2,1)S(1)} %slice.314), channel_id=1, source_target_pairs={{0,16},{4,20},{8,24},{12,28},{16,0},{20,4},{24,8},{28,12},{1,17},{... | collective-permute-start | bytes 884744 | tf_op jit(solution)/shard_map/ppermute | solution.py:525
  136.5 32.1 %collective-permute-start.15 = (bf16[4,4,96,768]{3,2,1,0:T(8,128)(2,1)S(1)}, bf16[4,4,96,768]{3,2,1,0:T(8,128)(2,1)}, u32[]{:S(2)}, u32[]{:S(2)}) collective-permute-start(bf16[4,4,96,768]{3,2,1,0:T(8,128)(2,1)S(1)} %bitcast.173), channel_id=1, source_target_pairs={{0,4},{4,0},{8,12},{12,8},{16,20},{20,16},{24,28},{28,24},{1,5},{5... | collective-permute-start | bytes 7077896 | tf_op jit(solution)/shard_map/ppermute | solution.py:525
  148.9 19.8 %collective-permute-start.20 = (bf16[4,4,96,768]{3,2,1,0:T(8,128)(2,1)}, bf16[4,4,96,768]{3,2,1,0:T(8,128)(2,1)}, u32[]{:S(2)}, u32[]{:S(2)}) collective-permute-start(bf16[4,4,96,768]{3,2,1,0:T(8,128)(2,1)} %bitcast.16.rest_2_), channel_id=1, source_target_pairs={{0,4},{4,0},{8,12},{12,8},{16,20},{20,16},{24,28},{28,24},{1,5},{5... | collective-permute-start | bytes 7077896 | tf_op jit(solution)/shard_map/ppermute | solution.py:525
  220.6 27.7 %collective-permute-start.22 = (bf16[2,96,1536]{2,1,0:T(8,128)(2,1)}, bf16[2,96,1536]{2,1,0:T(8,128)(2,1)S(1)}, u32[]{:S(2)}, u32[]{:S(2)}) collective-permute-start(bf16[2,96,1536]{2,1,0:T(8,128)(2,1)} %get-tuple-element.222), channel_id=1, source_target_pairs={{0,8},{4,12},{8,0},{12,4},{16,24},{20,28},{24,16},{28,20},{1,9},{5... | collective-permute-start | bytes 1769480 | tf_op jit(solution)/shard_map/ppermute | solution.py:525
  221.3 27.0 %collective-permute-start.23 = (bf16[2,96,1536]{2,1,0:T(8,128)(2,1)}, bf16[2,96,1536]{2,1,0:T(8,128)(2,1)S(1)}, u32[]{:S(2)}, u32[]{:S(2)}) collective-permute-start(bf16[2,96,1536]{2,1,0:T(8,128)(2,1)} %get-tuple-element.221), channel_id=1, source_target_pairs={{0,16},{4,20},{8,24},{12,28},{16,0},{20,4},{24,8},{28,12},{1,17},{... | collective-permute-start | bytes 1769480 | tf_op jit(solution)/shard_map/ppermute | solution.py:525
  267.7 45.7 %collective-permute-start.25 = (bf16[4,4,96,1536]{3,2,1,0:T(8,128)(2,1)}, bf16[4,4,96,1536]{3,2,1,0:T(8,128)(2,1)}, u32[]{:S(2)}, u32[]{:S(2)}) collective-permute-start(bf16[4,4,96,1536]{3,2,1,0:T(8,128)(2,1)} %get-tuple-element.145), channel_id=1, source_target_pairs={{0,4},{4,0},{8,12},{12,8},{16,20},{20,16},{24,28},{28,24},{1,5},{5... | collective-permute-start | bytes 14155784 | tf_op jit(solution)/shard_map/ppermute | solution.py:525
  272.1 29.1 %collective-permute-start.38 = (bf16[4,96,1536]{2,1,0:T(8,128)(2,1)}, bf16[4,96,1536]{2,1,0:T(8,128)(2,1)}, u32[]{:S(2)}, u32[]{:S(2)}) collective-permute-start(bf16[4,96,1536]{2,1,0:T(8,128)(2,1)} %pad_maximum_fusion), channel_id=1, source_target_pairs={{0,8},{4,12},{8,0},{12,4},{16,24},{20,28},{24,16},{28,20},{1,9},{5... | collective-permute-start | bytes 3538952 | tf_op jit(solution)/shard_map/ppermute | solution.py:525
  274.2 29.1 %collective-permute-start.39 = (bf16[4,96,1536]{2,1,0:T(8,128)(2,1)}, bf16[4,96,1536]{2,1,0:T(8,128)(2,1)}, u32[]{:S(2)}, u32[]{:S(2)}) collective-permute-start(bf16[4,96,1536]{2,1,0:T(8,128)(2,1)} %pad_maximum_fusion.1), channel_id=1, source_target_pairs={{0,16},{4,20},{8,24},{12,28},{16,0},{20,4},{24,8},{28,12},{1,17},{... | collective-permute-start | bytes 3538952 | tf_op jit(solution)/shard_map/ppermute | solution.py:525
  277.4 31.3 %collective-permute-start.27 = (bf16[2,96,768]{2,1,0:T(8,128)(2,1)}, bf16[2,96,768]{2,1,0:T(8,128)(2,1)}, u32[]{:S(2)}, u32[]{:S(2)}) collective-permute-start(bf16[2,96,768]{2,1,0:T(8,128)(2,1)} %get-tuple-element.148), channel_id=1, source_target_pairs={{0,16},{4,20},{8,24},{12,28},{16,0},{20,4},{24,8},{28,12},{1,17},{... | collective-permute-start | bytes 884744 | tf_op jit(solution)/shard_map/ppermute | solution.py:525
  278.1 30.6 %collective-permute-start.29 = (bf16[2,96,768]{2,1,0:T(8,128)(2,1)}, bf16[2,96,768]{2,1,0:T(8,128)(2,1)}, u32[]{:S(2)}, u32[]{:S(2)}) collective-permute-start(bf16[2,96,768]{2,1,0:T(8,128)(2,1)} %get-tuple-element.149), channel_id=1, source_target_pairs={{0,8},{4,12},{8,0},{12,4},{16,24},{20,28},{24,16},{28,20},{1,9},{5... | collective-permute-start | bytes 884744 | tf_op jit(solution)/shard_map/ppermute | solution.py:525
  316.8 24.8 %collective-permute-start.42 = (bf16[2,96,1536]{2,1,0:T(8,128)(2,1)S(1)}, bf16[2,96,1536]{2,1,0:T(8,128)(2,1)S(1)}, u32[]{:S(2)}, u32[]{:S(2)}) collective-permute-start(bf16[2,96,1536]{2,1,0:T(8,128)(2,1)S(1)} %get-tuple-element.154), channel_id=1, source_target_pairs={{0,8},{4,12},{8,0},{12,4},{16,24},{20,28},{24,16},{28,20},{1,9},{5... | collective-permute-start | bytes 1769480 | tf_op jit(solution)/shard_map/ppermute | solution.py:525
  318.0 23.6 %collective-permute-start.40 = (bf16[2,96,1536]{2,1,0:T(8,128)(2,1)S(1)}, bf16[2,96,1536]{2,1,0:T(8,128)(2,1)S(1)}, u32[]{:S(2)}, u32[]{:S(2)}) collective-permute-start(bf16[2,96,1536]{2,1,0:T(8,128)(2,1)S(1)} %get-tuple-element.153), channel_id=1, source_target_pairs={{0,16},{4,20},{8,24},{12,28},{16,0},{20,4},{24,8},{28,12},{1,17},{... | collective-permute-start | bytes 1769480 | tf_op jit(solution)/shard_map/ppermute | solution.py:525
  327.7 25.2 %collective-permute-start.47 = (bf16[2,96,1536]{2,1,0:T(8,128)(2,1)S(1)}, bf16[2,96,1536]{2,1,0:T(8,128)(2,1)S(1)}, u32[]{:S(2)}, u32[]{:S(2)}) collective-permute-start(bf16[2,96,1536]{2,1,0:T(8,128)(2,1)S(1)} %slice.572), channel_id=1, source_target_pairs={{0,2},{1,3},{2,0},{3,1},{4,6},{5,7},{6,4},{7,5},{8,10},{9,11},{10,... | collective-permute-start | bytes 1769480 | tf_op jit(solution)/shard_map/ppermute | solution.py:529
  328.5 30.3 %collective-permute-start.52 = (f32[16,768]{1,0:T(8,128)S(1)}, f32[16,768]{1,0:T(8,128)S(1)}, u32[]{:S(2)}, u32[]{:S(2)}) collective-permute-start(f32[16,768]{1,0:T(8,128)S(1)} %add.391), channel_id=1, source_target_pairs={{0,1},{1,0},{2,3},{3,2},{4,5},{5,4},{6,7},{7,6},{8,9},{9,8},{10,11... | collective-permute-start | bytes 147464 | tf_op jit(solution)/shard_map/ppermute | solution.py:529
  343.4 30.0 %collective-permute-start.41 = (bf16[4,96,1536]{2,1,0:T(8,128)(2,1)S(1)}, bf16[4,96,1536]{2,1,0:T(8,128)(2,1)S(1)}, u32[]{:S(2)}, u32[]{:S(2)}) collective-permute-start(bf16[4,96,1536]{2,1,0:T(8,128)(2,1)S(1)} %pad_maximum_fusion.2), channel_id=1, source_target_pairs={{0,8},{4,12},{8,0},{12,4},{16,24},{20,28},{24,16},{28,20},{1,9},{5... | collective-permute-start | bytes 3538952 | tf_op jit(solution)/shard_map/ppermute | solution.py:525
  345.3 28.1 %collective-permute-start.43 = (bf16[4,96,1536]{2,1,0:T(8,128)(2,1)S(1)}, bf16[4,96,1536]{2,1,0:T(8,128)(2,1)S(1)}, u32[]{:S(2)}, u32[]{:S(2)}) collective-permute-start(bf16[4,96,1536]{2,1,0:T(8,128)(2,1)S(1)} %pad_maximum_fusion.3), channel_id=1, source_target_pairs={{0,16},{4,20},{8,24},{12,28},{16,0},{20,4},{24,8},{28,12},{1,17},{... | collective-permute-start | bytes 3538952 | tf_op jit(solution)/shard_map/ppermute | solution.py:525
  358.8 25.5 %collective-permute-start.26 = (bf16[4,4,96,768]{3,2,1,0:T(8,128)(2,1)S(1)}, bf16[4,4,96,768]{3,2,1,0:T(8,128)(2,1)S(1)}, u32[]{:S(2)}, u32[]{:S(2)}) collective-permute-start(bf16[4,4,96,768]{3,2,1,0:T(8,128)(2,1)S(1)} %copy-done.39), channel_id=1, source_target_pairs={{0,4},{4,0},{8,12},{12,8},{16,20},{20,16},{24,28},{28,24},{1,5},{5... | collective-permute-start | bytes 7077896 | tf_op jit(solution)/shard_map/ppermute | solution.py:525
  364.5 19.0 %collective-permute-start.53 = (f32[16,768]{1,0:T(8,128)S(1)}, f32[16,768]{1,0:T(8,128)S(1)}, u32[]{:S(2)}, u32[]{:S(2)}) collective-permute-start(f32[16,768]{1,0:T(8,128)S(1)} %add.392), channel_id=1, source_target_pairs={{0,2},{1,3},{2,0},{3,1},{4,6},{5,7},{6,4},{7,5},{8,10},{9,11},{10,... | collective-permute-start | bytes 147464 | tf_op jit(solution)/shard_map/ppermute | solution.py:529
  373.5 22.2 %collective-permute-start.44 = (bf16[96,768]{1,0:T(8,128)(2,1)S(1)}, bf16[96,768]{1,0:T(8,128)(2,1)S(1)}, u32[]{:S(2)}, u32[]{:S(2)}) collective-permute-start(bf16[96,768]{1,0:T(8,128)(2,1)S(1)} %fusion.39), channel_id=1, source_target_pairs={{0,1},{1,0},{2,3},{3,2},{4,5},{5,4},{6,7},{7,6},{8,9},{9,8},{10,11... | collective-permute-start | bytes 442376 | tf_op jit(solution)/shard_map/ppermute | solution.py:529
  383.2 32.5 %collective-permute-start.45 = (bf16[2,96,1536]{2,1,0:T(8,128)(2,1)S(1)}, bf16[2,96,1536]{2,1,0:T(8,128)(2,1)S(1)}, u32[]{:S(2)}, u32[]{:S(2)}) collective-permute-start(bf16[2,96,1536]{2,1,0:T(8,128)(2,1)S(1)} %slice.573), channel_id=1, source_target_pairs={{0,2},{1,3},{2,0},{3,1},{4,6},{5,7},{6,4},{7,5},{8,10},{9,11},{10,... | collective-permute-start | bytes 1769480 | tf_op jit(solution)/shard_map/ppermute | solution.py:529
  (65 other events, 600.0 us)
Sparse Core Ops, SparseCore 0:
  11.5 150.5 all-gather.1

commit v3 on v2

--- a/solution.py
+++ b/solution.py
@@ -256,11 +256,12 @@
 
 
 def attend_back_kernel(
-    seq, level, n_pieces, n_after,
+    seq, level, whole_order, n_pieces, n_after,
     info_ref, dh1_ref, x_ref, gain_ref, qkv_ref, lse_ref, oext_ref, sums_in, bup_in, *rest,
 ):
     pieces = rest[:n_pieces]
-    near_ref, far_ref, below_ref, small_ref, dext, dmix, dqkv, dqx, w, sems = rest[n_pieces + n_after :]
+    *outs, below_ref, small_ref = rest[n_pieces + n_after : -6]
+    dext, dmix, dqkv, dqx, w, sems = rest[-6:]
     copies = piece_copies(info_ref, pieces, 0, w, sems)
     start_all(copies)
     turn = info_ref[0]
@@ -315,11 +316,14 @@
         first = dot_nn(a1_t, part)
         second = dot_nn(hb_t, oext_ref[own])
         for j in range(8):
-            ref = near_ref if j % 2 == 0 else far_ref
             rows = slice(j * PIECE, (j + 1) * PIECE)
-            ref[j // 2, s, :, 0:512] = first[rows, 0:512].astype(BF)
-            ref[j // 2, s, :, 512:640] = (first[rows, 512:640] + second[rows, 0:128]).astype(BF)
-            ref[j // 2, s, :, 640:768] = second[rows, 128:256].astype(BF)
+            if whole_order:
+                ref = outs[0].at[own, jnp.bitwise_xor(info_ref[1], j)]
+            else:
+                ref = outs[j % 2].at[j // 2, s]
+            ref[:, 0:512] = first[rows, 0:512].astype(BF)
+            ref[:, 512:640] = (first[rows, 512:640] + second[rows, 0:128]).astype(BF)
+            ref[:, 640:768] = second[rows, 128:256].astype(BF)
     below, grad_gain = norm_back(da1, scaled, inverse, gain)
     below = below + dh1
     if level == 0:
@@ -447,14 +451,14 @@
     )(info, g, h1, a2, gains, z, slope, *pieces, *after)
 
 
-def attend_back(seq, level, info, dh1, x, gains, qkv, lse, oext, sums, bup, pieces, after):
-    grad = sds((4, BLOCKS, PIECE, D), BF)
+def attend_back(seq, level, whole_order, info, dh1, x, gains, qkv, lse, oext, sums, bup, pieces, after):
+    grads = [sds((BLOCKS, 8, PIECE, D), BF)] if whole_order else [sds((4, BLOCKS, PIECE, D), BF)] * 2
     below = sds((1, seq, D), F32) if level == 0 else sds((ROWS, D), F32)
     return pl.pallas_call(
-        functools.partial(attend_back_kernel, seq, level, len(pieces), len(after)),
-        out_shape=(grad, grad, below, sds((8, D), F32)),
+        functools.partial(attend_back_kernel, seq, level, whole_order, len(pieces), len(after)),
+        out_shape=(*grads, below, sds((8, D), F32)),
         in_specs=[SM] + [VM] * 8 + [HB] * (len(pieces) + len(after)),
-        out_specs=[VM] * 4,
+        out_specs=[VM] * (len(grads) + 2),
         scratch_shapes=[
             pltpu.VMEM((BLOCKS, ROWS, 256), BF), pltpu.VMEM((ROWS, D), BF),
             pltpu.VMEM((ROWS, 3 * D), BF), pltpu.VMEM((BLOCKS, ROWS, 640), BF),
@@ -500,8 +504,15 @@
         return jnp.concatenate(parts, axis=2).reshape(BLOCKS, 8, PIECE, -1)
 
     def reduce(self, near, far, widths, *earlier):
-        full = jnp.stack([near, far], axis=1).transpose(0, 1, 3, 2, 4)
-        full = full.reshape(D, BLOCKS, -1)
+        done = self.scatter(jnp.stack([near, far], axis=1).transpose(2, 0, 1, 3, 4), widths)
+        for _ in range(2):
+            yield done
+        yield done, done
+        yield done
+        yield done
+
+    def scatter(self, full, widths):
+        full = full.reshape(BLOCKS, D, -1).transpose(1, 0, 2)
         parts = []
         start = 0
         for width in widths:
@@ -510,12 +521,7 @@
             parts.append(part.transpose(1, 0, 2))
             start += wide
         packed = jnp.concatenate(parts, axis=2).reshape(self.n_col * D, sum(widths))
-        done = lax.psum_scatter(packed, ("col", "row"), scatter_dimension=0, tiled=True).astype(F32)
-        for _ in range(2):
-            yield done
-        yield done, done
-        yield done
-        yield done
+        return lax.psum_scatter(packed, ("col", "row"), scatter_dimension=0, tiled=True).astype(F32)
 
     def total(self, values, stages):
         return lax.psum(values, ("row", "col"))
@@ -569,10 +575,15 @@
         full = lax.all_gather(shard, ("col", "row"), axis=0, tiled=True)
         return full.reshape(BLOCKS, 8, PIECE, -1)
 
+    def scatter(self, full, widths):
+        full = full.reshape(BLOCKS * D, -1)
+        return lax.psum_scatter(full, ("col", "row"), scatter_dimension=0, tiled=True).astype(F32)
+
     def reduce(self, near, far, widths, *earlier):
         far = after(far, *earlier)
         other = flip_row(far, CORE)
         hold = yield other
+        other = after(other, *hold)
 
         def joined(m, blocks):
             return near[m, blocks].astype(F32) + other[m, blocks].astype(F32)
@@ -586,8 +597,9 @@
         from_x = flip_row(after(to_x.astype(BF), *hold), NEXT_X)
         from_y = flip_row(after(to_y.astype(BF), *hold), NEXT_Y)
         hold = yield from_x, from_y
+        from_x, from_y = after(from_x, from_y, *hold), after(from_y, from_x, *hold)
         plane = joined(0, every) + from_x.astype(F32) + from_y.astype(F32)
-        others = flip_col(after(plane[2:4].astype(BF), *hold), 2)
+        others = flip_col(plane[2:4].astype(BF), 2)
         hold = yield others
         pair = plane[0:2] + after(others, *hold).astype(F32)
         yield pair[0] + flip_col(pair[1].astype(BF), 1).astype(F32)
@@ -645,18 +657,22 @@
         fetches = [RelativeFetch(shard) for shard in shards[0]]
         one = fetches[0].turn_one()
         two = fetches[0].turn_two()
-        plane, arrived = (), []
+        plane, ran, arrived = (), (), []
         for index, fetch in enumerate(fetches):
             plane = (fetch.plane(*plane),)
             if index + 1 < len(fetches):
                 one = fetches[index + 1].turn_one(one)
                 two = fetches[index + 1].turn_two(two)
-            arrived.append(fetch.rest(two))
-        sooner = arrived[0], arrived[1] + arrived[2]
+            if index == 2:
+                state = forward_attend(0, hidden, arrived[0])
+                ran = (state[1],)
+            arrived.append(fetch.rest(two, *ran))
+            ran = (gains,)
+        sooner = arrived[1] + arrived[2]
     else:
-        sooner = (gathered(0),) * 2
-    state = forward_attend(0, hidden, sooner[0])
-    middle = forward_feed(0, hidden, state, sooner[1])
+        sooner = gathered(0)
+        state = forward_attend(0, hidden, sooner)
+    middle = forward_feed(0, hidden, state, sooner)
     state = forward_attend(1, middle, later)
     hidden = forward_feed(1, middle, state, later)
     smalls = [None] * LAYERS
@@ -668,36 +684,29 @@
     def backward_attend(level, dh1, sums, bup_sum, landed):
         below, qkv, lse, oext, h1, a2, z, slope = saved[level]
         return attend_back(
-            seq, level, info, dh1, below, gains, qkv, lse, oext, sums, bup_sum, att_full[level], landed
+            seq, level, level == 1, info, dh1, below, gains, qkv, lse, oext, sums, bup_sum, att_full[level], landed
         )
 
+    done = {}
     near, far, bup_sum, dh1, sums = backward_feed(1, upstream, [])
     ffn_one = plan.reduce(near, far, ffn_widths)
-    core_ffn_one = next(ffn_one)
-    near, far, upstream, smalls[1] = backward_attend(1, dh1, sums, bup_sum, [])
-    one_near, one_far = near, far
-    near, far, bup_sum, dh1, sums = backward_feed(0, upstream, [core_ffn_one])
-    diag_ffn_one = ffn_one.send(())
-    zero_near, zero_far = near, far
-    near, far, upstream, smalls[0] = backward_attend(0, dh1, sums, bup_sum, [*diag_ffn_one])
-    plane_ffn_one = ffn_one.send(())
-    att_one = plan.reduce(one_near, one_far, att_widths, smalls[0])
-    core_att_one = next(att_one)
-    ffn_zero = plan.reduce(zero_near, zero_far, ffn_widths, smalls[0], core_att_one)
-    core_ffn_zero = next(ffn_zero)
-    att_zero = plan.reduce(near, far, att_widths, core_ffn_zero)
-    core_att_zero = next(att_zero)
-    diag_att_one = att_one.send(diag_ffn_one)
-    plane_att_one = att_one.send(())
-    diag_ffn_zero = ffn_zero.send(plane_ffn_one)
-    plane_ffn_zero = ffn_zero.send(())
-    diag_att_zero = att_zero.send(plane_att_one)
-    plane_att_zero = att_zero.send(())
-    turn_ffn_one, turn_att_one = ffn_one.send((smalls[0],)), att_one.send(())
-    turn_ffn_zero, turn_att_zero = ffn_zero.send(()), att_zero.send(())
-    done = {}
-    done["ffn", 1], done["att", 1] = ffn_one.send(diag_ffn_zero), att_one.send(plane_ffn_zero)
-    done["ffn", 0], done["att", 0] = ffn_zero.send(plane_att_zero), att_zero.send(())
+    core_one = next(ffn_one)
+    whole_one, upstream, smalls[1] = backward_attend(1, dh1, sums, bup_sum, [])
+    done["att", 1] = plan.scatter(whole_one, att_widths)
+    diag_one = ffn_one.send(())
+    near, far, bup_sum, dh1, sums = backward_feed(0, upstream, [*diag_one])
+    plane_one = ffn_one.send(())
+    ffn_zero = plan.reduce(near, far, ffn_widths)
+    core_zero = next(ffn_zero)
+    near, far, upstream, smalls[0] = backward_attend(0, dh1, sums, bup_sum, [])
+    att_zero = plan.reduce(near, far, att_widths, core_zero)
+    core_last = next(att_zero)
+    diag_zero = ffn_zero.send((smalls[0],))
+    plane_zero = ffn_zero.send(())
+    diag_last = att_zero.send(diag_zero)
+    plane_last = att_zero.send(())
+    turn_one, turn_zero, turn_last = ffn_one.send((smalls[0],)), ffn_zero.send(diag_last), att_zero.send(())
+    done["ffn", 1], done["ffn", 0], done["att", 0] = ffn_one.send(diag_zero), ffn_zero.send(plane_last), att_zero.send(())
     layer_out = finish(seq, info, counts, hidden, [upstream])
     grads = []
     for level in range(LAYERS):
@@ -705,7 +714,7 @@
         grads.append((
             att[:, : att_widths[0]], att[:, att_widths[0] :].T, ffn[:, : ffn_widths[0]], ffn[:, ffn_widths[0] :].T
         ))
-    stages = [plane_ffn_one, diag_att_one, plane_att_one, diag_ffn_zero, plane_ffn_zero]
+    stages = [diag_zero, diag_zero, plane_zero, plane_zero, diag_last]
     small = plan.total(jnp.concatenate(smalls, axis=0), stages).reshape(LAYERS, 8, D)
     grad_list = [jnp.stack([grads[level][index] for level in range(LAYERS)]) for index in range(4)]
     grad_list += [small[:, 0:2], small[:, 2:4], small[:, 4:8].reshape(LAYERS, FF)]

time: 451 us -> 489 us (1.084)
  waiting for transfers between devices: 194 us -> 253 us
  starting transfers between devices: 75.7 us -> 54.1 us
  other arithmetic: 36.5 us -> 30.8 us
  local copies, waits for them, and re-layouts: 28.6 us -> 34.2 us
    reduce_scatter x0 -> x1, waiting for transfers between devices: none -> 38.4 us  [scatter(): lax.psum_scatter(full, ('col', 'row'), scatter_dimension=0, tiled=True)]
    ppermute x16 -> x14, waiting for transfers between devices: 96 us -> 121 us  [flip_col(): return lax.ppermute(x, 'col', [(i, i ^ mask) for i in range(4)])]
    ppermute x16 -> x14, starting transfers between devices: 42.4 us -> 20 us  [flip_col(): return lax.ppermute(x, 'col', [(i, i ^ mask) for i in range(4)])]
    ppermute x38 -> x33, waiting for transfers between devices: 98.2 us -> 93.4 us  [flip_row(): return lax.ppermute(x, 'row', [(i, i ^ mask) for i in range(8)])]
    unnamed x110 -> x116, local copies, waits for them, and re-layouts: 22.2 us -> 25.3 us
    ppermute x38 -> x33, starting transfers between devices: 33.2 us -> 34.1 us  [flip_row(): return lax.ppermute(x, 'row', [(i, i ^ mask) for i in range(8)])]
  transfers between devices with their start and end apart: 55 -> 49, of which waited for: 23 -> 25; matrix products, arithmetic and copies ran while one was open for 11% -> 11% of each run, Pallas kernels for 11% -> 13%
where the time goes in v3:
time: 489 us; the launch traced here: 481 us
  waiting for transfers between devices  253 us (52%)
  Pallas kernels  93.4 us (19%)
  starting transfers between devices  54.1 us (11%)
  local copies, waits for them, and re-layouts  34.2 us (7%)
  other arithmetic  30.8 us (6%)
  between operations  15.4 us (3%)
    ppermute x14, waiting for transfers between devices, flip_col(): return lax.ppermute(x, 'col', [(i, i ^ mask) for i in range(4)])  121 us
    ppermute x33, waiting for transfers between devices, flip_row(): return lax.ppermute(x, 'row', [(i, i ^ mask) for i in range(8)])  93.4 us
    reduce_scatter x1, waiting for transfers between devices, scatter(): lax.psum_scatter(full, ('col', 'row'), scatter_dimension=0, tiled=True)  38.4 us
    ppermute x33, starting transfers between devices, flip_row(): return lax.ppermute(x, 'row', [(i, i ^ mask) for i in range(8)])  34.1 us
    pallas_call x2, Pallas kernels, attend_back(): pl.pallas_call(functools.partial(attend_back_kernel, seq, level, whole_or...  27.6 us
    pallas_call x2, Pallas kernels, feed_back(): pl.pallas_call(functools.partial(feed_back_kernel, level, len(pieces), le...  25.9 us
    unnamed x116, local copies, waits for them, and re-layouts  25.3 us
    ppermute x14, starting transfers between devices, flip_col(): return lax.ppermute(x, 'col', [(i, i ^ mask) for i in range(4)])  20 us
  transfers between devices with their start and end apart: 49, of which 25 were waited for; matrix products, arithmetic and copies ran while one was open for 11% of the time, Pallas kernels for 13%

profile of v3, /device:TPU:0, one launch (start us, length us, event | category | flops | bytes accessed | tf_op | source)
XLA Modules:
  0.0 481.2 jit_solution(12149161532627967528)
XLA Ops:
  10.8 3.1 collective-permute-start
  13.9 3.8 collective-permute-done
  20.6 22.1 %collective-permute-done.1 = bf16[2,96,768]{2,1,0:T(8,128)(2,1)S(1)} collective-permute-done((bf16[2,96,768]{2,1,0:T(8,128)(2,1)S(1)}, bf16[2,96,768]{2,1,0:T(8,128)(2,1)S(1)}, u32[]{:S(2)}, u32[]{:S(2)}) %collective-permute-start.1) | collective-permute-done | bytes 294944 | tf_op jit(solution)/shard_map/ppermute | solution.py:535
  46.4 8.2 %collective-permute-done.4 = bf16[96,768]{1,0:T(8,128)(2,1)S(1)} collective-permute-done((bf16[96,768]{1,0:T(8,128)(2,1)S(1)}, bf16[96,768]{1,0:T(8,128)(2,1)S(1)}, u32[]{:S(2)}, u32[]{:S(2)}) %collective-permute-start.4) | collective-permute-done | bytes 147488 | tf_op jit(solution)/shard_map/ppermute | solution.py:535
  54.6 5.2 %collective-permute-start.5 = (bf16[2,96,768]{2,1,0:T(8,128)(2,1)S(1)}, bf16[2,96,768]{2,1,0:T(8,128)(2,1)S(1)}, u32[]{:S(2)}, u32[]{:S(2)}) collective-permute-start(bf16[2,96,768]{2,1,0:T(8,128)(2,1)S(1)} %pad_maximum_fusion.13), channel_id=1, source_target_pairs={{0,2},{1,3},{2,0},{3,1},{4,6},{5,7},{6,4},{7,5},{8,10},{9,11},{10,... | collective-permute-start | bytes 884744 | tf_op jit(solution)/shard_map/ppermute | solution.py:535
  59.8 22.9 %collective-permute-done.5 = bf16[2,96,768]{2,1,0:T(8,128)(2,1)S(1)} collective-permute-done((bf16[2,96,768]{2,1,0:T(8,128)(2,1)S(1)}, bf16[2,96,768]{2,1,0:T(8,128)(2,1)S(1)}, u32[]{:S(2)}, u32[]{:S(2)}) %collective-permute-start.5) | collective-permute-done | bytes 294944 | tf_op jit(solution)/shard_map/ppermute | solution.py:535
  83.1 6.5 %collective-permute-done.6 = bf16[2,96,768]{2,1,0:T(8,128)(2,1)S(1)} collective-permute-done((bf16[2,96,768]{2,1,0:T(8,128)(2,1)S(1)}, bf16[2,96,768]{2,1,0:T(8,128)(2,1)S(1)}, u32[]{:S(2)}, u32[]{:S(2)}) %collective-permute-start.6) | collective-permute-done | bytes 294944 | tf_op jit(solution)/shard_map/ppermute | solution.py:531
  92.9 15.0 %collective-permute-done.11 = bf16[96,768]{1,0:T(8,128)(2,1)S(1)} collective-permute-done((bf16[96,768]{1,0:T(8,128)(2,1)S(1)}, bf16[96,768]{1,0:T(8,128)(2,1)S(1)}, u32[]{:S(2)}, u32[]{:S(2)}) %collective-permute-start.11) | collective-permute-done | bytes 147488 | tf_op jit(solution)/shard_map/ppermute | solution.py:535
  115.0 3.3 prepare.1
  118.3 13.1 %collective-permute-done.12 = bf16[2,96,768]{2,1,0:T(8,128)(2,1)} collective-permute-done((bf16[2,96,768]{2,1,0:T(8,128)(2,1)S(1)}, bf16[2,96,768]{2,1,0:T(8,128)(2,1)}, u32[]{:S(2)}, u32[]{:S(2)}) %collective-permute-start.12) | collective-permute-done | bytes 294944 | tf_op jit(solution)/shard_map/ppermute | solution.py:535
  134.1 3.7 collective-permute-start.17
  143.1 11.0 %collective-permute-done.13 = bf16[2,96,768]{2,1,0:T(8,128)(2,1)S(1)} collective-permute-done((bf16[2,96,768]{2,1,0:T(8,128)(2,1)S(1)}, bf16[2,96,768]{2,1,0:T(8,128)(2,1)S(1)}, u32[]{:S(2)}, u32[]{:S(2)}) %collective-permute-start.13) | collective-permute-done | bytes 294944 | tf_op jit(solution)/shard_map/ppermute | solution.py:531
  155.5 8.5 %attend.2 = (bf16[208,2304]{1,0:T(8,128)(2,1)}, f32[16,208]{1,0:T(8,128)}, bf16[4,208,256]{2,1,0:T(8,128)(2,1)}, f32[208,768]{1,0:T(8,128)}, bf16[208,768]{1,0:T(8,128)(2,1)}) custom-call(s32[4]{0:T(128)} %pad_add_fusion.info_ref, f32[208,768]{1,0:T(8,128)} %get-tuple-element.97.x_ref, f32[4,768]{1,0:T(4,128)} %get-tuple-element.98.gain_ref, ...), custom_call_target="tpu_custom_call" | custom-call | flops 10000000 | bytes 100000 | tf_op jit(solution)/shard_map/attend/pallas_call | solution.py:391
  168.3 3.4 collective-permute-start.19
  173.9 5.4 %collective-permute-done.19 = bf16[2,96,768]{2,1,0:T(8,128)(2,1)S(1)} collective-permute-done((bf16[2,96,768]{2,1,0:T(8,128)(2,1)S(1)}, bf16[2,96,768]{2,1,0:T(8,128)(2,1)S(1)}, u32[]{:S(2)}, u32[]{:S(2)}) %collective-permute-start.19) | collective-permute-done | bytes 294944 | tf_op jit(solution)/shard_map/ppermute | solution.py:531
  179.5 4.5 collective-permute-done.20.rest_3_
  185.4 9.0 %feed.2 = (bf16[4,208,768]{2,1,0:T(8,128)(2,1)}, f32[4,208,768]{2,1,0:T(8,128)}, f32[208,768]{1,0:T(8,128)}) custom-call(s32[4]{0:T(128)} %pad_add_fusion.info_ref, f32[208,768]{1,0:T(8,128)} %get-tuple-element.104.h1_ref, bf16[208,768]{1,0:T(8,128)(2,1)} %get-tuple-element.105.a2_ref, f32[4,768]{1,0:T(4,128)} %get-tuple-element.99.bias_ref, ...), custom_call_target="tpu_custom_call" | custom-call | flops 10000000 | bytes 100000 | tf_op jit(solution)/shard_map/feed/pallas_call | solution.py:411
  194.4 7.9 %attend.3 = (bf16[208,2304]{1,0:T(8,128)(2,1)}, f32[16,208]{1,0:T(8,128)}, bf16[4,208,256]{2,1,0:T(8,128)(2,1)}, f32[208,768]{1,0:T(8,128)}, bf16[208,768]{1,0:T(8,128)(2,1)}) custom-call(s32[4]{0:T(128)} %pad_add_fusion.info_ref, f32[208,768]{1,0:T(8,128)} %get-tuple-element.116.x_ref, f32[4,768]{1,0:T(4,128)} %get-tuple-element.98.gain_ref, ...), custom_call_target="tpu_custom_call" | custom-call | flops 10000000 | bytes 100000 | tf_op jit(solution)/shard_map/attend/pallas_call | solution.py:391
  202.3 8.6 %feed.3 = (bf16[4,208,768]{2,1,0:T(8,128)(2,1)}, f32[4,208,768]{2,1,0:T(8,128)}, f32[208,768]{1,0:T(8,128)}) custom-call(s32[4]{0:T(128)} %pad_add_fusion.info_ref, f32[208,768]{1,0:T(8,128)} %get-tuple-element.117.h1_ref, bf16[208,768]{1,0:T(8,128)(2,1)} %get-tuple-element.118.a2_ref, f32[4,768]{1,0:T(4,128)} %get-tuple-element.99.bias_ref, ...), custom_call_target="tpu_custom_call" | custom-call | flops 10000000 | bytes 100000 | tf_op jit(solution)/shard_map/feed/pallas_call | solution.py:411
  211.0 12.9 %feed_back.2 = (bf16[4,4,96,1536]{3,2,1,0:T(8,128)(2,1)}, bf16[4,4,96,1536]{3,2,1,0:T(8,128)(2,1)}, f32[4,1,768]{2,1,0:T(1,128)}, f32[208,768]{1,0:T(8,128)}, f32[8,768]{1,0:T(8,128)}) custom-call(s32[4]{0:T(128)} %pad_add_fusion.info_ref, f32[208,768]{1,0:T(8,128)} %get-tuple-element.120.g_ref, f32[208,768]{1,0:T(8,128)} %get-tuple-element.117.h1_ref, ...), custom_call_target="tpu_custom_call" | custom-call | flops 10000000 | bytes 100000 | tf_op jit(solution)/shard_map/feed_back/pallas_call | solution.py:436
  224.1 13.8 %attend_back.2 = (bf16[4,8,96,768]{3,2,1,0:T(8,128)(2,1)}, f32[208,768]{1,0:T(8,128)}, f32[8,768]{1,0:T(8,128)}) custom-call(s32[4]{0:T(128)} %pad_add_fusion.info_ref, f32[208,768]{1,0:T(8,128)} %get-tuple-element.123.dh1_ref, f32[208,768]{1,0:T(8,128)} %get-tuple-element.116.x_ref, f32[4,768]{1,0:T(4,128)} %get-tuple-element.98.gain_ref, ...), custom_call_target="tpu_custom_call" | custom-call | flops 10000000 | bytes 100000 | tf_op jit(solution)/shard_map/attend_back/pallas_call | solution.py:457
  242.9 13.6 %collective-permute-done.22.rest_4_ = bf16[2,96,1536]{2,1,0:T(8,128)(2,1)S(1)} collective-permute-done((bf16[2,96,1536]{2,1,0:T(8,128)(2,1)S(1)}, bf16[2,96,1536]{2,1,0:T(8,128)(2,1)S(1)}, u32[]{:S(2)}, u32[]{:S(2)}) %collective-permute-start.22) | collective-permute-done | bytes 589856 | tf_op jit(solution)/shard_map/ppermute | solution.py:531
  257.5 12.9 %feed_back.3 = (bf16[4,4,96,1536]{3,2,1,0:T(8,128)(2,1)}, bf16[4,4,96,1536]{3,2,1,0:T(8,128)(2,1)}, f32[4,1,768]{2,1,0:T(1,128)}, f32[208,768]{1,0:T(8,128)}, f32[8,768]{1,0:T(8,128)}) custom-call(s32[4]{0:T(128)} %pad_add_fusion.info_ref, f32[208,768]{1,0:T(8,128)} %get-tuple-element.129.g_ref, f32[208,768]{1,0:T(8,128)} %get-tuple-element.104.h1_ref, ...), custom_call_target="tpu_custom_call" | custom-call | flops 10000000 | bytes 100000 | tf_op jit(solution)/shard_map/feed_back/pallas_call | solution.py:436
  277.6 13.8 %attend_back.3 = (bf16[4,4,96,768]{3,2,1,0:T(8,128)(2,1)}, bf16[4,4,96,768]{3,2,1,0:T(8,128)(2,1)}, f32[1,197,768]{2,1,0:T(8,128)}, f32[8,768]{1,0:T(8,128)}) custom-call(s32[4]{0:T(128)} %pad_add_fusion.info_ref, f32[208,768]{1,0:T(8,128)} %get-tuple-element.134.dh1_ref, f32[208,768]{1,0:T(8,128)} %get-tuple-element.97.x_ref, ...), custom_call_target="tpu_custom_call" | custom-call | flops 10000000 | bytes 100000 | tf_op jit(solution)/shard_map/attend_back/pallas_call | solution.py:457
  291.5 18.6 %collective-permute-done.39 = bf16[4,96,1536]{2,1,0:T(8,128)(2,1)S(1)} collective-permute-done((bf16[4,96,1536]{2,1,0:T(8,128)(2,1)S(1)}, bf16[4,96,1536]{2,1,0:T(8,128)(2,1)S(1)}, u32[]{:S(2)}, u32[]{:S(2)}) %collective-permute-start.39) | collective-permute-done | bytes 1179680 | tf_op jit(solution)/shard_map/ppermute | solution.py:531
  317.4 3.5 fusion.13
  330.8 38.4 %reduce-scatter.2.cloned.1.call-done = bf16[96,768]{1,0:T(8,128)(2,1)} async-done(((bf16[3072,768]{1,0:T(8,128)(2,1)}), bf16[96,768]{1,0:T(8,128)(2,1)}) %reduce-scatter.2.cloned.1.call-update) | async-done | bytes 147472 | tf_op jit(solution)/shard_map/reduce_scatter | solution.py:580
  379.8 24.2 %collective-permute-done.43 = f32[16,768]{1,0:T(8,128)S(1)} collective-permute-done((f32[16,768]{1,0:T(8,128)S(1)}, f32[16,768]{1,0:T(8,128)S(1)}, u32[]{:S(2)}, u32[]{:S(2)}) %collective-permute-start.43) | collective-permute-done | bytes 49184 | tf_op jit(solution)/shard_map/ppermute | solution.py:531
  423.5 5.5 %collective-permute-done.31 = bf16[4,96,768]{2,1,0:T(8,128)(2,1)S(1)} collective-permute-done((bf16[4,96,768]{2,1,0:T(8,128)(2,1)S(1)}, bf16[4,96,768]{2,1,0:T(8,128)(2,1)S(1)}, u32[]{:S(2)}, u32[]{:S(2)}) %collective-permute-start.31) | collective-permute-done | bytes 589856 | tf_op jit(solution)/shard_map/ppermute | solution.py:531
  431.2 22.5 %collective-permute-done.36 = bf16[2,96,1536]{2,1,0:T(8,128)(2,1)S(1)} collective-permute-done((bf16[2,96,1536]{2,1,0:T(8,128)(2,1)S(1)}, bf16[2,96,1536]{2,1,0:T(8,128)(2,1)S(1)}, u32[]{:S(2)}, u32[]{:S(2)}) %collective-permute-start.36) | collective-permute-done | bytes 589856 | tf_op jit(solution)/shard_map/ppermute | solution.py:535
  454.0 4.9 %collective-permute-done.32 = bf16[2,96,768]{2,1,0:T(8,128)(2,1)S(1)} collective-permute-done((bf16[2,96,768]{2,1,0:T(8,128)(2,1)S(1)}, bf16[2,96,768]{2,1,0:T(8,128)(2,1)S(1)}, u32[]{:S(2)}, u32[]{:S(2)}) %collective-permute-start.32) | collective-permute-done | bytes 294944 | tf_op jit(solution)/shard_map/ppermute | solution.py:535
  459.1 6.1 %collective-permute-done.37 = bf16[96,1536]{1,0:T(8,128)(2,1)S(1)} collective-permute-done((bf16[96,1536]{1,0:T(8,128)(2,1)S(1)}, bf16[96,1536]{1,0:T(8,128)(2,1)S(1)}, u32[]{:S(2)}, u32[]{:S(2)}) %collective-permute-start.37) | collective-permute-done | bytes 294944 | tf_op jit(solution)/shard_map/ppermute | solution.py:535
  (271 shorter events, 109.7 us)
Async XLA Ops:
  7.2 187.2 %all-gather.2.cloned.1.call-start = ((), (), s32[]{:S(2)}) async-start(), calls=%async_computation.1 | async-start | bytes 14598144 | tf_op jit(solution)/shard_map/all_gather | solution.py:575
  10.7 358.5 %reduce-scatter.2.cloned.1.call-start = ((), (), s32[]{:S(2)}) async-start(), calls=%async_computation.2 | async-start | bytes 4866048 | tf_op jit(solution)/shard_map/reduce_scatter | solution.py:580
  17.8 25.0 %collective-permute-start.1 = (bf16[2,96,768]{2,1,0:T(8,128)(2,1)S(1)}, bf16[2,96,768]{2,1,0:T(8,128)(2,1)S(1)}, u32[]{:S(2)}, u32[]{:S(2)}) collective-permute-start(bf16[2,96,768]{2,1,0:T(8,128)(2,1)S(1)} %pad_maximum_fusion.12), channel_id=1, source_target_pairs={{0,2},{1,3},{2,0},{3,1},{4,6},{5,7},{6,4},{7,5},{8,10},{9,11},{10,... | collective-permute-start | bytes 884744 | tf_op jit(solution)/shard_map/ppermute | solution.py:535
  42.8 40.0 %collective-permute-start.2 = (bf16[4,96,768]{2,1,0:T(8,128)(2,1)S(1)}, bf16[4,96,768]{2,1,0:T(8,128)(2,1)S(1)}, u32[]{:S(2)}, u32[]{:S(2)}) collective-permute-start(bf16[4,96,768]{2,1,0:T(8,128)(2,1)S(1)} %pad_maximum_fusion.4), channel_id=1, source_target_pairs={{0,8},{4,12},{8,0},{12,4},{16,24},{20,28},{24,16},{28,20},{1,9},{5... | collective-permute-start | bytes 1769480 | tf_op jit(solution)/shard_map/ppermute | solution.py:531
  44.2 38.6 %collective-permute-start.3 = (bf16[4,96,768]{2,1,0:T(8,128)(2,1)S(1)}, bf16[4,96,768]{2,1,0:T(8,128)(2,1)S(1)}, u32[]{:S(2)}, u32[]{:S(2)}) collective-permute-start(bf16[4,96,768]{2,1,0:T(8,128)(2,1)S(1)} %pad_maximum_fusion.4), channel_id=1, source_target_pairs={{0,16},{4,20},{8,24},{12,28},{16,0},{20,4},{24,8},{28,12},{1,17},{... | collective-permute-start | bytes 1769480 | tf_op jit(solution)/shard_map/ppermute | solution.py:531
  54.6 28.1 %collective-permute-start.5 = (bf16[2,96,768]{2,1,0:T(8,128)(2,1)S(1)}, bf16[2,96,768]{2,1,0:T(8,128)(2,1)S(1)}, u32[]{:S(2)}, u32[]{:S(2)}) collective-permute-start(bf16[2,96,768]{2,1,0:T(8,128)(2,1)S(1)} %pad_maximum_fusion.13), channel_id=1, source_target_pairs={{0,2},{1,3},{2,0},{3,1},{4,6},{5,7},{6,4},{7,5},{8,10},{9,11},{10,... | collective-permute-start | bytes 884744 | tf_op jit(solution)/shard_map/ppermute | solution.py:535
  89.7 64.4 %collective-permute-start.8 = (bf16[4,4,96,768]{3,2,1,0:T(8,128)(2,1)S(1)}, bf16[4,4,96,768]{3,2,1,0:T(8,128)(2,1)}, u32[]{:S(2)}, u32[]{:S(2)}) collective-permute-start(bf16[4,4,96,768]{3,2,1,0:T(8,128)(2,1)S(1)} %bitcast.148), channel_id=1, source_target_pairs={{0,4},{4,0},{8,12},{12,8},{16,20},{20,16},{24,28},{28,24},{1,5},{5... | collective-permute-start | bytes 7077896 | tf_op jit(solution)/shard_map/ppermute | solution.py:531
  89.8 18.1 %collective-permute-start.11 = (bf16[96,768]{1,0:T(8,128)(2,1)S(1)}, bf16[96,768]{1,0:T(8,128)(2,1)S(1)}, u32[]{:S(2)}, u32[]{:S(2)}) collective-permute-start(bf16[96,768]{1,0:T(8,128)(2,1)S(1)} %get-tuple-element.108), channel_id=1, source_target_pairs={{0,1},{1,0},{2,3},{3,2},{4,5},{5,4},{6,7},{7,6},{8,9},{9,8},{10,11... | collective-permute-start | bytes 442376 | tf_op jit(solution)/shard_map/ppermute | solution.py:535
  90.0 42.6 %collective-permute-start.9 = (bf16[4,96,768]{2,1,0:T(8,128)(2,1)S(1)}, bf16[4,96,768]{2,1,0:T(8,128)(2,1)}, u32[]{:S(2)}, u32[]{:S(2)}) collective-permute-start(bf16[4,96,768]{2,1,0:T(8,128)(2,1)S(1)} %pad_maximum_fusion.5), channel_id=1, source_target_pairs={{0,8},{4,12},{8,0},{12,4},{16,24},{20,28},{24,16},{28,20},{1,9},{5... | collective-permute-start | bytes 1769480 | tf_op jit(solution)/shard_map/ppermute | solution.py:531
  92.9 45.0 %collective-permute-start.10 = (bf16[4,96,768]{2,1,0:T(8,128)(2,1)S(1)}, bf16[4,96,768]{2,1,0:T(8,128)(2,1)}, u32[]{:S(2)}, u32[]{:S(2)}) collective-permute-start(bf16[4,96,768]{2,1,0:T(8,128)(2,1)S(1)} %pad_maximum_fusion.5), channel_id=1, source_target_pairs={{0,16},{4,20},{8,24},{12,28},{16,0},{20,4},{24,8},{28,12},{1,17},{... | collective-permute-start | bytes 1769480 | tf_op jit(solution)/shard_map/ppermute | solution.py:531
  108.6 22.8 %collective-permute-start.12 = (bf16[2,96,768]{2,1,0:T(8,128)(2,1)S(1)}, bf16[2,96,768]{2,1,0:T(8,128)(2,1)}, u32[]{:S(2)}, u32[]{:S(2)}) collective-permute-start(bf16[2,96,768]{2,1,0:T(8,128)(2,1)S(1)} %pad_maximum_fusion.14), channel_id=1, source_target_pairs={{0,2},{1,3},{2,0},{3,1},{4,6},{5,7},{6,4},{7,5},{8,10},{9,11},{10,... | collective-permute-start | bytes 884744 | tf_op jit(solution)/shard_map/ppermute | solution.py:535
  132.6 31.5 %collective-permute-start.16 = (bf16[4,96,768]{2,1,0:T(8,128)(2,1)S(1)}, bf16[4,96,768]{2,1,0:T(8,128)(2,1)}, u32[]{:S(2)}, u32[]{:S(2)}) collective-permute-start(bf16[4,96,768]{2,1,0:T(8,128)(2,1)S(1)} %pad_maximum_fusion.6), channel_id=1, source_target_pairs={{0,8},{4,12},{8,0},{12,4},{16,24},{20,28},{24,16},{28,20},{1,9},{5... | collective-permute-start | bytes 1769480 | tf_op jit(solution)/shard_map/ppermute | solution.py:531
  134.1 30.0 %collective-permute-start.17 = (bf16[4,96,768]{2,1,0:T(8,128)(2,1)S(1)}, bf16[4,96,768]{2,1,0:T(8,128)(2,1)}, u32[]{:S(2)}, u32[]{:S(2)}) collective-permute-start(bf16[4,96,768]{2,1,0:T(8,128)(2,1)S(1)} %pad_maximum_fusion.6), channel_id=1, source_target_pairs={{0,16},{4,20},{8,24},{12,28},{16,0},{20,4},{24,8},{28,12},{1,17},{... | collective-permute-start | bytes 1769480 | tf_op jit(solution)/shard_map/ppermute | solution.py:531
  138.8 15.3 %collective-permute-start.13 = (bf16[2,96,768]{2,1,0:T(8,128)(2,1)S(1)}, bf16[2,96,768]{2,1,0:T(8,128)(2,1)S(1)}, u32[]{:S(2)}, u32[]{:S(2)}) collective-permute-start(bf16[2,96,768]{2,1,0:T(8,128)(2,1)S(1)} %slice.257), channel_id=1, source_target_pairs={{0,8},{4,12},{8,0},{12,4},{16,24},{20,28},{24,16},{28,20},{1,9},{5... | collective-permute-start | bytes 884744 | tf_op jit(solution)/shard_map/ppermute | solution.py:531
  140.8 25.7 %collective-permute-start.14 = (bf16[2,96,768]{2,1,0:T(8,128)(2,1)S(1)}, bf16[2,96,768]{2,1,0:T(8,128)(2,1)S(1)}, u32[]{:S(2)}, u32[]{:S(2)}) collective-permute-start(bf16[2,96,768]{2,1,0:T(8,128)(2,1)S(1)} %slice.258), channel_id=1, source_target_pairs={{0,16},{4,20},{8,24},{12,28},{16,0},{20,4},{24,8},{28,12},{1,17},{... | collective-permute-start | bytes 884744 | tf_op jit(solution)/shard_map/ppermute | solution.py:531
  240.9 15.7 %collective-permute-start.22 = (bf16[2,96,1536]{2,1,0:T(8,128)(2,1)S(1)}, bf16[2,96,1536]{2,1,0:T(8,128)(2,1)S(1)}, u32[]{:S(2)}, u32[]{:S(2)}) collective-permute-start(bf16[2,96,1536]{2,1,0:T(8,128)(2,1)S(1)} %get-tuple-element.222), channel_id=1, source_target_pairs={{0,8},{4,12},{8,0},{12,4},{16,24},{20,28},{24,16},{28,20},{1,9},{5... | collective-permute-start | bytes 1769480 | tf_op jit(solution)/shard_map/ppermute | solution.py:531
  241.2 15.4 %collective-permute-start.23 = (bf16[2,96,1536]{2,1,0:T(8,128)(2,1)S(1)}, bf16[2,96,1536]{2,1,0:T(8,128)(2,1)S(1)}, u32[]{:S(2)}, u32[]{:S(2)}) collective-permute-start(bf16[2,96,1536]{2,1,0:T(8,128)(2,1)S(1)} %get-tuple-element.221), channel_id=1, source_target_pairs={{0,16},{4,20},{8,24},{12,28},{16,0},{20,4},{24,8},{28,12},{1,17},{... | collective-permute-start | bytes 1769480 | tf_op jit(solution)/shard_map/ppermute | solution.py:531
  270.5 46.9 %collective-permute-start.24 = (bf16[4,4,96,1536]{3,2,1,0:T(8,128)(2,1)}, bf16[4,4,96,1536]{3,2,1,0:T(8,128)(2,1)}, u32[]{:S(2)}, u32[]{:S(2)}) collective-permute-start(bf16[4,4,96,1536]{3,2,1,0:T(8,128)(2,1)} %get-tuple-element.142), channel_id=1, source_target_pairs={{0,4},{4,0},{8,12},{12,8},{16,20},{20,16},{24,28},{28,24},{1,5},{5... | collective-permute-start | bytes 14155784 | tf_op jit(solution)/shard_map/ppermute | solution.py:531
  273.2 36.9 %collective-permute-start.39 = (bf16[4,96,1536]{2,1,0:T(8,128)(2,1)S(1)}, bf16[4,96,1536]{2,1,0:T(8,128)(2,1)S(1)}, u32[]{:S(2)}, u32[]{:S(2)}) collective-permute-start(bf16[4,96,1536]{2,1,0:T(8,128)(2,1)S(1)} %pad_maximum_fusion.3), channel_id=1, source_target_pairs={{0,16},{4,20},{8,24},{12,28},{16,0},{20,4},{24,8},{28,12},{1,17},{... | collective-permute-start | bytes 3538952 | tf_op jit(solution)/shard_map/ppermute | solution.py:531
  276.0 36.7 %collective-permute-start.38 = (bf16[4,96,1536]{2,1,0:T(8,128)(2,1)}, bf16[4,96,1536]{2,1,0:T(8,128)(2,1)S(1)}, u32[]{:S(2)}, u32[]{:S(2)}) collective-permute-start(bf16[4,96,1536]{2,1,0:T(8,128)(2,1)} %pad_maximum_fusion.2), channel_id=1, source_target_pairs={{0,8},{4,12},{8,0},{12,4},{16,24},{20,28},{24,16},{28,20},{1,9},{5... | collective-permute-start | bytes 3538952 | tf_op jit(solution)/shard_map/ppermute | solution.py:531
  317.4 53.1 %collective-permute-start.40 = (bf16[2,96,1536]{2,1,0:T(8,128)(2,1)}, bf16[2,96,1536]{2,1,0:T(8,128)(2,1)}, u32[]{:S(2)}, u32[]{:S(2)}) collective-permute-start(bf16[2,96,1536]{2,1,0:T(8,128)(2,1)} %slice.451), channel_id=1, source_target_pairs={{0,2},{1,3},{2,0},{3,1},{4,6},{5,7},{6,4},{7,5},{8,10},{9,11},{10,... | collective-permute-start | bytes 1769480 | tf_op jit(solution)/shard_map/ppermute | solution.py:535
  320.9 49.5 %collective-permute-start.26 = (bf16[2,96,1536]{2,1,0:T(8,128)(2,1)}, bf16[2,96,1536]{2,1,0:T(8,128)(2,1)}, u32[]{:S(2)}, u32[]{:S(2)}) collective-permute-start(bf16[2,96,1536]{2,1,0:T(8,128)(2,1)} %get-tuple-element.147), channel_id=1, source_target_pairs={{0,8},{4,12},{8,0},{12,4},{16,24},{20,28},{24,16},{28,20},{1,9},{5... | collective-permute-start | bytes 1769480 | tf_op jit(solution)/shard_map/ppermute | solution.py:531
  322.5 47.9 %collective-permute-start.27 = (bf16[2,96,1536]{2,1,0:T(8,128)(2,1)}, bf16[2,96,1536]{2,1,0:T(8,128)(2,1)}, u32[]{:S(2)}, u32[]{:S(2)}) collective-permute-start(bf16[2,96,1536]{2,1,0:T(8,128)(2,1)} %get-tuple-element.148), channel_id=1, source_target_pairs={{0,16},{4,20},{8,24},{12,28},{16,0},{20,4},{24,8},{28,12},{1,17},{... | collective-permute-start | bytes 1769480 | tf_op jit(solution)/shard_map/ppermute | solution.py:531
  330.7 48.3 %collective-permute-start.42 = (f32[16,768]{1,0:T(8,128)S(1)}, f32[16,768]{1,0:T(8,128)S(1)}, u32[]{:S(2)}, u32[]{:S(2)}) collective-permute-start(f32[16,768]{1,0:T(8,128)S(1)} %constant_dynamic-update-slice_fusion.15), channel_id=1, source_target_pairs={{0,4},{4,0},{8,12},{12,8},{16,20},{20,16},{24,28},{28,24},{1,5},{5... | collective-permute-start | bytes 147464 | tf_op jit(solution)/shard_map/ppermute | solution.py:531
  370.1 35.0 %collective-permute-start.25 = (bf16[4,4,96,768]{3,2,1,0:T(8,128)(2,1)}, bf16[4,4,96,768]{3,2,1,0:T(8,128)(2,1)S(1)}, u32[]{:S(2)}, u32[]{:S(2)}) collective-permute-start(bf16[4,4,96,768]{3,2,1,0:T(8,128)(2,1)} %get-tuple-element.143), channel_id=1, source_target_pairs={{0,4},{4,0},{8,12},{12,8},{16,20},{20,16},{24,28},{28,24},{1,5},{5... | collective-permute-start | bytes 7077896 | tf_op jit(solution)/shard_map/ppermute | solution.py:531
  373.0 35.6 %collective-permute-start.35 = (bf16[4,96,1536]{2,1,0:T(8,128)(2,1)S(1)}, bf16[4,96,1536]{2,1,0:T(8,128)(2,1)S(1)}, u32[]{:S(2)}, u32[]{:S(2)}) collective-permute-start(bf16[4,96,1536]{2,1,0:T(8,128)(2,1)S(1)} %pad_maximum_fusion.1), channel_id=1, source_target_pairs={{0,16},{4,20},{8,24},{12,28},{16,0},{20,4},{24,8},{28,12},{1,17},{... | collective-permute-start | bytes 3538952 | tf_op jit(solution)/shard_map/ppermute | solution.py:531
  374.7 33.9 %collective-permute-start.34 = (bf16[4,96,1536]{2,1,0:T(8,128)(2,1)S(1)}, bf16[4,96,1536]{2,1,0:T(8,128)(2,1)S(1)}, u32[]{:S(2)}, u32[]{:S(2)}) collective-permute-start(bf16[4,96,1536]{2,1,0:T(8,128)(2,1)S(1)} %pad_maximum_fusion), channel_id=1, source_target_pairs={{0,8},{4,12},{8,0},{12,4},{16,24},{20,28},{24,16},{28,20},{1,9},{5... | collective-permute-start | bytes 3538952 | tf_op jit(solution)/shard_map/ppermute | solution.py:531
  377.3 29.1 %collective-permute-start.41 = (bf16[96,1536]{1,0:T(8,128)(2,1)S(1)}, bf16[96,1536]{1,0:T(8,128)(2,1)S(1)}, u32[]{:S(2)}, u32[]{:S(2)}) collective-permute-start(bf16[96,1536]{1,0:T(8,128)(2,1)S(1)} %fusion.27), channel_id=1, source_target_pairs={{0,1},{1,0},{2,3},{3,2},{4,5},{5,4},{6,7},{7,6},{8,9},{9,8},{10,11... | collective-permute-start | bytes 884744 | tf_op jit(solution)/shard_map/ppermute | solution.py:535
  379.0 24.9 %collective-permute-start.43 = (f32[16,768]{1,0:T(8,128)S(1)}, f32[16,768]{1,0:T(8,128)S(1)}, u32[]{:S(2)}, u32[]{:S(2)}) collective-permute-start(f32[16,768]{1,0:T(8,128)S(1)} %add.317), channel_id=1, source_target_pairs={{0,8},{4,12},{8,0},{12,4},{16,24},{20,28},{24,16},{28,20},{1,9},{5... | collective-permute-start | bytes 147464 | tf_op jit(solution)/shard_map/ppermute | solution.py:531
  414.7 14.3 %collective-permute-start.31 = (bf16[4,96,768]{2,1,0:T(8,128)(2,1)S(1)}, bf16[4,96,768]{2,1,0:T(8,128)(2,1)S(1)}, u32[]{:S(2)}, u32[]{:S(2)}) collective-permute-start(bf16[4,96,768]{2,1,0:T(8,128)(2,1)S(1)} %pad_maximum_fusion.8), channel_id=1, source_target_pairs={{0,16},{4,20},{8,24},{12,28},{16,0},{20,4},{24,8},{28,12},{1,17},{... | collective-permute-start | bytes 1769480 | tf_op jit(solution)/shard_map/ppermute | solution.py:531
  419.7 34.0 %collective-permute-start.36 = (bf16[2,96,1536]{2,1,0:T(8,128)(2,1)S(1)}, bf16[2,96,1536]{2,1,0:T(8,128)(2,1)S(1)}, u32[]{:S(2)}, u32[]{:S(2)}) collective-permute-start(bf16[2,96,1536]{2,1,0:T(8,128)(2,1)S(1)} %slice.452), channel_id=1, source_target_pairs={{0,2},{1,3},{2,0},{3,1},{4,6},{5,7},{6,4},{7,5},{8,10},{9,11},{10,... | collective-permute-start | bytes 1769480 | tf_op jit(solution)/shard_map/ppermute | solution.py:535
  429.6 29.3 %collective-permute-start.32 = (bf16[2,96,768]{2,1,0:T(8,128)(2,1)S(1)}, bf16[2,96,768]{2,1,0:T(8,128)(2,1)S(1)}, u32[]{:S(2)}, u32[]{:S(2)}) collective-permute-start(bf16[2,96,768]{2,1,0:T(8,128)(2,1)S(1)} %slice.453), channel_id=1, source_target_pairs={{0,2},{1,3},{2,0},{3,1},{4,6},{5,7},{6,4},{7,5},{8,10},{9,11},{10,... | collective-permute-start | bytes 884744 | tf_op jit(solution)/shard_map/ppermute | solution.py:535
  (62 other events, 675.5 us)
Sparse Core Ops, SparseCore 0:
  11.5 134.8 all-gather.1
  238.0 131.1 reduce-scatter.1

commit v4 on v3

--- a/solution.py
+++ b/solution.py
@@ -521,7 +521,7 @@
             parts.append(part.transpose(1, 0, 2))
             start += wide
         packed = jnp.concatenate(parts, axis=2).reshape(self.n_col * D, sum(widths))
-        return lax.psum_scatter(packed, ("col", "row"), scatter_dimension=0, tiled=True).astype(F32)
+        return lax.psum_scatter(packed, ("col", "row"), scatter_dimension=0, tiled=True)
 
     def total(self, values, stages):
         return lax.psum(values, ("row", "col"))
@@ -536,6 +536,32 @@
 
 
 CORE, NEXT_X, NEXT_Y = 1, 2, 4
+
+
+def update_kernel(*refs):
+    grads, inputs, outputs = refs[:LAYERS], refs[LAYERS : LAYERS + 6], refs[LAYERS + 6 :]
+    cut = inputs[0].shape[2]
+    for level in range(LAYERS):
+        both = grads[level][...].astype(F32)
+        for index in range(2):
+            param, first, second = inputs[3 * index : 3 * index + 3]
+            grad_out, param_out, first_out, second_out = outputs[4 * index : 4 * index + 4]
+            gradient = both[:, cut:].T if index else both[:, :cut]
+            grad_out[level] = gradient
+            fresh = adamw_step(param[level], gradient, first[level], second[level])
+            param_out[level], first_out[level], second_out[level] = fresh
+
+
+def update_matrices(grads, first, second):
+    return pl.pallas_call(
+        update_kernel,
+        out_shape=[sds(group[0].shape, F32) for group in (first, second) for _ in range(4)],
+        in_specs=[VM] * (LAYERS + 6),
+        out_specs=[VM] * 8,
+        compiler_params=params(),
+        cost_estimate=cost(10**7, 10**5),
+        name="update",
+    )(*grads, *first, *second)
 
 
 class RelativeFetch:
@@ -577,7 +603,7 @@
 
     def scatter(self, full, widths):
         full = full.reshape(BLOCKS * D, -1)
-        return lax.psum_scatter(full, ("col", "row"), scatter_dimension=0, tiled=True).astype(F32)
+        return lax.psum_scatter(full, ("col", "row"), scatter_dimension=0, tiled=True)
 
     def reduce(self, near, far, widths, *earlier):
         far = after(far, *earlier)
@@ -605,7 +631,7 @@
         yield pair[0] + flip_col(pair[1].astype(BF), 1).astype(F32)
 
     def total(self, values, stages):
-        hops = [(flip_row, CORE), (flip_row, NEXT_X), (flip_row, NEXT_Y), (flip_col, 1), (flip_col, 2)]
+        hops = [(flip_col, 1), (flip_col, 2), (flip_row, CORE), (flip_row, NEXT_X), (flip_row, NEXT_Y)]
         for (flip, mask), stage in zip(hops, stages):
             values = values + after(flip(values, mask), *stage)
         return values
@@ -657,22 +683,19 @@
         fetches = [RelativeFetch(shard) for shard in shards[0]]
         one = fetches[0].turn_one()
         two = fetches[0].turn_two()
-        plane, ran, arrived = (), (), []
+        plane, ran, arrived = (), (gains,), []
         for index, fetch in enumerate(fetches):
             plane = (fetch.plane(*plane),)
             if index + 1 < len(fetches):
                 one = fetches[index + 1].turn_one(one)
                 two = fetches[index + 1].turn_two(two)
-            if index == 2:
-                state = forward_attend(0, hidden, arrived[0])
-                ran = (state[1],)
             arrived.append(fetch.rest(two, *ran))
-            ran = (gains,)
-        sooner = arrived[1] + arrived[2]
+            ran = ()
+        sooner = arrived[0], arrived[1] + arrived[2]
     else:
-        sooner = gathered(0)
-        state = forward_attend(0, hidden, sooner)
-    middle = forward_feed(0, hidden, state, sooner)
+        sooner = (gathered(0),) * 2
+    state = forward_attend(0, hidden, sooner[0])
+    middle = forward_feed(0, hidden, state, sooner[1])
     state = forward_attend(1, middle, later)
     hidden = forward_feed(1, middle, state, later)
     smalls = [None] * LAYERS
@@ -708,29 +731,29 @@
     turn_one, turn_zero, turn_last = ffn_one.send((smalls[0],)), ffn_zero.send(diag_last), att_zero.send(())
     done["ffn", 1], done["ffn", 0], done["att", 0] = ffn_one.send(diag_zero), ffn_zero.send(plane_last), att_zero.send(())
     layer_out = finish(seq, info, counts, hidden, [upstream])
-    grads = []
-    for level in range(LAYERS):
-        ffn, att = done["ffn", level], done["att", level]
-        grads.append((
-            att[:, : att_widths[0]], att[:, att_widths[0] :].T, ffn[:, : ffn_widths[0]], ffn[:, ffn_widths[0] :].T
-        ))
-    stages = [diag_zero, diag_zero, plane_zero, plane_zero, diag_last]
+    stages = [(), (), (), plane_one, plane_last]
     small = plan.total(jnp.concatenate(smalls, axis=0), stages).reshape(LAYERS, 8, D)
-    grad_list = [jnp.stack([grads[level][index] for level in range(LAYERS)]) for index in range(4)]
-    grad_list += [small[:, 0:2], small[:, 2:4], small[:, 4:8].reshape(LAYERS, FF)]
-    params_in = [w_qkv, w_out, w_up, w_down, norm_gains, res_biases, b_up]
-    firsts = [m_qkv, m_out, m_up, m_down, m_gains, m_biases, m_bup]
-    seconds = [v_qkv, v_out, v_up, v_down, v_gains, v_biases, v_bup]
-    results = [
-        adamw_step(params_in[index], grad_list[index], firsts[index], seconds[index])
-        for index in range(7)
+    ffn, att = [[done[name, level] for level in range(LAYERS)] for name in ("ffn", "att")]
+    tops = update_matrices(att, (w_qkv, m_qkv, v_qkv), (w_out, m_out, v_out))
+    feeds = update_matrices(ffn, (w_up, m_up, v_up), (w_down, m_down, v_down))
+    matrices = [tops[0:4], tops[4:8], feeds[0:4], feeds[4:8]]
+    vector_grads = [small[:, 0:2], small[:, 2:4], small[:, 4:8].reshape(LAYERS, FF)]
+    params_in = [norm_gains, res_biases, b_up]
+    firsts = [m_gains, m_biases, m_bup]
+    seconds = [v_gains, v_biases, v_bup]
+    vectors = [
+        adamw_step(params_in[index], vector_grads[index], firsts[index], seconds[index])
+        for index in range(3)
     ]
     return (
         (layer_out, upstream)
-        + tuple(grad_list)
-        + tuple(result[0] for result in results[:4])
-        + tuple(result[1] for result in results)
-        + tuple(result[2] for result in results)
+        + tuple(matrix[0] for matrix in matrices)
+        + tuple(vector_grads)
+        + tuple(matrix[1] for matrix in matrices)
+        + tuple(matrix[2] for matrix in matrices)
+        + tuple(vector[1] for vector in vectors)
+        + tuple(matrix[3] for matrix in matrices)
+        + tuple(vector[2] for vector in vectors)
     )
 
 

time: 489 us -> 447 us (0.914)
  waiting for transfers between devices: 253 us -> 204 us
  Pallas kernels: 93.4 us -> 103 us
    reduce_scatter x1, waiting for transfers between devices: 38.4 us -> 0.01 us  [scatter(): lax.psum_scatter(full, ('col', 'row'), scatter_dimension=0, tiled=True)]
    pallas_call x0 -> x2, Pallas kernels: none -> 9.47 us  [update_matrices(): pl.pallas_call(update_kernel, out_shape=[sds(group[0].shape, F32) for gro...]
    ppermute x33, starting transfers between devices: 34.1 us -> 27.3 us  [flip_row(): return lax.ppermute(x, 'row', [(i, i ^ mask) for i in range(8)])]
    ppermute x14, waiting for transfers between devices: 121 us -> 116 us  [flip_col(): return lax.ppermute(x, 'col', [(i, i ^ mask) for i in range(4)])]
    unnamed x116 -> x85, local copies, waits for them, and re-layouts: 25.3 us -> 30.1 us
  transfers between devices with their start and end apart: 49 -> 49, of which waited for: 25 -> 23; matrix products, arithmetic and copies ran while one was open for 11% -> 13% of each run, Pallas kernels for 13% -> 13%
where the time goes in v4:
time: 447 us; the launch traced here: 439 us
  waiting for transfers between devices  204 us (46%)
  Pallas kernels  103 us (23%)
  starting transfers between devices  50.8 us (11%)
  local copies, waits for them, and re-layouts  34.8 us (8%)
  other arithmetic  31.9 us (7%)
  between operations  15 us (3%)
    ppermute x14, waiting for transfers between devices, flip_col(): return lax.ppermute(x, 'col', [(i, i ^ mask) for i in range(4)])  116 us
    ppermute x33, waiting for transfers between devices, flip_row(): return lax.ppermute(x, 'row', [(i, i ^ mask) for i in range(8)])  88.6 us
    unnamed x85, local copies, waits for them, and re-layouts  30.1 us
    pallas_call x2, Pallas kernels, attend_back(): pl.pallas_call(functools.partial(attend_back_kernel, seq, level, whole_or...  27.5 us
    ppermute x33, starting transfers between devices, flip_row(): return lax.ppermute(x, 'row', [(i, i ^ mask) for i in range(8)])  27.3 us
    pallas_call x2, Pallas kernels, feed_back(): pl.pallas_call(functools.partial(feed_back_kernel, level, len(pieces), le...  25.7 us
    ppermute x14, starting transfers between devices, flip_col(): return lax.ppermute(x, 'col', [(i, i ^ mask) for i in range(4)])  23.5 us
    pallas_call x2, Pallas kernels, feed(): pl.pallas_call(functools.partial(feed_kernel, level, len(pieces)), grid=(...  17.6 us
  transfers between devices with their start and end apart: 49, of which 23 were waited for; matrix products, arithmetic and copies ran while one was open for 13% of the time, Pallas kernels for 13%

profile of v4, /device:TPU:0, one launch (start us, length us, event | category | flops | bytes accessed | tf_op | source)
XLA Modules:
  0.0 439.5 jit_solution(5748118790849980254)
XLA Ops:
  11.7 3.1 collective-permute-start
  14.8 3.8 collective-permute-done
  18.7 2.8 collective-permute-start.1
  23.1 16.2 %collective-permute-done.4 = bf16[96,768]{1,0:T(8,128)(2,1)S(1)} collective-permute-done((bf16[96,768]{1,0:T(8,128)(2,1)S(1)}, bf16[96,768]{1,0:T(8,128)(2,1)S(1)}, u32[]{:S(2)}, u32[]{:S(2)}) %collective-permute-start.4) | collective-permute-done | bytes 147488 | tf_op jit(solution)/shard_map/ppermute | solution.py:535
  52.8 3.3 prepare.1
  57.1 19.3 %collective-permute-done.5 = bf16[2,96,768]{2,1,0:T(8,128)(2,1)} collective-permute-done((bf16[2,96,768]{2,1,0:T(8,128)(2,1)}, bf16[2,96,768]{2,1,0:T(8,128)(2,1)}, u32[]{:S(2)}, u32[]{:S(2)}) %collective-permute-start.5) | collective-permute-done | bytes 294944 | tf_op jit(solution)/shard_map/ppermute | solution.py:535
  82.7 9.8 %collective-permute-done.12 = bf16[2,96,768]{2,1,0:T(8,128)(2,1)S(1)} collective-permute-done((bf16[2,96,768]{2,1,0:T(8,128)(2,1)S(1)}, bf16[2,96,768]{2,1,0:T(8,128)(2,1)S(1)}, u32[]{:S(2)}, u32[]{:S(2)}) %collective-permute-start.12) | collective-permute-done | bytes 294944 | tf_op jit(solution)/shard_map/ppermute | solution.py:535
  93.5 8.4 %collective-permute-done.6 = bf16[2,96,768]{2,1,0:T(8,128)(2,1)S(1)} collective-permute-done((bf16[2,96,768]{2,1,0:T(8,128)(2,1)S(1)}, bf16[2,96,768]{2,1,0:T(8,128)(2,1)S(1)}, u32[]{:S(2)}, u32[]{:S(2)}) %collective-permute-start.6) | collective-permute-done | bytes 294944 | tf_op jit(solution)/shard_map/ppermute | solution.py:531
  109.9 28.1 %collective-permute-done.13 = bf16[2,96,768]{2,1,0:T(8,128)(2,1)S(1)} collective-permute-done((bf16[2,96,768]{2,1,0:T(8,128)(2,1)S(1)}, bf16[2,96,768]{2,1,0:T(8,128)(2,1)S(1)}, u32[]{:S(2)}, u32[]{:S(2)}) %collective-permute-start.13) | collective-permute-done | bytes 294944 | tf_op jit(solution)/shard_map/ppermute | solution.py:531
  142.3 3.3 collective-permute-done.18
  146.3 3.4 collective-permute-done.19
  151.9 8.5 %attend.2 = (bf16[208,2304]{1,0:T(8,128)(2,1)}, f32[16,208]{1,0:T(8,128)}, bf16[4,208,256]{2,1,0:T(8,128)(2,1)}, f32[208,768]{1,0:T(8,128)}, bf16[208,768]{1,0:T(8,128)(2,1)}) custom-call(s32[4]{0:T(128)} %pad_add_fusion.info_ref, f32[208,768]{1,0:T(8,128)} %get-tuple-element.110.x_ref, f32[4,768]{1,0:T(4,128)} %get-tuple-element.111.gain_ref, ...), custom_call_target="tpu_custom_call" | custom-call | flops 10000000 | bytes 100000 | tf_op jit(solution)/shard_map/attend/pallas_call | solution.py:391
  160.4 9.1 %feed.2 = (bf16[4,208,768]{2,1,0:T(8,128)(2,1)}, f32[4,208,768]{2,1,0:T(8,128)}, f32[208,768]{1,0:T(8,128)}) custom-call(s32[4]{0:T(128)} %pad_add_fusion.info_ref, f32[208,768]{1,0:T(8,128)} %get-tuple-element.117.h1_ref, bf16[208,768]{1,0:T(8,128)(2,1)} %get-tuple-element.118.a2_ref, f32[4,768]{1,0:T(4,128)} %get-tuple-element.112.bias_ref, ...), custom_call_target="tpu_custom_call" | custom-call | flops 10000000 | bytes 100000 | tf_op jit(solution)/shard_map/feed/pallas_call | solution.py:411
  169.5 7.9 %attend.3 = (bf16[208,2304]{1,0:T(8,128)(2,1)}, f32[16,208]{1,0:T(8,128)}, bf16[4,208,256]{2,1,0:T(8,128)(2,1)}, f32[208,768]{1,0:T(8,128)}, bf16[208,768]{1,0:T(8,128)(2,1)}) custom-call(s32[4]{0:T(128)} %pad_add_fusion.info_ref, f32[208,768]{1,0:T(8,128)} %get-tuple-element.128.x_ref, f32[4,768]{1,0:T(4,128)} %get-tuple-element.111.gain_ref, ...), custom_call_target="tpu_custom_call" | custom-call | flops 10000000 | bytes 100000 | tf_op jit(solution)/shard_map/attend/pallas_call | solution.py:391
  177.5 8.6 %feed.3 = (bf16[4,208,768]{2,1,0:T(8,128)(2,1)}, f32[4,208,768]{2,1,0:T(8,128)}, f32[208,768]{1,0:T(8,128)}) custom-call(s32[4]{0:T(128)} %pad_add_fusion.info_ref, f32[208,768]{1,0:T(8,128)} %get-tuple-element.129.h1_ref, bf16[208,768]{1,0:T(8,128)(2,1)} %get-tuple-element.130.a2_ref, f32[4,768]{1,0:T(4,128)} %get-tuple-element.112.bias_ref, ...), custom_call_target="tpu_custom_call" | custom-call | flops 10000000 | bytes 100000 | tf_op jit(solution)/shard_map/feed/pallas_call | solution.py:411
  186.0 13.0 %feed_back.2 = (bf16[4,4,96,1536]{3,2,1,0:T(8,128)(2,1)}, bf16[4,4,96,1536]{3,2,1,0:T(8,128)(2,1)}, f32[4,1,768]{2,1,0:T(1,128)}, f32[208,768]{1,0:T(8,128)}, f32[8,768]{1,0:T(8,128)}) custom-call(s32[4]{0:T(128)} %pad_add_fusion.info_ref, f32[208,768]{1,0:T(8,128)} %get-tuple-element.132.g_ref, f32[208,768]{1,0:T(8,128)} %get-tuple-element.129.h1_ref, ...), custom_call_target="tpu_custom_call" | custom-call | flops 10000000 | bytes 100000 | tf_op jit(solution)/shard_map/feed_back/pallas_call | solution.py:436
  199.5 7.8 %collective-permute-done.21 = bf16[4,4,96,1536]{3,2,1,0:T(8,128)(2,1)S(1)} collective-permute-done((bf16[4,4,96,1536]{3,2,1,0:T(8,128)(2,1)}, bf16[4,4,96,1536]{3,2,1,0:T(8,128)(2,1)S(1)}, u32[]{:S(2)}, u32[]{:S(2)}) %collective-permute-start.21) | collective-permute-done | bytes 4718624 | tf_op jit(solution)/shard_map/ppermute | solution.py:531
  207.3 4.0 fusion.13
  213.4 13.8 %attend_back.2 = (bf16[4,8,96,768]{3,2,1,0:T(8,128)(2,1)}, f32[208,768]{1,0:T(8,128)}, f32[8,768]{1,0:T(8,128)}) custom-call(s32[4]{0:T(128)} %pad_add_fusion.info_ref, f32[208,768]{1,0:T(8,128)} %get-tuple-element.135.dh1_ref, f32[208,768]{1,0:T(8,128)} %get-tuple-element.128.x_ref, f32[4,768]{1,0:T(4,128)} %get-tuple-element.111.gain_ref, ...), custom_call_target="tpu_custom_call" | custom-call | flops 10000000 | bytes 100000 | tf_op jit(solution)/shard_map/attend_back/pallas_call | solution.py:457
  228.9 12.7 %feed_back.3 = (bf16[4,4,96,1536]{3,2,1,0:T(8,128)(2,1)}, bf16[4,4,96,1536]{3,2,1,0:T(8,128)(2,1)}, f32[4,1,768]{2,1,0:T(1,128)}, f32[208,768]{1,0:T(8,128)}, f32[8,768]{1,0:T(8,128)}) custom-call(s32[4]{0:T(128)} %pad_add_fusion.info_ref, f32[208,768]{1,0:T(8,128)} %get-tuple-element.141.g_ref, f32[208,768]{1,0:T(8,128)} %get-tuple-element.117.h1_ref, ...), custom_call_target="tpu_custom_call" | custom-call | flops 10000000 | bytes 100000 | tf_op jit(solution)/shard_map/feed_back/pallas_call | solution.py:436
  247.6 13.8 %attend_back.3 = (bf16[4,4,96,768]{3,2,1,0:T(8,128)(2,1)}, bf16[4,4,96,768]{3,2,1,0:T(8,128)(2,1)}, f32[1,197,768]{2,1,0:T(8,128)}, f32[8,768]{1,0:T(8,128)}) custom-call(s32[4]{0:T(128)} %pad_add_fusion.info_ref, f32[208,768]{1,0:T(8,128)} %get-tuple-element.146.dh1_ref, f32[208,768]{1,0:T(8,128)} %get-tuple-element.110.x_ref, ...), custom_call_target="tpu_custom_call" | custom-call | flops 10000000 | bytes 100000 | tf_op jit(solution)/shard_map/attend_back/pallas_call | solution.py:457
  262.1 7.8 %collective-permute-start.42 = (f32[16,768]{1,0:T(8,128)S(1)}, f32[16,768]{1,0:T(8,128)S(1)}, u32[]{:S(2)}, u32[]{:S(2)}) collective-permute-start(f32[16,768]{1,0:T(8,128)S(1)} %constant_dynamic-update-slice_fusion.15), channel_id=1, source_target_pairs={{0,1},{1,0},{2,3},{3,2},{4,5},{5,4},{6,7},{7,6},{8,9},{9,8},{10,11... | collective-permute-start | bytes 147464 | tf_op jit(solution)/shard_map/ppermute | solution.py:535
  272.6 4.6 %collective-permute-done.43 = f32[16,768]{1,0:T(8,128)S(1)} collective-permute-done((f32[16,768]{1,0:T(8,128)S(1)}, f32[16,768]{1,0:T(8,128)S(1)}, u32[]{:S(2)}, u32[]{:S(2)}) %collective-permute-start.43) | collective-permute-done | bytes 49184 | tf_op jit(solution)/shard_map/ppermute | solution.py:535
  292.2 3.2 fusion.11
  301.6 9.4 %collective-permute-done.26 = bf16[2,96,1536]{2,1,0:T(8,128)(2,1)S(1)} collective-permute-done((bf16[2,96,1536]{2,1,0:T(8,128)(2,1)S(1)}, bf16[2,96,1536]{2,1,0:T(8,128)(2,1)S(1)}, u32[]{:S(2)}, u32[]{:S(2)}) %collective-permute-start.26) | collective-permute-done | bytes 589856 | tf_op jit(solution)/shard_map/ppermute | solution.py:531
  316.7 11.7 %collective-permute-done.40 = bf16[2,96,1536]{2,1,0:T(8,128)(2,1)S(1)} collective-permute-done((bf16[2,96,1536]{2,1,0:T(8,128)(2,1)S(1)}, bf16[2,96,1536]{2,1,0:T(8,128)(2,1)S(1)}, u32[]{:S(2)}, u32[]{:S(2)}) %collective-permute-start.40) | collective-permute-done | bytes 589856 | tf_op jit(solution)/shard_map/ppermute | solution.py:535
  331.2 24.1 %collective-permute-done.28 = bf16[2,96,768]{2,1,0:T(8,128)(2,1)S(1)} collective-permute-done((bf16[2,96,768]{2,1,0:T(8,128)(2,1)S(1)}, bf16[2,96,768]{2,1,0:T(8,128)(2,1)S(1)}, u32[]{:S(2)}, u32[]{:S(2)}) %collective-permute-start.28) | collective-permute-done | bytes 294944 | tf_op jit(solution)/shard_map/ppermute | solution.py:531
  362.7 7.7 %collective-permute-done.41 = bf16[96,1536]{1,0:T(8,128)(2,1)S(1)} collective-permute-done((bf16[96,1536]{1,0:T(8,128)(2,1)S(1)}, bf16[96,1536]{1,0:T(8,128)(2,1)S(1)}, u32[]{:S(2)}, u32[]{:S(2)}) %collective-permute-start.41) | collective-permute-done | bytes 294944 | tf_op jit(solution)/shard_map/ppermute | solution.py:535
  373.4 30.2 %collective-permute-done.36 = bf16[2,96,1536]{2,1,0:T(8,128)(2,1)S(1)} collective-permute-done((bf16[2,96,1536]{2,1,0:T(8,128)(2,1)S(1)}, bf16[2,96,1536]{2,1,0:T(8,128)(2,1)S(1)}, u32[]{:S(2)}, u32[]{:S(2)}) %collective-permute-start.36) | collective-permute-done | bytes 589856 | tf_op jit(solution)/shard_map/ppermute | solution.py:535
  408.1 6.5 %collective-permute-done.37 = bf16[96,1536]{1,0:T(8,128)(2,1)S(1)} collective-permute-done((bf16[96,1536]{1,0:T(8,128)(2,1)S(1)}, bf16[96,1536]{1,0:T(8,128)(2,1)S(1)}, u32[]{:S(2)}, u32[]{:S(2)}) %collective-permute-start.37) | collective-permute-done | bytes 294944 | tf_op jit(solution)/shard_map/ppermute | solution.py:535
  415.5 5.8 %update.3 = (f32[2,96,768]{2,1,0:T(8,128)}, f32[2,96,768]{2,1,0:T(8,128)}, f32[2,96,768]{2,1,0:T(8,128)}, f32[2,96,768]{2,1,0:T(8,128)}, f32[2,768,96]{2,1,0:T(8...) custom-call(f32[96,1536]{1,0:T(8,128)} %fusion.16.refs_0_, ...), custom_call_target="tpu_custom_call" | custom-call | flops 10000000 | bytes 100000 | tf_op jit(solution)/shard_map/update/pallas_call | solution.py:556
  428.7 3.7 update.2
  (230 shorter events, 109.2 us)
Async XLA Ops:
  7.2 162.3 %all-gather.2.cloned.1.call-start = ((), (), s32[]{:S(2)}) async-start(), calls=%async_computation.1 | async-start | bytes 14598144 | tf_op jit(solution)/shard_map/all_gather | solution.py:601
  11.6 417.1 %reduce-scatter.2.cloned.1.call-start = ((), (), s32[]{:S(2)}) async-start(), calls=%async_computation.2 | async-start | bytes 4866048 | tf_op jit(solution)/shard_map/reduce_scatter | solution.py:606
  18.7 25.0 %collective-permute-start.1 = (bf16[2,96,768]{2,1,0:T(8,128)(2,1)S(1)}, bf16[2,96,768]{2,1,0:T(8,128)(2,1)S(1)}, u32[]{:S(2)}, u32[]{:S(2)}) collective-permute-start(bf16[2,96,768]{2,1,0:T(8,128)(2,1)S(1)} %pad_maximum_fusion.9), channel_id=1, source_target_pairs={{0,2},{1,3},{2,0},{3,1},{4,6},{5,7},{6,4},{7,5},{8,10},{9,11},{10,... | collective-permute-start | bytes 884744 | tf_op jit(solution)/shard_map/ppermute | solution.py:535
  21.5 17.8 %collective-permute-start.4 = (bf16[96,768]{1,0:T(8,128)(2,1)S(1)}, bf16[96,768]{1,0:T(8,128)(2,1)S(1)}, u32[]{:S(2)}, u32[]{:S(2)}) collective-permute-start(bf16[96,768]{1,0:T(8,128)(2,1)S(1)} %get-tuple-element.113), channel_id=1, source_target_pairs={{0,1},{1,0},{2,3},{3,2},{4,5},{5,4},{6,7},{7,6},{8,9},{9,8},{10,11... | collective-permute-start | bytes 442376 | tf_op jit(solution)/shard_map/ppermute | solution.py:535
  39.3 16.8 %collective-permute-start.11 = (bf16[96,768]{1,0:T(8,128)(2,1)S(1)}, bf16[96,768]{1,0:T(8,128)(2,1)}, u32[]{:S(2)}, u32[]{:S(2)}) collective-permute-start(bf16[96,768]{1,0:T(8,128)(2,1)S(1)} %get-tuple-element.121), channel_id=1, source_target_pairs={{0,1},{1,0},{2,3},{3,2},{4,5},{5,4},{6,7},{7,6},{8,9},{9,8},{10,11... | collective-permute-start | bytes 442376 | tf_op jit(solution)/shard_map/ppermute | solution.py:535
  43.8 33.7 %collective-permute-start.2 = (bf16[4,96,768]{2,1,0:T(8,128)(2,1)S(1)}, bf16[4,96,768]{2,1,0:T(8,128)(2,1)S(1)}, u32[]{:S(2)}, u32[]{:S(2)}) collective-permute-start(bf16[4,96,768]{2,1,0:T(8,128)(2,1)S(1)} %pad_maximum_fusion.4), channel_id=1, source_target_pairs={{0,8},{4,12},{8,0},{12,4},{16,24},{20,28},{24,16},{28,20},{1,9},{5... | collective-permute-start | bytes 1769480 | tf_op jit(solution)/shard_map/ppermute | solution.py:531
  45.9 33.4 %collective-permute-start.3 = (bf16[4,96,768]{2,1,0:T(8,128)(2,1)S(1)}, bf16[4,96,768]{2,1,0:T(8,128)(2,1)S(1)}, u32[]{:S(2)}, u32[]{:S(2)}) collective-permute-start(bf16[4,96,768]{2,1,0:T(8,128)(2,1)S(1)} %pad_maximum_fusion.4), channel_id=1, source_target_pairs={{0,16},{4,20},{8,24},{12,28},{16,0},{20,4},{24,8},{28,12},{1,17},{... | collective-permute-start | bytes 1769480 | tf_op jit(solution)/shard_map/ppermute | solution.py:531
  47.4 29.0 %collective-permute-start.5 = (bf16[2,96,768]{2,1,0:T(8,128)(2,1)}, bf16[2,96,768]{2,1,0:T(8,128)(2,1)}, u32[]{:S(2)}, u32[]{:S(2)}) collective-permute-start(bf16[2,96,768]{2,1,0:T(8,128)(2,1)} %pad_maximum_fusion.10), channel_id=1, source_target_pairs={{0,2},{1,3},{2,0},{3,1},{4,6},{5,7},{6,4},{7,5},{8,10},{9,11},{10,... | collective-permute-start | bytes 884744 | tf_op jit(solution)/shard_map/ppermute | solution.py:535
  76.5 16.0 %collective-permute-start.12 = (bf16[2,96,768]{2,1,0:T(8,128)(2,1)S(1)}, bf16[2,96,768]{2,1,0:T(8,128)(2,1)S(1)}, u32[]{:S(2)}, u32[]{:S(2)}) collective-permute-start(bf16[2,96,768]{2,1,0:T(8,128)(2,1)S(1)} %pad_maximum_fusion.11), channel_id=1, source_target_pairs={{0,2},{1,3},{2,0},{3,1},{4,6},{5,7},{6,4},{7,5},{8,10},{9,11},{10,... | collective-permute-start | bytes 884744 | tf_op jit(solution)/shard_map/ppermute | solution.py:535
  77.5 24.4 %collective-permute-start.9 = (bf16[4,96,768]{2,1,0:T(8,128)(2,1)S(1)}, bf16[4,96,768]{2,1,0:T(8,128)(2,1)S(1)}, u32[]{:S(2)}, u32[]{:S(2)}) collective-permute-start(bf16[4,96,768]{2,1,0:T(8,128)(2,1)S(1)} %pad_maximum_fusion.5), channel_id=1, source_target_pairs={{0,8},{4,12},{8,0},{12,4},{16,24},{20,28},{24,16},{28,20},{1,9},{5... | collective-permute-start | bytes 1769480 | tf_op jit(solution)/shard_map/ppermute | solution.py:531
  79.0 26.1 %collective-permute-start.10 = (bf16[4,96,768]{2,1,0:T(8,128)(2,1)S(1)}, bf16[4,96,768]{2,1,0:T(8,128)(2,1)S(1)}, u32[]{:S(2)}, u32[]{:S(2)}) collective-permute-start(bf16[4,96,768]{2,1,0:T(8,128)(2,1)S(1)} %pad_maximum_fusion.5), channel_id=1, source_target_pairs={{0,16},{4,20},{8,24},{12,28},{16,0},{20,4},{24,8},{28,12},{1,17},{... | collective-permute-start | bytes 1769480 | tf_op jit(solution)/shard_map/ppermute | solution.py:531
  79.3 22.6 %collective-permute-start.6 = (bf16[2,96,768]{2,1,0:T(8,128)(2,1)S(1)}, bf16[2,96,768]{2,1,0:T(8,128)(2,1)S(1)}, u32[]{:S(2)}, u32[]{:S(2)}) collective-permute-start(bf16[2,96,768]{2,1,0:T(8,128)(2,1)S(1)} %slice.230), channel_id=1, source_target_pairs={{0,8},{4,12},{8,0},{12,4},{16,24},{20,28},{24,16},{28,20},{1,9},{5... | collective-permute-start | bytes 884744 | tf_op jit(solution)/shard_map/ppermute | solution.py:531
  81.2 23.8 %collective-permute-start.7 = (bf16[2,96,768]{2,1,0:T(8,128)(2,1)S(1)}, bf16[2,96,768]{2,1,0:T(8,128)(2,1)S(1)}, u32[]{:S(2)}, u32[]{:S(2)}) collective-permute-start(bf16[2,96,768]{2,1,0:T(8,128)(2,1)S(1)} %slice.231), channel_id=1, source_target_pairs={{0,16},{4,20},{8,24},{12,28},{16,0},{20,4},{24,8},{28,12},{1,17},{... | collective-permute-start | bytes 884744 | tf_op jit(solution)/shard_map/ppermute | solution.py:531
  101.9 36.8 %collective-permute-start.16 = (bf16[4,96,768]{2,1,0:T(8,128)(2,1)S(1)}, bf16[4,96,768]{2,1,0:T(8,128)(2,1)S(1)}, u32[]{:S(2)}, u32[]{:S(2)}) collective-permute-start(bf16[4,96,768]{2,1,0:T(8,128)(2,1)S(1)} %pad_maximum_fusion.6), channel_id=1, source_target_pairs={{0,8},{4,12},{8,0},{12,4},{16,24},{20,28},{24,16},{28,20},{1,9},{5... | collective-permute-start | bytes 1769480 | tf_op jit(solution)/shard_map/ppermute | solution.py:531
  103.0 35.7 %collective-permute-start.17 = (bf16[4,96,768]{2,1,0:T(8,128)(2,1)S(1)}, bf16[4,96,768]{2,1,0:T(8,128)(2,1)S(1)}, u32[]{:S(2)}, u32[]{:S(2)}) collective-permute-start(bf16[4,96,768]{2,1,0:T(8,128)(2,1)S(1)} %pad_maximum_fusion.6), channel_id=1, source_target_pairs={{0,16},{4,20},{8,24},{12,28},{16,0},{20,4},{24,8},{28,12},{1,17},{... | collective-permute-start | bytes 1769480 | tf_op jit(solution)/shard_map/ppermute | solution.py:531
  105.0 45.5 %collective-permute-start.8 = (bf16[4,4,96,768]{3,2,1,0:T(8,128)(2,1)S(1)}, bf16[4,4,96,768]{3,2,1,0:T(8,128)(2,1)S(1)}, u32[]{:S(2)}, u32[]{:S(2)}) collective-permute-start(bf16[4,4,96,768]{3,2,1,0:T(8,128)(2,1)S(1)} %bitcast.124), channel_id=1, source_target_pairs={{0,4},{4,0},{8,12},{12,8},{16,20},{20,16},{24,28},{28,24},{1,5},{5... | collective-permute-start | bytes 7077896 | tf_op jit(solution)/shard_map/ppermute | solution.py:531
  105.1 32.9 %collective-permute-start.13 = (bf16[2,96,768]{2,1,0:T(8,128)(2,1)S(1)}, bf16[2,96,768]{2,1,0:T(8,128)(2,1)S(1)}, u32[]{:S(2)}, u32[]{:S(2)}) collective-permute-start(bf16[2,96,768]{2,1,0:T(8,128)(2,1)S(1)} %slice.233), channel_id=1, source_target_pairs={{0,8},{4,12},{8,0},{12,4},{16,24},{20,28},{24,16},{28,20},{1,9},{5... | collective-permute-start | bytes 884744 | tf_op jit(solution)/shard_map/ppermute | solution.py:531
  107.5 32.0 %collective-permute-start.14 = (bf16[2,96,768]{2,1,0:T(8,128)(2,1)S(1)}, bf16[2,96,768]{2,1,0:T(8,128)(2,1)S(1)}, u32[]{:S(2)}, u32[]{:S(2)}) collective-permute-start(bf16[2,96,768]{2,1,0:T(8,128)(2,1)S(1)} %slice.234), channel_id=1, source_target_pairs={{0,16},{4,20},{8,24},{12,28},{16,0},{20,4},{24,8},{28,12},{1,17},{... | collective-permute-start | bytes 884744 | tf_op jit(solution)/shard_map/ppermute | solution.py:531
  140.2 20.2 %collective-permute-start.15 = (bf16[4,4,96,768]{3,2,1,0:T(8,128)(2,1)}, bf16[4,4,96,768]{3,2,1,0:T(8,128)(2,1)}, u32[]{:S(2)}, u32[]{:S(2)}) collective-permute-start(bf16[4,4,96,768]{3,2,1,0:T(8,128)(2,1)} %bitcast.15.rest_0_), channel_id=1, source_target_pairs={{0,4},{4,0},{8,12},{12,8},{16,20},{20,16},{24,28},{28,24},{1,5},{5... | collective-permute-start | bytes 7077896 | tf_op jit(solution)/shard_map/ppermute | solution.py:531
  241.5 50.3 %collective-permute-start.24 = (bf16[4,4,96,1536]{3,2,1,0:T(8,128)(2,1)}, bf16[4,4,96,1536]{3,2,1,0:T(8,128)(2,1)}, u32[]{:S(2)}, u32[]{:S(2)}) collective-permute-start(bf16[4,4,96,1536]{3,2,1,0:T(8,128)(2,1)} %get-tuple-element.155), channel_id=1, source_target_pairs={{0,4},{4,0},{8,12},{12,8},{16,20},{20,16},{24,28},{28,24},{1,5},{5... | collective-permute-start | bytes 14155784 | tf_op jit(solution)/shard_map/ppermute | solution.py:531
  245.2 46.7 %collective-permute-start.39 = (bf16[4,96,1536]{2,1,0:T(8,128)(2,1)}, bf16[4,96,1536]{2,1,0:T(8,128)(2,1)S(1)}, u32[]{:S(2)}, u32[]{:S(2)}) collective-permute-start(bf16[4,96,1536]{2,1,0:T(8,128)(2,1)} %pad_maximum_fusion.3), channel_id=1, source_target_pairs={{0,16},{4,20},{8,24},{12,28},{16,0},{20,4},{24,8},{28,12},{1,17},{... | collective-permute-start | bytes 3538952 | tf_op jit(solution)/shard_map/ppermute | solution.py:531
  247.0 44.9 %collective-permute-start.38 = (bf16[4,96,1536]{2,1,0:T(8,128)(2,1)}, bf16[4,96,1536]{2,1,0:T(8,128)(2,1)S(1)}, u32[]{:S(2)}, u32[]{:S(2)}) collective-permute-start(bf16[4,96,1536]{2,1,0:T(8,128)(2,1)} %pad_maximum_fusion.2), channel_id=1, source_target_pairs={{0,8},{4,12},{8,0},{12,4},{16,24},{20,28},{24,16},{28,20},{1,9},{5... | collective-permute-start | bytes 3538952 | tf_op jit(solution)/shard_map/ppermute | solution.py:531
  291.9 36.7 %collective-permute-start.25 = (bf16[4,4,96,768]{3,2,1,0:T(8,128)(2,1)}, bf16[4,4,96,768]{3,2,1,0:T(8,128)(2,1)S(1)}, u32[]{:S(2)}, u32[]{:S(2)}) collective-permute-start(bf16[4,4,96,768]{3,2,1,0:T(8,128)(2,1)} %get-tuple-element.156), channel_id=1, source_target_pairs={{0,4},{4,0},{8,12},{12,8},{16,20},{20,16},{24,28},{28,24},{1,5},{5... | collective-permute-start | bytes 7077896 | tf_op jit(solution)/shard_map/ppermute | solution.py:531
  299.8 28.6 %collective-permute-start.40 = (bf16[2,96,1536]{2,1,0:T(8,128)(2,1)S(1)}, bf16[2,96,1536]{2,1,0:T(8,128)(2,1)S(1)}, u32[]{:S(2)}, u32[]{:S(2)}) collective-permute-start(bf16[2,96,1536]{2,1,0:T(8,128)(2,1)S(1)} %slice.403), channel_id=1, source_target_pairs={{0,2},{1,3},{2,0},{3,1},{4,6},{5,7},{6,4},{7,5},{8,10},{9,11},{10,... | collective-permute-start | bytes 1769480 | tf_op jit(solution)/shard_map/ppermute | solution.py:535
  300.4 103.5 %collective-permute-start.46 = (f32[16,768]{1,0:T(8,128)S(1)}, f32[16,768]{1,0:T(8,128)S(1)}, u32[]{:S(2)}, u32[]{:S(2)}) collective-permute-start(f32[16,768]{1,0:T(8,128)S(1)} %add.260), channel_id=1, source_target_pairs={{0,16},{4,20},{8,24},{12,28},{16,0},{20,4},{24,8},{28,12},{1,17},{... | collective-permute-start | bytes 147464 | tf_op jit(solution)/shard_map/ppermute | solution.py:531
  314.1 44.6 %collective-permute-start.35 = (bf16[4,96,1536]{2,1,0:T(8,128)(2,1)S(1)}, bf16[4,96,1536]{2,1,0:T(8,128)(2,1)S(1)}, u32[]{:S(2)}, u32[]{:S(2)}) collective-permute-start(bf16[4,96,1536]{2,1,0:T(8,128)(2,1)S(1)} %pad_maximum_fusion.1), channel_id=1, source_target_pairs={{0,16},{4,20},{8,24},{12,28},{16,0},{20,4},{24,8},{28,12},{1,17},{... | collective-permute-start | bytes 3538952 | tf_op jit(solution)/shard_map/ppermute | solution.py:531
  315.1 45.1 %collective-permute-start.34 = (bf16[4,96,1536]{2,1,0:T(8,128)(2,1)S(1)}, bf16[4,96,1536]{2,1,0:T(8,128)(2,1)S(1)}, u32[]{:S(2)}, u32[]{:S(2)}) collective-permute-start(bf16[4,96,1536]{2,1,0:T(8,128)(2,1)S(1)} %pad_maximum_fusion), channel_id=1, source_target_pairs={{0,8},{4,12},{8,0},{12,4},{16,24},{20,28},{24,16},{28,20},{1,9},{5... | collective-permute-start | bytes 3538952 | tf_op jit(solution)/shard_map/ppermute | solution.py:531
  328.9 26.5 %collective-permute-start.28 = (bf16[2,96,768]{2,1,0:T(8,128)(2,1)S(1)}, bf16[2,96,768]{2,1,0:T(8,128)(2,1)S(1)}, u32[]{:S(2)}, u32[]{:S(2)}) collective-permute-start(bf16[2,96,768]{2,1,0:T(8,128)(2,1)S(1)} %get-tuple-element.163), channel_id=1, source_target_pairs={{0,16},{4,20},{8,24},{12,28},{16,0},{20,4},{24,8},{28,12},{1,17},{... | collective-permute-start | bytes 884744 | tf_op jit(solution)/shard_map/ppermute | solution.py:531
  330.1 27.1 %collective-permute-start.30 = (bf16[2,96,768]{2,1,0:T(8,128)(2,1)S(1)}, bf16[2,96,768]{2,1,0:T(8,128)(2,1)S(1)}, u32[]{:S(2)}, u32[]{:S(2)}) collective-permute-start(bf16[2,96,768]{2,1,0:T(8,128)(2,1)S(1)} %get-tuple-element.164), channel_id=1, source_target_pairs={{0,8},{4,12},{8,0},{12,4},{16,24},{20,28},{24,16},{28,20},{1,9},{5... | collective-permute-start | bytes 884744 | tf_op jit(solution)/shard_map/ppermute | solution.py:531
  362.0 41.6 %collective-permute-start.36 = (bf16[2,96,1536]{2,1,0:T(8,128)(2,1)S(1)}, bf16[2,96,1536]{2,1,0:T(8,128)(2,1)S(1)}, u32[]{:S(2)}, u32[]{:S(2)}) collective-permute-start(bf16[2,96,1536]{2,1,0:T(8,128)(2,1)S(1)} %slice.404), channel_id=1, source_target_pairs={{0,2},{1,3},{2,0},{3,1},{4,6},{5,7},{6,4},{7,5},{8,10},{9,11},{10,... | collective-permute-start | bytes 1769480 | tf_op jit(solution)/shard_map/ppermute | solution.py:535
  371.7 36.0 %collective-permute-start.32 = (bf16[2,96,768]{2,1,0:T(8,128)(2,1)S(1)}, bf16[2,96,768]{2,1,0:T(8,128)(2,1)S(1)}, u32[]{:S(2)}, u32[]{:S(2)}) collective-permute-start(bf16[2,96,768]{2,1,0:T(8,128)(2,1)S(1)} %slice.405), channel_id=1, source_target_pairs={{0,2},{1,3},{2,0},{3,1},{4,6},{5,7},{6,4},{7,5},{8,10},{9,11},{10,... | collective-permute-start | bytes 884744 | tf_op jit(solution)/shard_map/ppermute | solution.py:535
  407.8 20.1 %collective-permute-start.33 = (bf16[96,768]{1,0:T(8,128)(2,1)S(1)}, bf16[96,768]{1,0:T(8,128)(2,1)S(1)}, u32[]{:S(2)}, u32[]{:S(2)}) collective-permute-start(bf16[96,768]{1,0:T(8,128)(2,1)S(1)} %fusion.26), channel_id=1, source_target_pairs={{0,1},{1,0},{2,3},{3,2},{4,5},{5,4},{6,7},{7,6},{8,9},{9,8},{10,11... | collective-permute-start | bytes 442376 | tf_op jit(solution)/shard_map/ppermute | solution.py:535
  (46 other events, 731.3 us)
Sparse Core Ops, SparseCore 0:
  11.7 146.3 all-gather.1
  282.5 142.2 reduce-scatter.1

commit v5 on v4

--- a/solution.py
+++ b/solution.py
@@ -538,7 +538,7 @@
 CORE, NEXT_X, NEXT_Y = 1, 2, 4
 
 
-def update_kernel(*refs):
+def update_kernel(turn, *refs):
     grads, inputs, outputs = refs[:LAYERS], refs[LAYERS : LAYERS + 6], refs[LAYERS + 6 :]
     cut = inputs[0].shape[2]
     for level in range(LAYERS):
@@ -546,15 +546,17 @@
         for index in range(2):
             param, first, second = inputs[3 * index : 3 * index + 3]
             grad_out, param_out, first_out, second_out = outputs[4 * index : 4 * index + 4]
-            gradient = both[:, cut:].T if index else both[:, :cut]
+            gradient = both[:, cut:] if index else both[:, :cut]
+            if index and turn:
+                gradient = gradient.T
             grad_out[level] = gradient
             fresh = adamw_step(param[level], gradient, first[level], second[level])
             param_out[level], first_out[level], second_out[level] = fresh
 
 
-def update_matrices(grads, first, second):
+def update_matrices(turn, grads, first, second):
     return pl.pallas_call(
-        update_kernel,
+        functools.partial(update_kernel, turn),
         out_shape=[sds(group[0].shape, F32) for group in (first, second) for _ in range(4)],
         in_specs=[VM] * (LAYERS + 6),
         out_specs=[VM] * 8,
@@ -626,9 +628,9 @@
         from_x, from_y = after(from_x, from_y, *hold), after(from_y, from_x, *hold)
         plane = joined(0, every) + from_x.astype(F32) + from_y.astype(F32)
         others = flip_col(plane[2:4].astype(BF), 2)
-        hold = yield others
+        hold, last = yield others
         pair = plane[0:2] + after(others, *hold).astype(F32)
-        yield pair[0] + flip_col(pair[1].astype(BF), 1).astype(F32)
+        yield pair[0] + flip_col(after(pair[1].astype(BF), *last), 1).astype(F32)
 
     def total(self, values, stages):
         hops = [(flip_col, 1), (flip_col, 2), (flip_row, CORE), (flip_row, NEXT_X), (flip_row, NEXT_Y)]
@@ -728,15 +730,23 @@
     plane_zero = ffn_zero.send(())
     diag_last = att_zero.send(diag_zero)
     plane_last = att_zero.send(())
-    turn_one, turn_zero, turn_last = ffn_one.send((smalls[0],)), ffn_zero.send(diag_last), att_zero.send(())
-    done["ffn", 1], done["ffn", 0], done["att", 0] = ffn_one.send(diag_zero), ffn_zero.send(plane_last), att_zero.send(())
+    turn_one, turn_zero, turn_last = ffn_one.send((smalls[0],)), ffn_zero.send(diag_last), att_zero.send((done["att", 1],))
+    done["ffn", 1], done["ffn", 0], done["att", 0] = (
+        ffn_one.send((diag_zero, ())),
+        ffn_zero.send((plane_last, ())),
+        att_zero.send(((), ())),
+    )
     layer_out = finish(seq, info, counts, hidden, [upstream])
     stages = [(), (), (), plane_one, plane_last]
     small = plan.total(jnp.concatenate(smalls, axis=0), stages).reshape(LAYERS, 8, D)
     ffn, att = [[done[name, level] for level in range(LAYERS)] for name in ("ffn", "att")]
-    tops = update_matrices(att, (w_qkv, m_qkv, v_qkv), (w_out, m_out, v_out))
-    feeds = update_matrices(ffn, (w_up, m_up, v_up), (w_down, m_down, v_down))
-    matrices = [tops[0:4], tops[4:8], feeds[0:4], feeds[4:8]]
+
+    def turned(arrays):
+        return [array.transpose(0, 2, 1) for array in arrays]
+
+    tops = update_matrices(True, att, (w_qkv, m_qkv, v_qkv), (w_out, m_out, v_out))
+    feeds = update_matrices(False, ffn, (w_up, m_up, v_up), turned((w_down, m_down, v_down)))
+    matrices = [tops[0:4], tops[4:8], feeds[0:4], turned(feeds[4:8])]
     vector_grads = [small[:, 0:2], small[:, 2:4], small[:, 4:8].reshape(LAYERS, FF)]
     params_in = [norm_gains, res_biases, b_up]
     firsts = [m_gains, m_biases, m_bup]

time: 447 us -> 438 us (0.980)
  waiting for transfers between devices: 204 us -> 186 us
  starting transfers between devices: 50.8 us -> 66.2 us
  local copies, waits for them, and re-layouts: 34.8 us -> 22.9 us
  other arithmetic: 31.9 us -> 38.2 us
    ppermute x14, waiting for transfers between devices: 116 us -> 89.5 us  [flip_col(): return lax.ppermute(x, 'col', [(i, i ^ mask) for i in range(4)])]
    unnamed x85 -> x78, local copies, waits for them, and re-layouts: 30.1 us -> 17.4 us
    ppermute x14, starting transfers between devices: 23.5 us -> 35.8 us  [flip_col(): return lax.ppermute(x, 'col', [(i, i ^ mask) for i in range(4)])]
    ppermute x33, waiting for transfers between devices: 88.6 us -> 96.8 us  [flip_row(): return lax.ppermute(x, 'row', [(i, i ^ mask) for i in range(8)])]
  transfers between devices with their start and end apart: 49 -> 49, of which waited for: 23 -> 21; matrix products, arithmetic and copies ran while one was open for 13% -> 11% of each run, Pallas kernels for 13% -> 13%
where the time goes in v5:
time: 438 us; the launch traced here: 431 us
  waiting for transfers between devices  186 us (42%)
  Pallas kernels  102 us (23%)
  starting transfers between devices  66.2 us (15%)
  other arithmetic  38.2 us (9%)
  local copies, waits for them, and re-layouts  22.9 us (5%)
  between operations  15.1 us (3%)
    ppermute x33, waiting for transfers between devices, flip_row(): return lax.ppermute(x, 'row', [(i, i ^ mask) for i in range(8)])  96.8 us
    ppermute x14, waiting for transfers between devices, flip_col(): return lax.ppermute(x, 'col', [(i, i ^ mask) for i in range(4)])  89.5 us
    ppermute x14, starting transfers between devices, flip_col(): return lax.ppermute(x, 'col', [(i, i ^ mask) for i in range(4)])  35.8 us
    ppermute x33, starting transfers between devices, flip_row(): return lax.ppermute(x, 'row', [(i, i ^ mask) for i in range(8)])  30.2 us
    pallas_call x2, Pallas kernels, attend_back(): pl.pallas_call(functools.partial(attend_back_kernel, seq, level, whole_or...  27.5 us
    pallas_call x2, Pallas kernels, feed_back(): pl.pallas_call(functools.partial(feed_back_kernel, level, len(pieces), le...  25.6 us
    pallas_call x2, Pallas kernels, feed(): pl.pallas_call(functools.partial(feed_kernel, level, len(pieces)), grid=(...  17.6 us
    unnamed x78, local copies, waits for them, and re-layouts  17.4 us
  transfers between devices with their start and end apart: 49, of which 21 were waited for; matrix products, arithmetic and copies ran while one was open for 11% of the time, Pallas kernels for 13%

profile of v5, /device:TPU:0, one launch (start us, length us, event | category | flops | bytes accessed | tf_op | source)
XLA Modules:
  0.0 430.8 jit_solution(13882129387847726156)
XLA Ops:
  11.7 3.1 collective-permute-start
  14.8 3.8 collective-permute-done
  18.7 2.8 collective-permute-start.1
  23.1 16.2 %collective-permute-done.4 = bf16[96,768]{1,0:T(8,128)(2,1)S(1)} collective-permute-done((bf16[96,768]{1,0:T(8,128)(2,1)S(1)}, bf16[96,768]{1,0:T(8,128)(2,1)S(1)}, u32[]{:S(2)}, u32[]{:S(2)}) %collective-permute-start.4) | collective-permute-done | bytes 147488 | tf_op jit(solution)/shard_map/ppermute | solution.py:535
  51.7 3.3 prepare.1
  56.1 20.5 %collective-permute-done.5 = bf16[2,96,768]{2,1,0:T(8,128)(2,1)} collective-permute-done((bf16[2,96,768]{2,1,0:T(8,128)(2,1)}, bf16[2,96,768]{2,1,0:T(8,128)(2,1)}, u32[]{:S(2)}, u32[]{:S(2)}) %collective-permute-start.5) | collective-permute-done | bytes 294944 | tf_op jit(solution)/shard_map/ppermute | solution.py:535
  82.8 9.7 %collective-permute-done.12 = bf16[2,96,768]{2,1,0:T(8,128)(2,1)S(1)} collective-permute-done((bf16[2,96,768]{2,1,0:T(8,128)(2,1)S(1)}, bf16[2,96,768]{2,1,0:T(8,128)(2,1)S(1)}, u32[]{:S(2)}, u32[]{:S(2)}) %collective-permute-start.12) | collective-permute-done | bytes 294944 | tf_op jit(solution)/shard_map/ppermute | solution.py:535
  93.6 10.0 %collective-permute-done.6 = bf16[2,96,768]{2,1,0:T(8,128)(2,1)S(1)} collective-permute-done((bf16[2,96,768]{2,1,0:T(8,128)(2,1)S(1)}, bf16[2,96,768]{2,1,0:T(8,128)(2,1)S(1)}, u32[]{:S(2)}, u32[]{:S(2)}) %collective-permute-start.6) | collective-permute-done | bytes 294944 | tf_op jit(solution)/shard_map/ppermute | solution.py:531
  110.6 28.0 %collective-permute-done.13 = bf16[2,96,768]{2,1,0:T(8,128)(2,1)S(1)} collective-permute-done((bf16[2,96,768]{2,1,0:T(8,128)(2,1)S(1)}, bf16[2,96,768]{2,1,0:T(8,128)(2,1)S(1)}, u32[]{:S(2)}, u32[]{:S(2)}) %collective-permute-start.13) | collective-permute-done | bytes 294944 | tf_op jit(solution)/shard_map/ppermute | solution.py:531
  146.9 3.1 collective-permute-done.19
  152.2 8.4 %attend.2 = (bf16[208,2304]{1,0:T(8,128)(2,1)}, f32[16,208]{1,0:T(8,128)}, bf16[4,208,256]{2,1,0:T(8,128)(2,1)}, f32[208,768]{1,0:T(8,128)}, bf16[208,768]{1,0:T(8,128)(2,1)}) custom-call(s32[4]{0:T(128)} %pad_add_fusion.info_ref, f32[208,768]{1,0:T(8,128)} %get-tuple-element.110.x_ref, f32[4,768]{1,0:T(4,128)} %get-tuple-element.111.gain_ref, ...), custom_call_target="tpu_custom_call" | custom-call | flops 10000000 | bytes 100000 | tf_op jit(solution)/shard_map/attend/pallas_call | solution.py:391
  160.6 9.0 %feed.2 = (bf16[4,208,768]{2,1,0:T(8,128)(2,1)}, f32[4,208,768]{2,1,0:T(8,128)}, f32[208,768]{1,0:T(8,128)}) custom-call(s32[4]{0:T(128)} %pad_add_fusion.info_ref, f32[208,768]{1,0:T(8,128)} %get-tuple-element.117.h1_ref, bf16[208,768]{1,0:T(8,128)(2,1)} %get-tuple-element.118.a2_ref, f32[4,768]{1,0:T(4,128)} %get-tuple-element.112.bias_ref, ...), custom_call_target="tpu_custom_call" | custom-call | flops 10000000 | bytes 100000 | tf_op jit(solution)/shard_map/feed/pallas_call | solution.py:411
  169.7 7.9 %attend.3 = (bf16[208,2304]{1,0:T(8,128)(2,1)}, f32[16,208]{1,0:T(8,128)}, bf16[4,208,256]{2,1,0:T(8,128)(2,1)}, f32[208,768]{1,0:T(8,128)}, bf16[208,768]{1,0:T(8,128)(2,1)}) custom-call(s32[4]{0:T(128)} %pad_add_fusion.info_ref, f32[208,768]{1,0:T(8,128)} %get-tuple-element.128.x_ref, f32[4,768]{1,0:T(4,128)} %get-tuple-element.111.gain_ref, ...), custom_call_target="tpu_custom_call" | custom-call | flops 10000000 | bytes 100000 | tf_op jit(solution)/shard_map/attend/pallas_call | solution.py:391
  177.6 8.6 %feed.3 = (bf16[4,208,768]{2,1,0:T(8,128)(2,1)}, f32[4,208,768]{2,1,0:T(8,128)}, f32[208,768]{1,0:T(8,128)}) custom-call(s32[4]{0:T(128)} %pad_add_fusion.info_ref, f32[208,768]{1,0:T(8,128)} %get-tuple-element.129.h1_ref, bf16[208,768]{1,0:T(8,128)(2,1)} %get-tuple-element.130.a2_ref, f32[4,768]{1,0:T(4,128)} %get-tuple-element.112.bias_ref, ...), custom_call_target="tpu_custom_call" | custom-call | flops 10000000 | bytes 100000 | tf_op jit(solution)/shard_map/feed/pallas_call | solution.py:411
  186.2 12.9 %feed_back.2 = (bf16[4,4,96,1536]{3,2,1,0:T(8,128)(2,1)}, bf16[4,4,96,1536]{3,2,1,0:T(8,128)(2,1)}, f32[4,1,768]{2,1,0:T(1,128)}, f32[208,768]{1,0:T(8,128)}, f32[8,768]{1,0:T(8,128)}) custom-call(s32[4]{0:T(128)} %pad_add_fusion.info_ref, f32[208,768]{1,0:T(8,128)} %get-tuple-element.132.g_ref, f32[208,768]{1,0:T(8,128)} %get-tuple-element.129.h1_ref, ...), custom_call_target="tpu_custom_call" | custom-call | flops 10000000 | bytes 100000 | tf_op jit(solution)/shard_map/feed_back/pallas_call | solution.py:436
  199.6 7.7 %collective-permute-done.21 = bf16[4,4,96,1536]{3,2,1,0:T(8,128)(2,1)S(1)} collective-permute-done((bf16[4,4,96,1536]{3,2,1,0:T(8,128)(2,1)}, bf16[4,4,96,1536]{3,2,1,0:T(8,128)(2,1)S(1)}, u32[]{:S(2)}, u32[]{:S(2)}) %collective-permute-start.21) | collective-permute-done | bytes 4718624 | tf_op jit(solution)/shard_map/ppermute | solution.py:531
  207.4 4.0 fusion.13
  214.6 13.8 %attend_back.2 = (bf16[4,8,96,768]{3,2,1,0:T(8,128)(2,1)}, f32[208,768]{1,0:T(8,128)}, f32[8,768]{1,0:T(8,128)}) custom-call(s32[4]{0:T(128)} %pad_add_fusion.info_ref, f32[208,768]{1,0:T(8,128)} %get-tuple-element.135.dh1_ref, f32[208,768]{1,0:T(8,128)} %get-tuple-element.128.x_ref, f32[4,768]{1,0:T(4,128)} %get-tuple-element.111.gain_ref, ...), custom_call_target="tpu_custom_call" | custom-call | flops 10000000 | bytes 100000 | tf_op jit(solution)/shard_map/attend_back/pallas_call | solution.py:457
  229.4 12.7 %feed_back.3 = (bf16[4,4,96,1536]{3,2,1,0:T(8,128)(2,1)}, bf16[4,4,96,1536]{3,2,1,0:T(8,128)(2,1)}, f32[4,1,768]{2,1,0:T(1,128)}, f32[208,768]{1,0:T(8,128)}, f32[8,768]{1,0:T(8,128)}) custom-call(s32[4]{0:T(128)} %pad_add_fusion.info_ref, f32[208,768]{1,0:T(8,128)} %get-tuple-element.141.g_ref, f32[208,768]{1,0:T(8,128)} %get-tuple-element.117.h1_ref, ...), custom_call_target="tpu_custom_call" | custom-call | flops 10000000 | bytes 100000 | tf_op jit(solution)/shard_map/feed_back/pallas_call | solution.py:436
  247.7 13.7 %attend_back.3 = (bf16[4,4,96,768]{3,2,1,0:T(8,128)(2,1)}, bf16[4,4,96,768]{3,2,1,0:T(8,128)(2,1)}, f32[1,197,768]{2,1,0:T(8,128)}, f32[8,768]{1,0:T(8,128)}) custom-call(s32[4]{0:T(128)} %pad_add_fusion.info_ref, f32[208,768]{1,0:T(8,128)} %get-tuple-element.146.dh1_ref, f32[208,768]{1,0:T(8,128)} %get-tuple-element.110.x_ref, ...), custom_call_target="tpu_custom_call" | custom-call | flops 10000000 | bytes 100000 | tf_op jit(solution)/shard_map/attend_back/pallas_call | solution.py:457
  261.5 12.9 %collective-permute-done.39 = bf16[4,96,1536]{2,1,0:T(8,128)(2,1)S(1)} collective-permute-done((bf16[4,96,1536]{2,1,0:T(8,128)(2,1)}, bf16[4,96,1536]{2,1,0:T(8,128)(2,1)S(1)}, u32[]{:S(2)}, u32[]{:S(2)}) %collective-permute-start.39) | collective-permute-done | bytes 1179680 | tf_op jit(solution)/shard_map/ppermute | solution.py:531
  282.8 7.1 %collective-permute-start.42 = (f32[16,768]{1,0:T(8,128)S(1)}, f32[16,768]{1,0:T(8,128)S(1)}, u32[]{:S(2)}, u32[]{:S(2)}) collective-permute-start(f32[16,768]{1,0:T(8,128)S(1)} %constant_dynamic-update-slice_fusion.15), channel_id=1, source_target_pairs={{0,1},{1,0},{2,3},{3,2},{4,5},{5,4},{6,7},{7,6},{8,9},{9,8},{10,11... | collective-permute-start | bytes 147464 | tf_op jit(solution)/shard_map/ppermute | solution.py:535
  292.2 13.6 %collective-permute-start.43 = (f32[16,768]{1,0:T(8,128)S(1)}, f32[16,768]{1,0:T(8,128)S(1)}, u32[]{:S(2)}, u32[]{:S(2)}) collective-permute-start(f32[16,768]{1,0:T(8,128)S(1)} %add.257), channel_id=1, source_target_pairs={{0,2},{1,3},{2,0},{3,1},{4,6},{5,7},{6,4},{7,5},{8,10},{9,11},{10,... | collective-permute-start | bytes 147464 | tf_op jit(solution)/shard_map/ppermute | solution.py:535
  305.8 5.4 %collective-permute-done.43 = f32[16,768]{1,0:T(8,128)S(1)} collective-permute-done((f32[16,768]{1,0:T(8,128)S(1)}, f32[16,768]{1,0:T(8,128)S(1)}, u32[]{:S(2)}, u32[]{:S(2)}) %collective-permute-start.43) | collective-permute-done | bytes 49184 | tf_op jit(solution)/shard_map/ppermute | solution.py:535
  335.4 16.2 %collective-permute-done.35 = bf16[4,96,1536]{2,1,0:T(8,128)(2,1)} collective-permute-done((bf16[4,96,1536]{2,1,0:T(8,128)(2,1)}, bf16[4,96,1536]{2,1,0:T(8,128)(2,1)}, u32[]{:S(2)}, u32[]{:S(2)}) %collective-permute-start.35) | collective-permute-done | bytes 1179680 | tf_op jit(solution)/shard_map/ppermute | solution.py:531
  351.6 7.2 %collective-permute-done.28 = bf16[2,96,768]{2,1,0:T(8,128)(2,1)S(1)} collective-permute-done((bf16[2,96,768]{2,1,0:T(8,128)(2,1)S(1)}, bf16[2,96,768]{2,1,0:T(8,128)(2,1)S(1)}, u32[]{:S(2)}, u32[]{:S(2)}) %collective-permute-start.28) | collective-permute-done | bytes 294944 | tf_op jit(solution)/shard_map/ppermute | solution.py:531
  361.9 3.0 fusion.1
  366.6 7.9 %collective-permute-done.31 = bf16[4,96,768]{2,1,0:T(8,128)(2,1)S(1)} collective-permute-done((bf16[4,96,768]{2,1,0:T(8,128)(2,1)S(1)}, bf16[4,96,768]{2,1,0:T(8,128)(2,1)S(1)}, u32[]{:S(2)}, u32[]{:S(2)}) %collective-permute-start.31) | collective-permute-done | bytes 589856 | tf_op jit(solution)/shard_map/ppermute | solution.py:531
  378.5 23.4 %collective-permute-done.36 = bf16[2,96,1536]{2,1,0:T(8,128)(2,1)} collective-permute-done((bf16[2,96,1536]{2,1,0:T(8,128)(2,1)}, bf16[2,96,1536]{2,1,0:T(8,128)(2,1)}, u32[]{:S(2)}, u32[]{:S(2)}) %collective-permute-start.36) | collective-permute-done | bytes 589856 | tf_op jit(solution)/shard_map/ppermute | solution.py:535
  407.4 5.8 %collective-permute-done.37 = bf16[96,1536]{1,0:T(8,128)(2,1)S(1)} collective-permute-done((bf16[96,1536]{1,0:T(8,128)(2,1)S(1)}, bf16[96,1536]{1,0:T(8,128)(2,1)S(1)}, u32[]{:S(2)}, u32[]{:S(2)}) %collective-permute-start.37) | collective-permute-done | bytes 294944 | tf_op jit(solution)/shard_map/ppermute | solution.py:535
  414.1 5.1 %update.3 = (f32[2,96,768]{2,1,0:T(8,128)}, f32[2,96,768]{2,1,0:T(8,128)}, f32[2,96,768]{2,1,0:T(8,128)}, f32[2,96,768]{2,1,0:T(8,128)}, f32[2,96,768]{2,1,0:T(8...) custom-call(f32[96,1536]{1,0:T(8,128)} %fusion.16.refs_0_, ...), custom_call_target="tpu_custom_call" | custom-call | flops 10000000 | bytes 100000 | tf_op jit(solution)/shard_map/update/pallas_call | solution.py:558
  420.0 3.7 update.2
  (223 shorter events, 105.0 us)
Async XLA Ops:
  7.2 162.4 %all-gather.2.cloned.1.call-start = ((), (), s32[]{:S(2)}) async-start(), calls=%async_computation.1 | async-start | bytes 14598144 | tf_op jit(solution)/shard_map/all_gather | solution.py:603
  11.6 363.9 %reduce-scatter.2.cloned.1.call-start = ((), (), s32[]{:S(2)}) async-start(), calls=%async_computation.2 | async-start | bytes 4866048 | tf_op jit(solution)/shard_map/reduce_scatter | solution.py:608
  18.7 25.0 %collective-permute-start.1 = (bf16[2,96,768]{2,1,0:T(8,128)(2,1)S(1)}, bf16[2,96,768]{2,1,0:T(8,128)(2,1)S(1)}, u32[]{:S(2)}, u32[]{:S(2)}) collective-permute-start(bf16[2,96,768]{2,1,0:T(8,128)(2,1)S(1)} %pad_maximum_fusion.9), channel_id=1, source_target_pairs={{0,2},{1,3},{2,0},{3,1},{4,6},{5,7},{6,4},{7,5},{8,10},{9,11},{10,... | collective-permute-start | bytes 884744 | tf_op jit(solution)/shard_map/ppermute | solution.py:535
  21.5 17.8 %collective-permute-start.4 = (bf16[96,768]{1,0:T(8,128)(2,1)S(1)}, bf16[96,768]{1,0:T(8,128)(2,1)S(1)}, u32[]{:S(2)}, u32[]{:S(2)}) collective-permute-start(bf16[96,768]{1,0:T(8,128)(2,1)S(1)} %get-tuple-element.113), channel_id=1, source_target_pairs={{0,1},{1,0},{2,3},{3,2},{4,5},{5,4},{6,7},{7,6},{8,9},{9,8},{10,11... | collective-permute-start | bytes 442376 | tf_op jit(solution)/shard_map/ppermute | solution.py:535
  43.8 33.8 %collective-permute-start.2 = (bf16[4,96,768]{2,1,0:T(8,128)(2,1)S(1)}, bf16[4,96,768]{2,1,0:T(8,128)(2,1)S(1)}, u32[]{:S(2)}, u32[]{:S(2)}) collective-permute-start(bf16[4,96,768]{2,1,0:T(8,128)(2,1)S(1)} %pad_maximum_fusion.4), channel_id=1, source_target_pairs={{0,8},{4,12},{8,0},{12,4},{16,24},{20,28},{24,16},{28,20},{1,9},{5... | collective-permute-start | bytes 1769480 | tf_op jit(solution)/shard_map/ppermute | solution.py:531
  45.9 33.4 %collective-permute-start.3 = (bf16[4,96,768]{2,1,0:T(8,128)(2,1)S(1)}, bf16[4,96,768]{2,1,0:T(8,128)(2,1)S(1)}, u32[]{:S(2)}, u32[]{:S(2)}) collective-permute-start(bf16[4,96,768]{2,1,0:T(8,128)(2,1)S(1)} %pad_maximum_fusion.4), channel_id=1, source_target_pairs={{0,16},{4,20},{8,24},{12,28},{16,0},{20,4},{24,8},{28,12},{1,17},{... | collective-permute-start | bytes 1769480 | tf_op jit(solution)/shard_map/ppermute | solution.py:531
  47.5 29.1 %collective-permute-start.5 = (bf16[2,96,768]{2,1,0:T(8,128)(2,1)}, bf16[2,96,768]{2,1,0:T(8,128)(2,1)}, u32[]{:S(2)}, u32[]{:S(2)}) collective-permute-start(bf16[2,96,768]{2,1,0:T(8,128)(2,1)} %pad_maximum_fusion.10), channel_id=1, source_target_pairs={{0,2},{1,3},{2,0},{3,1},{4,6},{5,7},{6,4},{7,5},{8,10},{9,11},{10,... | collective-permute-start | bytes 884744 | tf_op jit(solution)/shard_map/ppermute | solution.py:535
  77.6 28.3 %collective-permute-start.10 = (bf16[4,96,768]{2,1,0:T(8,128)(2,1)S(1)}, bf16[4,96,768]{2,1,0:T(8,128)(2,1)S(1)}, u32[]{:S(2)}, u32[]{:S(2)}) collective-permute-start(bf16[4,96,768]{2,1,0:T(8,128)(2,1)S(1)} %pad_maximum_fusion.5), channel_id=1, source_target_pairs={{0,16},{4,20},{8,24},{12,28},{16,0},{20,4},{24,8},{28,12},{1,17},{... | collective-permute-start | bytes 1769480 | tf_op jit(solution)/shard_map/ppermute | solution.py:531
  78.2 25.4 %collective-permute-start.9 = (bf16[4,96,768]{2,1,0:T(8,128)(2,1)S(1)}, bf16[4,96,768]{2,1,0:T(8,128)(2,1)S(1)}, u32[]{:S(2)}, u32[]{:S(2)}) collective-permute-start(bf16[4,96,768]{2,1,0:T(8,128)(2,1)S(1)} %pad_maximum_fusion.5), channel_id=1, source_target_pairs={{0,8},{4,12},{8,0},{12,4},{16,24},{20,28},{24,16},{28,20},{1,9},{5... | collective-permute-start | bytes 1769480 | tf_op jit(solution)/shard_map/ppermute | solution.py:531
  79.4 24.2 %collective-permute-start.6 = (bf16[2,96,768]{2,1,0:T(8,128)(2,1)S(1)}, bf16[2,96,768]{2,1,0:T(8,128)(2,1)S(1)}, u32[]{:S(2)}, u32[]{:S(2)}) collective-permute-start(bf16[2,96,768]{2,1,0:T(8,128)(2,1)S(1)} %slice.230), channel_id=1, source_target_pairs={{0,8},{4,12},{8,0},{12,4},{16,24},{20,28},{24,16},{28,20},{1,9},{5... | collective-permute-start | bytes 884744 | tf_op jit(solution)/shard_map/ppermute | solution.py:531
  81.2 24.7 %collective-permute-start.7 = (bf16[2,96,768]{2,1,0:T(8,128)(2,1)S(1)}, bf16[2,96,768]{2,1,0:T(8,128)(2,1)S(1)}, u32[]{:S(2)}, u32[]{:S(2)}) collective-permute-start(bf16[2,96,768]{2,1,0:T(8,128)(2,1)S(1)} %slice.231), channel_id=1, source_target_pairs={{0,16},{4,20},{8,24},{12,28},{16,0},{20,4},{24,8},{28,12},{1,17},{... | collective-permute-start | bytes 884744 | tf_op jit(solution)/shard_map/ppermute | solution.py:531
  103.6 35.8 %collective-permute-start.17 = (bf16[4,96,768]{2,1,0:T(8,128)(2,1)S(1)}, bf16[4,96,768]{2,1,0:T(8,128)(2,1)S(1)}, u32[]{:S(2)}, u32[]{:S(2)}) collective-permute-start(bf16[4,96,768]{2,1,0:T(8,128)(2,1)S(1)} %pad_maximum_fusion.6), channel_id=1, source_target_pairs={{0,16},{4,20},{8,24},{12,28},{16,0},{20,4},{24,8},{28,12},{1,17},{... | collective-permute-start | bytes 1769480 | tf_op jit(solution)/shard_map/ppermute | solution.py:531
  105.3 34.0 %collective-permute-start.16 = (bf16[4,96,768]{2,1,0:T(8,128)(2,1)S(1)}, bf16[4,96,768]{2,1,0:T(8,128)(2,1)S(1)}, u32[]{:S(2)}, u32[]{:S(2)}) collective-permute-start(bf16[4,96,768]{2,1,0:T(8,128)(2,1)S(1)} %pad_maximum_fusion.6), channel_id=1, source_target_pairs={{0,8},{4,12},{8,0},{12,4},{16,24},{20,28},{24,16},{28,20},{1,9},{5... | collective-permute-start | bytes 1769480 | tf_op jit(solution)/shard_map/ppermute | solution.py:531
  105.9 44.9 %collective-permute-start.8 = (bf16[4,4,96,768]{3,2,1,0:T(8,128)(2,1)S(1)}, bf16[4,4,96,768]{3,2,1,0:T(8,128)(2,1)S(1)}, u32[]{:S(2)}, u32[]{:S(2)}) collective-permute-start(bf16[4,4,96,768]{3,2,1,0:T(8,128)(2,1)S(1)} %bitcast.131), channel_id=1, source_target_pairs={{0,4},{4,0},{8,12},{12,8},{16,20},{20,16},{24,28},{28,24},{1,5},{5... | collective-permute-start | bytes 7077896 | tf_op jit(solution)/shard_map/ppermute | solution.py:531
  106.0 32.6 %collective-permute-start.13 = (bf16[2,96,768]{2,1,0:T(8,128)(2,1)S(1)}, bf16[2,96,768]{2,1,0:T(8,128)(2,1)S(1)}, u32[]{:S(2)}, u32[]{:S(2)}) collective-permute-start(bf16[2,96,768]{2,1,0:T(8,128)(2,1)S(1)} %slice.233), channel_id=1, source_target_pairs={{0,8},{4,12},{8,0},{12,4},{16,24},{20,28},{24,16},{28,20},{1,9},{5... | collective-permute-start | bytes 884744 | tf_op jit(solution)/shard_map/ppermute | solution.py:531
  108.5 31.3 %collective-permute-start.14 = (bf16[2,96,768]{2,1,0:T(8,128)(2,1)S(1)}, bf16[2,96,768]{2,1,0:T(8,128)(2,1)S(1)}, u32[]{:S(2)}, u32[]{:S(2)}) collective-permute-start(bf16[2,96,768]{2,1,0:T(8,128)(2,1)S(1)} %slice.234), channel_id=1, source_target_pairs={{0,16},{4,20},{8,24},{12,28},{16,0},{20,4},{24,8},{28,12},{1,17},{... | collective-permute-start | bytes 884744 | tf_op jit(solution)/shard_map/ppermute | solution.py:531
  140.5 20.1 %collective-permute-start.15 = (bf16[4,4,96,768]{3,2,1,0:T(8,128)(2,1)}, bf16[4,4,96,768]{3,2,1,0:T(8,128)(2,1)}, u32[]{:S(2)}, u32[]{:S(2)}) collective-permute-start(bf16[4,4,96,768]{3,2,1,0:T(8,128)(2,1)} %bitcast.15.rest_0_), channel_id=1, source_target_pairs={{0,4},{4,0},{8,12},{12,8},{16,20},{20,16},{24,28},{28,24},{1,5},{5... | collective-permute-start | bytes 7077896 | tf_op jit(solution)/shard_map/ppermute | solution.py:531
  242.1 34.9 %collective-permute-start.24 = (bf16[4,4,96,1536]{3,2,1,0:T(8,128)(2,1)}, bf16[4,4,96,1536]{3,2,1,0:T(8,128)(2,1)}, u32[]{:S(2)}, u32[]{:S(2)}) collective-permute-start(bf16[4,4,96,1536]{3,2,1,0:T(8,128)(2,1)} %get-tuple-element.155), channel_id=1, source_target_pairs={{0,4},{4,0},{8,12},{12,8},{16,20},{20,16},{24,28},{28,24},{1,5},{5... | collective-permute-start | bytes 14155784 | tf_op jit(solution)/shard_map/ppermute | solution.py:531
  245.9 28.6 %collective-permute-start.39 = (bf16[4,96,1536]{2,1,0:T(8,128)(2,1)}, bf16[4,96,1536]{2,1,0:T(8,128)(2,1)S(1)}, u32[]{:S(2)}, u32[]{:S(2)}) collective-permute-start(bf16[4,96,1536]{2,1,0:T(8,128)(2,1)} %pad_maximum_fusion.3), channel_id=1, source_target_pairs={{0,16},{4,20},{8,24},{12,28},{16,0},{20,4},{24,8},{28,12},{1,17},{... | collective-permute-start | bytes 3538952 | tf_op jit(solution)/shard_map/ppermute | solution.py:531
  246.4 28.1 %collective-permute-start.38 = (bf16[4,96,1536]{2,1,0:T(8,128)(2,1)S(1)}, bf16[4,96,1536]{2,1,0:T(8,128)(2,1)S(1)}, u32[]{:S(2)}, u32[]{:S(2)}) collective-permute-start(bf16[4,96,1536]{2,1,0:T(8,128)(2,1)S(1)} %pad_maximum_fusion.2), channel_id=1, source_target_pairs={{0,8},{4,12},{8,0},{12,4},{16,24},{20,28},{24,16},{28,20},{1,9},{5... | collective-permute-start | bytes 3538952 | tf_op jit(solution)/shard_map/ppermute | solution.py:531
  276.9 37.3 %collective-permute-start.40 = (bf16[2,96,1536]{2,1,0:T(8,128)(2,1)S(1)}, bf16[2,96,1536]{2,1,0:T(8,128)(2,1)S(1)}, u32[]{:S(2)}, u32[]{:S(2)}) collective-permute-start(bf16[2,96,1536]{2,1,0:T(8,128)(2,1)S(1)} %slice.403), channel_id=1, source_target_pairs={{0,2},{1,3},{2,0},{3,1},{4,6},{5,7},{6,4},{7,5},{8,10},{9,11},{10,... | collective-permute-start | bytes 1769480 | tf_op jit(solution)/shard_map/ppermute | solution.py:535
  279.9 34.4 %collective-permute-start.26 = (bf16[2,96,1536]{2,1,0:T(8,128)(2,1)S(1)}, bf16[2,96,1536]{2,1,0:T(8,128)(2,1)S(1)}, u32[]{:S(2)}, u32[]{:S(2)}) collective-permute-start(bf16[2,96,1536]{2,1,0:T(8,128)(2,1)S(1)} %get-tuple-element.160), channel_id=1, source_target_pairs={{0,8},{4,12},{8,0},{12,4},{16,24},{20,28},{24,16},{28,20},{1,9},{5... | collective-permute-start | bytes 1769480 | tf_op jit(solution)/shard_map/ppermute | solution.py:531
  281.2 33.0 %collective-permute-start.27 = (bf16[2,96,1536]{2,1,0:T(8,128)(2,1)S(1)}, bf16[2,96,1536]{2,1,0:T(8,128)(2,1)S(1)}, u32[]{:S(2)}, u32[]{:S(2)}) collective-permute-start(bf16[2,96,1536]{2,1,0:T(8,128)(2,1)S(1)} %get-tuple-element.161), channel_id=1, source_target_pairs={{0,16},{4,20},{8,24},{12,28},{16,0},{20,4},{24,8},{28,12},{1,17},{... | collective-permute-start | bytes 1769480 | tf_op jit(solution)/shard_map/ppermute | solution.py:531
  282.8 47.0 %collective-permute-start.25 = (bf16[4,4,96,768]{3,2,1,0:T(8,128)(2,1)}, bf16[4,4,96,768]{3,2,1,0:T(8,128)(2,1)}, u32[]{:S(2)}, u32[]{:S(2)}) collective-permute-start(bf16[4,4,96,768]{3,2,1,0:T(8,128)(2,1)} %get-tuple-element.156), channel_id=1, source_target_pairs={{0,4},{4,0},{8,12},{12,8},{16,20},{20,16},{24,28},{28,24},{1,5},{5... | collective-permute-start | bytes 7077896 | tf_op jit(solution)/shard_map/ppermute | solution.py:531
  292.2 19.0 %collective-permute-start.43 = (f32[16,768]{1,0:T(8,128)S(1)}, f32[16,768]{1,0:T(8,128)S(1)}, u32[]{:S(2)}, u32[]{:S(2)}) collective-permute-start(f32[16,768]{1,0:T(8,128)S(1)} %add.257), channel_id=1, source_target_pairs={{0,2},{1,3},{2,0},{3,1},{4,6},{5,7},{6,4},{7,5},{8,10},{9,11},{10,... | collective-permute-start | bytes 147464 | tf_op jit(solution)/shard_map/ppermute | solution.py:535
  318.2 33.4 %collective-permute-start.35 = (bf16[4,96,1536]{2,1,0:T(8,128)(2,1)}, bf16[4,96,1536]{2,1,0:T(8,128)(2,1)}, u32[]{:S(2)}, u32[]{:S(2)}) collective-permute-start(bf16[4,96,1536]{2,1,0:T(8,128)(2,1)} %pad_maximum_fusion.1), channel_id=1, source_target_pairs={{0,16},{4,20},{8,24},{12,28},{16,0},{20,4},{24,8},{28,12},{1,17},{... | collective-permute-start | bytes 3538952 | tf_op jit(solution)/shard_map/ppermute | solution.py:531
  318.7 32.8 %collective-permute-start.34 = (bf16[4,96,1536]{2,1,0:T(8,128)(2,1)}, bf16[4,96,1536]{2,1,0:T(8,128)(2,1)}, u32[]{:S(2)}, u32[]{:S(2)}) collective-permute-start(bf16[4,96,1536]{2,1,0:T(8,128)(2,1)} %pad_maximum_fusion), channel_id=1, source_target_pairs={{0,8},{4,12},{8,0},{12,4},{16,24},{20,28},{24,16},{28,20},{1,9},{5... | collective-permute-start | bytes 3538952 | tf_op jit(solution)/shard_map/ppermute | solution.py:531
  329.6 37.1 %collective-permute-start.46 = (f32[16,768]{1,0:T(8,128)S(1)}, f32[16,768]{1,0:T(8,128)S(1)}, u32[]{:S(2)}, u32[]{:S(2)}) collective-permute-start(f32[16,768]{1,0:T(8,128)S(1)} %add.260), channel_id=1, source_target_pairs={{0,16},{4,20},{8,24},{12,28},{16,0},{20,4},{24,8},{28,12},{1,17},{... | collective-permute-start | bytes 147464 | tf_op jit(solution)/shard_map/ppermute | solution.py:531
  331.3 27.5 %collective-permute-start.28 = (bf16[2,96,768]{2,1,0:T(8,128)(2,1)S(1)}, bf16[2,96,768]{2,1,0:T(8,128)(2,1)S(1)}, u32[]{:S(2)}, u32[]{:S(2)}) collective-permute-start(bf16[2,96,768]{2,1,0:T(8,128)(2,1)S(1)} %get-tuple-element.163), channel_id=1, source_target_pairs={{0,16},{4,20},{8,24},{12,28},{16,0},{20,4},{24,8},{28,12},{1,17},{... | collective-permute-start | bytes 884744 | tf_op jit(solution)/shard_map/ppermute | solution.py:531
  333.2 25.6 %collective-permute-start.30 = (bf16[2,96,768]{2,1,0:T(8,128)(2,1)S(1)}, bf16[2,96,768]{2,1,0:T(8,128)(2,1)S(1)}, u32[]{:S(2)}, u32[]{:S(2)}) collective-permute-start(bf16[2,96,768]{2,1,0:T(8,128)(2,1)S(1)} %get-tuple-element.164), channel_id=1, source_target_pairs={{0,8},{4,12},{8,0},{12,4},{16,24},{20,28},{24,16},{28,20},{1,9},{5... | collective-permute-start | bytes 884744 | tf_op jit(solution)/shard_map/ppermute | solution.py:531
  365.8 36.2 %collective-permute-start.36 = (bf16[2,96,1536]{2,1,0:T(8,128)(2,1)}, bf16[2,96,1536]{2,1,0:T(8,128)(2,1)}, u32[]{:S(2)}, u32[]{:S(2)}) collective-permute-start(bf16[2,96,1536]{2,1,0:T(8,128)(2,1)} %slice.404), channel_id=1, source_target_pairs={{0,2},{1,3},{2,0},{3,1},{4,6},{5,7},{6,4},{7,5},{8,10},{9,11},{10,... | collective-permute-start | bytes 1769480 | tf_op jit(solution)/shard_map/ppermute | solution.py:535
  378.0 27.6 %collective-permute-start.32 = (bf16[2,96,768]{2,1,0:T(8,128)(2,1)S(1)}, bf16[2,96,768]{2,1,0:T(8,128)(2,1)S(1)}, u32[]{:S(2)}, u32[]{:S(2)}) collective-permute-start(bf16[2,96,768]{2,1,0:T(8,128)(2,1)S(1)} %slice.405), channel_id=1, source_target_pairs={{0,2},{1,3},{2,0},{3,1},{4,6},{5,7},{6,4},{7,5},{8,10},{9,11},{10,... | collective-permute-start | bytes 884744 | tf_op jit(solution)/shard_map/ppermute | solution.py:535
  (46 other events, 731.3 us)
Sparse Core Ops, SparseCore 0:
  11.7 145.8 all-gather.1
  247.8 119.1 reduce-scatter.1

commit v6 on v5

--- a/solution.py
+++ b/solution.py
@@ -737,7 +737,7 @@
         att_zero.send(((), ())),
     )
     layer_out = finish(seq, info, counts, hidden, [upstream])
-    stages = [(), (), (), plane_one, plane_last]
+    stages = [plane_zero, plane_zero, diag_last, plane_last, plane_last]
     small = plan.total(jnp.concatenate(smalls, axis=0), stages).reshape(LAYERS, 8, D)
     ffn, att = [[done[name, level] for level in range(LAYERS)] for name in ("ffn", "att")]
 

time: 438 us -> 435 us (level)
  the two profiles are of different devices: /device:TPU:0 before, /device:TPU:29 now
where the time goes in v6:
time: 435 us; the launch traced here: 428 us
  waiting for transfers between devices  209 us (48%)
  Pallas kernels  102 us (23%)
  starting transfers between devices  42.1 us (10%)
  other arithmetic  37.8 us (9%)
  local copies, waits for them, and re-layouts  21.8 us (5%)
  between operations  15.1 us (3%)
    ppermute x14, waiting for transfers between devices, flip_col(): return lax.ppermute(x, 'col', [(i, i ^ mask) for i in range(4)])  108 us
    ppermute x33, waiting for transfers between devices, flip_row(): return lax.ppermute(x, 'row', [(i, i ^ mask) for i in range(8)])  88.8 us
    ppermute x33, starting transfers between devices, flip_row(): return lax.ppermute(x, 'row', [(i, i ^ mask) for i in range(8)])  35.4 us
    pallas_call x2, Pallas kernels, attend_back(): pl.pallas_call(functools.partial(attend_back_kernel, seq, level, whole_or...  27.4 us
    pallas_call x2, Pallas kernels, feed_back(): pl.pallas_call(functools.partial(feed_back_kernel, level, len(pieces), le...  25.6 us
    pallas_call x2, Pallas kernels, feed(): pl.pallas_call(functools.partial(feed_kernel, level, len(pieces)), grid=(...  17.5 us
    unnamed x82, local copies, waits for them, and re-layouts  16.3 us
    pallas_call x2, Pallas kernels, attend(): pl.pallas_call(functools.partial(attend_kernel, seq, level, len(pieces)),...  16.3 us
  transfers between devices with their start and end apart: 49, of which 22 were waited for; matrix products, arithmetic and copies ran while one was open for 11% of the time, Pallas kernels for 13%

profile of v6, /device:TPU:29, one launch (start us, length us, event | category | flops | bytes accessed | tf_op | source)
XLA Modules:
  0.0 427.6 jit_solution(10422445966720285040)
XLA Ops:
  12.0 4.5 %collective-permute-done = bf16[96,768]{1,0:T(8,128)(2,1)S(1)} collective-permute-done((bf16[96,768]{1,0:T(8,128)(2,1)S(1)}, bf16[96,768]{1,0:T(8,128)(2,1)S(1)}, u32[]{:S(2)}, u32[]{:S(2)}) %collective-permute-start) | collective-permute-done | bytes 147488 | tf_op jit(solution)/shard_map/ppermute | solution.py:535
  16.9 9.7 %collective-permute-done.4 = bf16[96,768]{1,0:T(8,128)(2,1)S(1)} collective-permute-done((bf16[96,768]{1,0:T(8,128)(2,1)S(1)}, bf16[96,768]{1,0:T(8,128)(2,1)S(1)}, u32[]{:S(2)}, u32[]{:S(2)}) %collective-permute-start.4) | collective-permute-done | bytes 147488 | tf_op jit(solution)/shard_map/ppermute | solution.py:535
  28.8 13.3 %collective-permute-done.1 = bf16[2,96,768]{2,1,0:T(8,128)(2,1)S(1)} collective-permute-done((bf16[2,96,768]{2,1,0:T(8,128)(2,1)S(1)}, bf16[2,96,768]{2,1,0:T(8,128)(2,1)S(1)}, u32[]{:S(2)}, u32[]{:S(2)}) %collective-permute-start.1) | collective-permute-done | bytes 294944 | tf_op jit(solution)/shard_map/ppermute | solution.py:535
  48.7 3.4 prepare.1
  53.1 19.2 %collective-permute-done.5 = bf16[2,96,768]{2,1,0:T(8,128)(2,1)} collective-permute-done((bf16[2,96,768]{2,1,0:T(8,128)(2,1)}, bf16[2,96,768]{2,1,0:T(8,128)(2,1)}, u32[]{:S(2)}, u32[]{:S(2)}) %collective-permute-start.5) | collective-permute-done | bytes 294944 | tf_op jit(solution)/shard_map/ppermute | solution.py:535
  77.4 10.8 %collective-permute-done.12 = bf16[2,96,768]{2,1,0:T(8,128)(2,1)S(1)} collective-permute-done((bf16[2,96,768]{2,1,0:T(8,128)(2,1)S(1)}, bf16[2,96,768]{2,1,0:T(8,128)(2,1)S(1)}, u32[]{:S(2)}, u32[]{:S(2)}) %collective-permute-start.12) | collective-permute-done | bytes 294944 | tf_op jit(solution)/shard_map/ppermute | solution.py:535
  89.2 7.7 %collective-permute-done.6 = bf16[2,96,768]{2,1,0:T(8,128)(2,1)S(1)} collective-permute-done((bf16[2,96,768]{2,1,0:T(8,128)(2,1)S(1)}, bf16[2,96,768]{2,1,0:T(8,128)(2,1)S(1)}, u32[]{:S(2)}, u32[]{:S(2)}) %collective-permute-start.6) | collective-permute-done | bytes 294944 | tf_op jit(solution)/shard_map/ppermute | solution.py:531
  98.9 6.1 %collective-permute-start.8 = (bf16[4,4,96,768]{3,2,1,0:T(8,128)(2,1)S(1)}, bf16[4,4,96,768]{3,2,1,0:T(8,128)(2,1)S(1)}, u32[]{:S(2)}, u32[]{:S(2)}) collective-permute-start(bf16[4,4,96,768]{3,2,1,0:T(8,128)(2,1)S(1)} %bitcast.131), channel_id=1, source_target_pairs={{0,4},{4,0},{8,12},{12,8},{16,20},{20,16},{24,28},{28,24},{1,5},{5... | collective-permute-start | bytes 7077896 | tf_op jit(solution)/shard_map/ppermute | solution.py:531
  109.5 27.2 %collective-permute-done.13 = bf16[2,96,768]{2,1,0:T(8,128)(2,1)S(1)} collective-permute-done((bf16[2,96,768]{2,1,0:T(8,128)(2,1)S(1)}, bf16[2,96,768]{2,1,0:T(8,128)(2,1)S(1)}, u32[]{:S(2)}, u32[]{:S(2)}) %collective-permute-start.13) | collective-permute-done | bytes 294944 | tf_op jit(solution)/shard_map/ppermute | solution.py:531
  139.9 4.1 collective-permute-start.15
  146.6 6.1 %collective-permute-done.19 = bf16[2,96,768]{2,1,0:T(8,128)(2,1)S(1)} collective-permute-done((bf16[2,96,768]{2,1,0:T(8,128)(2,1)S(1)}, bf16[2,96,768]{2,1,0:T(8,128)(2,1)S(1)}, u32[]{:S(2)}, u32[]{:S(2)}) %collective-permute-start.19) | collective-permute-done | bytes 294944 | tf_op jit(solution)/shard_map/ppermute | solution.py:531
  155.6 8.4 %attend.2 = (bf16[208,2304]{1,0:T(8,128)(2,1)}, f32[16,208]{1,0:T(8,128)}, bf16[4,208,256]{2,1,0:T(8,128)(2,1)}, f32[208,768]{1,0:T(8,128)}, bf16[208,768]{1,0:T(8,128)(2,1)}) custom-call(s32[4]{0:T(128)} %pad_add_fusion.info_ref, f32[208,768]{1,0:T(8,128)} %get-tuple-element.113.x_ref, f32[4,768]{1,0:T(4,128)} %get-tuple-element.114.gain_ref, ...), custom_call_target="tpu_custom_call" | custom-call | flops 10000000 | bytes 100000 | tf_op jit(solution)/shard_map/attend/pallas_call | solution.py:391
  164.0 9.0 %feed.2 = (bf16[4,208,768]{2,1,0:T(8,128)(2,1)}, f32[4,208,768]{2,1,0:T(8,128)}, f32[208,768]{1,0:T(8,128)}) custom-call(s32[4]{0:T(128)} %pad_add_fusion.info_ref, f32[208,768]{1,0:T(8,128)} %get-tuple-element.120.h1_ref, bf16[208,768]{1,0:T(8,128)(2,1)} %get-tuple-element.121.a2_ref, f32[4,768]{1,0:T(4,128)} %get-tuple-element.115.bias_ref, ...), custom_call_target="tpu_custom_call" | custom-call | flops 10000000 | bytes 100000 | tf_op jit(solution)/shard_map/feed/pallas_call | solution.py:411
  173.0 7.9 %attend.3 = (bf16[208,2304]{1,0:T(8,128)(2,1)}, f32[16,208]{1,0:T(8,128)}, bf16[4,208,256]{2,1,0:T(8,128)(2,1)}, f32[208,768]{1,0:T(8,128)}, bf16[208,768]{1,0:T(8,128)(2,1)}) custom-call(s32[4]{0:T(128)} %pad_add_fusion.info_ref, f32[208,768]{1,0:T(8,128)} %get-tuple-element.131.x_ref, f32[4,768]{1,0:T(4,128)} %get-tuple-element.114.gain_ref, ...), custom_call_target="tpu_custom_call" | custom-call | flops 10000000 | bytes 100000 | tf_op jit(solution)/shard_map/attend/pallas_call | solution.py:391
  180.9 8.5 %feed.3 = (bf16[4,208,768]{2,1,0:T(8,128)(2,1)}, f32[4,208,768]{2,1,0:T(8,128)}, f32[208,768]{1,0:T(8,128)}) custom-call(s32[4]{0:T(128)} %pad_add_fusion.info_ref, f32[208,768]{1,0:T(8,128)} %get-tuple-element.132.h1_ref, bf16[208,768]{1,0:T(8,128)(2,1)} %get-tuple-element.133.a2_ref, f32[4,768]{1,0:T(4,128)} %get-tuple-element.115.bias_ref, ...), custom_call_target="tpu_custom_call" | custom-call | flops 10000000 | bytes 100000 | tf_op jit(solution)/shard_map/feed/pallas_call | solution.py:411
  189.5 12.9 %feed_back.2 = (bf16[4,4,96,1536]{3,2,1,0:T(8,128)(2,1)}, bf16[4,4,96,1536]{3,2,1,0:T(8,128)(2,1)}, f32[4,1,768]{2,1,0:T(1,128)}, f32[208,768]{1,0:T(8,128)}, f32[8,768]{1,0:T(8,128)}) custom-call(s32[4]{0:T(128)} %pad_add_fusion.info_ref, f32[208,768]{1,0:T(8,128)} %get-tuple-element.135.g_ref, f32[208,768]{1,0:T(8,128)} %get-tuple-element.132.h1_ref, ...), custom_call_target="tpu_custom_call" | custom-call | flops 10000000 | bytes 100000 | tf_op jit(solution)/shard_map/feed_back/pallas_call | solution.py:436
  202.5 8.1 %collective-permute-done.21 = bf16[4,4,96,1536]{3,2,1,0:T(8,128)(2,1)S(1)} collective-permute-done((bf16[4,4,96,1536]{3,2,1,0:T(8,128)(2,1)}, bf16[4,4,96,1536]{3,2,1,0:T(8,128)(2,1)S(1)}, u32[]{:S(2)}, u32[]{:S(2)}) %collective-permute-start.21) | collective-permute-done | bytes 4718624 | tf_op jit(solution)/shard_map/ppermute | solution.py:531
  210.6 4.0 fusion.13
  215.3 13.7 %attend_back.2 = (bf16[4,8,96,768]{3,2,1,0:T(8,128)(2,1)}, f32[208,768]{1,0:T(8,128)}, f32[8,768]{1,0:T(8,128)}) custom-call(s32[4]{0:T(128)} %pad_add_fusion.info_ref, f32[208,768]{1,0:T(8,128)} %get-tuple-element.138.dh1_ref, f32[208,768]{1,0:T(8,128)} %get-tuple-element.131.x_ref, f32[4,768]{1,0:T(4,128)} %get-tuple-element.114.gain_ref, ...), custom_call_target="tpu_custom_call" | custom-call | flops 10000000 | bytes 100000 | tf_op jit(solution)/shard_map/attend_back/pallas_call | solution.py:457
  230.4 12.7 %feed_back.3 = (bf16[4,4,96,1536]{3,2,1,0:T(8,128)(2,1)}, bf16[4,4,96,1536]{3,2,1,0:T(8,128)(2,1)}, f32[4,1,768]{2,1,0:T(1,128)}, f32[208,768]{1,0:T(8,128)}, f32[8,768]{1,0:T(8,128)}) custom-call(s32[4]{0:T(128)} %pad_add_fusion.info_ref, f32[208,768]{1,0:T(8,128)} %get-tuple-element.144.g_ref, f32[208,768]{1,0:T(8,128)} %get-tuple-element.120.h1_ref, ...), custom_call_target="tpu_custom_call" | custom-call | flops 10000000 | bytes 100000 | tf_op jit(solution)/shard_map/feed_back/pallas_call | solution.py:436
  249.7 13.7 %attend_back.3 = (bf16[4,4,96,768]{3,2,1,0:T(8,128)(2,1)}, bf16[4,4,96,768]{3,2,1,0:T(8,128)(2,1)}, f32[1,197,768]{2,1,0:T(8,128)}, f32[8,768]{1,0:T(8,128)}) custom-call(s32[4]{0:T(128)} %pad_add_fusion.info_ref, f32[208,768]{1,0:T(8,128)} %get-tuple-element.149.dh1_ref, f32[208,768]{1,0:T(8,128)} %get-tuple-element.113.x_ref, ...), custom_call_target="tpu_custom_call" | custom-call | flops 10000000 | bytes 100000 | tf_op jit(solution)/shard_map/attend_back/pallas_call | solution.py:457
  263.4 3.1 fusion.11
  267.6 8.0 %collective-permute-done.39 = bf16[4,96,1536]{2,1,0:T(8,128)(2,1)S(1)} collective-permute-done((bf16[4,96,1536]{2,1,0:T(8,128)(2,1)}, bf16[4,96,1536]{2,1,0:T(8,128)(2,1)S(1)}, u32[]{:S(2)}, u32[]{:S(2)}) %collective-permute-start.39) | collective-permute-done | bytes 1179680 | tf_op jit(solution)/shard_map/ppermute | solution.py:531
  278.2 10.8 %collective-permute-done.26 = bf16[2,96,1536]{2,1,0:T(8,128)(2,1)S(1)} collective-permute-done((bf16[2,96,1536]{2,1,0:T(8,128)(2,1)S(1)}, bf16[2,96,1536]{2,1,0:T(8,128)(2,1)S(1)}, u32[]{:S(2)}, u32[]{:S(2)}) %collective-permute-start.26) | collective-permute-done | bytes 589856 | tf_op jit(solution)/shard_map/ppermute | solution.py:531
  306.7 27.2 %collective-permute-done.40 = bf16[2,96,1536]{2,1,0:T(8,128)(2,1)} collective-permute-done((bf16[2,96,1536]{2,1,0:T(8,128)(2,1)}, bf16[2,96,1536]{2,1,0:T(8,128)(2,1)}, u32[]{:S(2)}, u32[]{:S(2)}) %collective-permute-start.40) | collective-permute-done | bytes 589856 | tf_op jit(solution)/shard_map/ppermute | solution.py:535
  343.4 8.9 %collective-permute-done.28 = bf16[2,96,768]{2,1,0:T(8,128)(2,1)S(1)} collective-permute-done((bf16[2,96,768]{2,1,0:T(8,128)(2,1)S(1)}, bf16[2,96,768]{2,1,0:T(8,128)(2,1)S(1)}, u32[]{:S(2)}, u32[]{:S(2)}) %collective-permute-start.28) | collective-permute-done | bytes 294944 | tf_op jit(solution)/shard_map/ppermute | solution.py:531
  360.2 10.0 %collective-permute-done.31 = bf16[4,96,768]{2,1,0:T(8,128)(2,1)} collective-permute-done((bf16[4,96,768]{2,1,0:T(8,128)(2,1)S(1)}, bf16[4,96,768]{2,1,0:T(8,128)(2,1)}, u32[]{:S(2)}, u32[]{:S(2)}) %collective-permute-start.31) | collective-permute-done | bytes 589856 | tf_op jit(solution)/shard_map/ppermute | solution.py:531
  371.8 12.5 %reduce-scatter.2.cloned.1.call-done.refs_1_ = bf16[96,768]{1,0:T(8,128)(2,1)} async-done(((bf16[3072,768]{1,0:T(8,128)(2,1)}), bf16[96,768]{1,0:T(8,128)(2,1)}) %reduce-scatter.2.cloned.1.call-update) | async-done | bytes 147472 | tf_op jit(solution)/shard_map/reduce_scatter | solution.py:608
  387.4 9.9 %collective-permute-done.36 = bf16[2,96,1536]{2,1,0:T(8,128)(2,1)S(1)} collective-permute-done((bf16[2,96,1536]{2,1,0:T(8,128)(2,1)S(1)}, bf16[2,96,1536]{2,1,0:T(8,128)(2,1)S(1)}, u32[]{:S(2)}, u32[]{:S(2)}) %collective-permute-start.36) | collective-permute-done | bytes 589856 | tf_op jit(solution)/shard_map/ppermute | solution.py:535
  402.3 7.7 %collective-permute-done.37 = bf16[96,1536]{1,0:T(8,128)(2,1)S(1)} collective-permute-done((bf16[96,1536]{1,0:T(8,128)(2,1)S(1)}, bf16[96,1536]{1,0:T(8,128)(2,1)S(1)}, u32[]{:S(2)}, u32[]{:S(2)}) %collective-permute-start.37) | collective-permute-done | bytes 294944 | tf_op jit(solution)/shard_map/ppermute | solution.py:535
  410.9 5.1 %update.3 = (f32[2,96,768]{2,1,0:T(8,128)}, f32[2,96,768]{2,1,0:T(8,128)}, f32[2,96,768]{2,1,0:T(8,128)}, f32[2,96,768]{2,1,0:T(8,128)}, f32[2,96,768]{2,1,0:T(8...) custom-call(f32[96,1536]{1,0:T(8,128)} %fusion.16.refs_0_, ...), custom_call_target="tpu_custom_call" | custom-call | flops 10000000 | bytes 100000 | tf_op jit(solution)/shard_map/update/pallas_call | solution.py:558
  416.8 3.7 update.2
  (226 shorter events, 94.5 us)
Async XLA Ops:
  7.2 165.8 %all-gather.2.cloned.1.call-start = ((), (), s32[]{:S(2)}) async-start(), calls=%async_computation.1 | async-start | bytes 14598144 | tf_op jit(solution)/shard_map/all_gather | solution.py:603
  11.6 372.7 %reduce-scatter.2.cloned.1.call-start = ((), (), s32[]{:S(2)}) async-start(), calls=%async_computation.2 | async-start | bytes 4866048 | tf_op jit(solution)/shard_map/reduce_scatter | solution.py:608
  16.6 25.6 %collective-permute-start.1 = (bf16[2,96,768]{2,1,0:T(8,128)(2,1)S(1)}, bf16[2,96,768]{2,1,0:T(8,128)(2,1)S(1)}, u32[]{:S(2)}, u32[]{:S(2)}) collective-permute-start(bf16[2,96,768]{2,1,0:T(8,128)(2,1)S(1)} %pad_maximum_fusion.9), channel_id=1, source_target_pairs={{0,2},{1,3},{2,0},{3,1},{4,6},{5,7},{6,4},{7,5},{8,10},{9,11},{10,... | collective-permute-start | bytes 884744 | tf_op jit(solution)/shard_map/ppermute | solution.py:535
  26.6 25.5 %collective-permute-start.11 = (bf16[96,768]{1,0:T(8,128)(2,1)S(1)}, bf16[96,768]{1,0:T(8,128)(2,1)}, u32[]{:S(2)}, u32[]{:S(2)}) collective-permute-start(bf16[96,768]{1,0:T(8,128)(2,1)S(1)} %get-tuple-element.124), channel_id=1, source_target_pairs={{0,1},{1,0},{2,3},{3,2},{4,5},{5,4},{6,7},{7,6},{8,9},{9,8},{10,11... | collective-permute-start | bytes 442376 | tf_op jit(solution)/shard_map/ppermute | solution.py:535
  42.2 31.2 %collective-permute-start.2 = (bf16[4,96,768]{2,1,0:T(8,128)(2,1)S(1)}, bf16[4,96,768]{2,1,0:T(8,128)(2,1)S(1)}, u32[]{:S(2)}, u32[]{:S(2)}) collective-permute-start(bf16[4,96,768]{2,1,0:T(8,128)(2,1)S(1)} %pad_maximum_fusion.4), channel_id=1, source_target_pairs={{0,8},{4,12},{8,0},{12,4},{16,24},{20,28},{24,16},{28,20},{1,9},{5... | collective-permute-start | bytes 1769480 | tf_op jit(solution)/shard_map/ppermute | solution.py:531
  44.2 32.4 %collective-permute-start.3 = (bf16[4,96,768]{2,1,0:T(8,128)(2,1)S(1)}, bf16[4,96,768]{2,1,0:T(8,128)(2,1)S(1)}, u32[]{:S(2)}, u32[]{:S(2)}) collective-permute-start(bf16[4,96,768]{2,1,0:T(8,128)(2,1)S(1)} %pad_maximum_fusion.4), channel_id=1, source_target_pairs={{0,16},{4,20},{8,24},{12,28},{16,0},{20,4},{24,8},{28,12},{1,17},{... | collective-permute-start | bytes 1769480 | tf_op jit(solution)/shard_map/ppermute | solution.py:531
  44.4 27.9 %collective-permute-start.5 = (bf16[2,96,768]{2,1,0:T(8,128)(2,1)}, bf16[2,96,768]{2,1,0:T(8,128)(2,1)}, u32[]{:S(2)}, u32[]{:S(2)}) collective-permute-start(bf16[2,96,768]{2,1,0:T(8,128)(2,1)} %pad_maximum_fusion.10), channel_id=1, source_target_pairs={{0,2},{1,3},{2,0},{3,1},{4,6},{5,7},{6,4},{7,5},{8,10},{9,11},{10,... | collective-permute-start | bytes 884744 | tf_op jit(solution)/shard_map/ppermute | solution.py:535
  72.3 15.9 %collective-permute-start.12 = (bf16[2,96,768]{2,1,0:T(8,128)(2,1)S(1)}, bf16[2,96,768]{2,1,0:T(8,128)(2,1)S(1)}, u32[]{:S(2)}, u32[]{:S(2)}) collective-permute-start(bf16[2,96,768]{2,1,0:T(8,128)(2,1)S(1)} %pad_maximum_fusion.11), channel_id=1, source_target_pairs={{0,2},{1,3},{2,0},{3,1},{4,6},{5,7},{6,4},{7,5},{8,10},{9,11},{10,... | collective-permute-start | bytes 884744 | tf_op jit(solution)/shard_map/ppermute | solution.py:535
  73.4 31.7 %collective-permute-start.10 = (bf16[4,96,768]{2,1,0:T(8,128)(2,1)S(1)}, bf16[4,96,768]{2,1,0:T(8,128)(2,1)S(1)}, u32[]{:S(2)}, u32[]{:S(2)}) collective-permute-start(bf16[4,96,768]{2,1,0:T(8,128)(2,1)S(1)} %pad_maximum_fusion.5), channel_id=1, source_target_pairs={{0,16},{4,20},{8,24},{12,28},{16,0},{20,4},{24,8},{28,12},{1,17},{... | collective-permute-start | bytes 1769480 | tf_op jit(solution)/shard_map/ppermute | solution.py:531
  74.7 22.2 %collective-permute-start.9 = (bf16[4,96,768]{2,1,0:T(8,128)(2,1)S(1)}, bf16[4,96,768]{2,1,0:T(8,128)(2,1)S(1)}, u32[]{:S(2)}, u32[]{:S(2)}) collective-permute-start(bf16[4,96,768]{2,1,0:T(8,128)(2,1)S(1)} %pad_maximum_fusion.5), channel_id=1, source_target_pairs={{0,8},{4,12},{8,0},{12,4},{16,24},{20,28},{24,16},{28,20},{1,9},{5... | collective-permute-start | bytes 1769480 | tf_op jit(solution)/shard_map/ppermute | solution.py:531
  76.7 20.2 %collective-permute-start.6 = (bf16[2,96,768]{2,1,0:T(8,128)(2,1)S(1)}, bf16[2,96,768]{2,1,0:T(8,128)(2,1)S(1)}, u32[]{:S(2)}, u32[]{:S(2)}) collective-permute-start(bf16[2,96,768]{2,1,0:T(8,128)(2,1)S(1)} %slice.230), channel_id=1, source_target_pairs={{0,8},{4,12},{8,0},{12,4},{16,24},{20,28},{24,16},{28,20},{1,9},{5... | collective-permute-start | bytes 884744 | tf_op jit(solution)/shard_map/ppermute | solution.py:531
  77.1 21.7 %collective-permute-start.7 = (bf16[2,96,768]{2,1,0:T(8,128)(2,1)S(1)}, bf16[2,96,768]{2,1,0:T(8,128)(2,1)S(1)}, u32[]{:S(2)}, u32[]{:S(2)}) collective-permute-start(bf16[2,96,768]{2,1,0:T(8,128)(2,1)S(1)} %slice.231), channel_id=1, source_target_pairs={{0,16},{4,20},{8,24},{12,28},{16,0},{20,4},{24,8},{28,12},{1,17},{... | collective-permute-start | bytes 884744 | tf_op jit(solution)/shard_map/ppermute | solution.py:531
  96.9 40.5 %collective-permute-start.17 = (bf16[4,96,768]{2,1,0:T(8,128)(2,1)S(1)}, bf16[4,96,768]{2,1,0:T(8,128)(2,1)S(1)}, u32[]{:S(2)}, u32[]{:S(2)}) collective-permute-start(bf16[4,96,768]{2,1,0:T(8,128)(2,1)S(1)} %pad_maximum_fusion.6), channel_id=1, source_target_pairs={{0,16},{4,20},{8,24},{12,28},{16,0},{20,4},{24,8},{28,12},{1,17},{... | collective-permute-start | bytes 1769480 | tf_op jit(solution)/shard_map/ppermute | solution.py:531
  97.2 40.3 %collective-permute-start.16 = (bf16[4,96,768]{2,1,0:T(8,128)(2,1)S(1)}, bf16[4,96,768]{2,1,0:T(8,128)(2,1)S(1)}, u32[]{:S(2)}, u32[]{:S(2)}) collective-permute-start(bf16[4,96,768]{2,1,0:T(8,128)(2,1)S(1)} %pad_maximum_fusion.6), channel_id=1, source_target_pairs={{0,8},{4,12},{8,0},{12,4},{16,24},{20,28},{24,16},{28,20},{1,9},{5... | collective-permute-start | bytes 1769480 | tf_op jit(solution)/shard_map/ppermute | solution.py:531
  98.9 55.3 %collective-permute-start.8 = (bf16[4,4,96,768]{3,2,1,0:T(8,128)(2,1)S(1)}, bf16[4,4,96,768]{3,2,1,0:T(8,128)(2,1)S(1)}, u32[]{:S(2)}, u32[]{:S(2)}) collective-permute-start(bf16[4,4,96,768]{3,2,1,0:T(8,128)(2,1)S(1)} %bitcast.131), channel_id=1, source_target_pairs={{0,4},{4,0},{8,12},{12,8},{16,20},{20,16},{24,28},{28,24},{1,5},{5... | collective-permute-start | bytes 7077896 | tf_op jit(solution)/shard_map/ppermute | solution.py:531
  105.1 31.6 %collective-permute-start.13 = (bf16[2,96,768]{2,1,0:T(8,128)(2,1)S(1)}, bf16[2,96,768]{2,1,0:T(8,128)(2,1)S(1)}, u32[]{:S(2)}, u32[]{:S(2)}) collective-permute-start(bf16[2,96,768]{2,1,0:T(8,128)(2,1)S(1)} %slice.233), channel_id=1, source_target_pairs={{0,8},{4,12},{8,0},{12,4},{16,24},{20,28},{24,16},{28,20},{1,9},{5... | collective-permute-start | bytes 884744 | tf_op jit(solution)/shard_map/ppermute | solution.py:531
  106.0 33.1 %collective-permute-start.14 = (bf16[2,96,768]{2,1,0:T(8,128)(2,1)S(1)}, bf16[2,96,768]{2,1,0:T(8,128)(2,1)S(1)}, u32[]{:S(2)}, u32[]{:S(2)}) collective-permute-start(bf16[2,96,768]{2,1,0:T(8,128)(2,1)S(1)} %slice.234), channel_id=1, source_target_pairs={{0,16},{4,20},{8,24},{12,28},{16,0},{20,4},{24,8},{28,12},{1,17},{... | collective-permute-start | bytes 884744 | tf_op jit(solution)/shard_map/ppermute | solution.py:531
  139.9 24.1 %collective-permute-start.15 = (bf16[4,4,96,768]{3,2,1,0:T(8,128)(2,1)}, bf16[4,4,96,768]{3,2,1,0:T(8,128)(2,1)}, u32[]{:S(2)}, u32[]{:S(2)}) collective-permute-start(bf16[4,4,96,768]{3,2,1,0:T(8,128)(2,1)} %bitcast.15.rest_0_), channel_id=1, source_target_pairs={{0,4},{4,0},{8,12},{12,8},{16,20},{20,16},{24,28},{28,24},{1,5},{5... | collective-permute-start | bytes 7077896 | tf_op jit(solution)/shard_map/ppermute | solution.py:531
  243.1 20.2 %collective-permute-start.24 = (bf16[4,4,96,1536]{3,2,1,0:T(8,128)(2,1)}, bf16[4,4,96,1536]{3,2,1,0:T(8,128)(2,1)}, u32[]{:S(2)}, u32[]{:S(2)}) collective-permute-start(bf16[4,4,96,1536]{3,2,1,0:T(8,128)(2,1)} %get-tuple-element.158), channel_id=1, source_target_pairs={{0,4},{4,0},{8,12},{12,8},{16,20},{20,16},{24,28},{28,24},{1,5},{5... | collective-permute-start | bytes 14155784 | tf_op jit(solution)/shard_map/ppermute | solution.py:531
  247.8 27.8 %collective-permute-start.39 = (bf16[4,96,1536]{2,1,0:T(8,128)(2,1)}, bf16[4,96,1536]{2,1,0:T(8,128)(2,1)S(1)}, u32[]{:S(2)}, u32[]{:S(2)}) collective-permute-start(bf16[4,96,1536]{2,1,0:T(8,128)(2,1)} %pad_maximum_fusion.3), channel_id=1, source_target_pairs={{0,16},{4,20},{8,24},{12,28},{16,0},{20,4},{24,8},{28,12},{1,17},{... | collective-permute-start | bytes 3538952 | tf_op jit(solution)/shard_map/ppermute | solution.py:531
  249.1 27.3 %collective-permute-start.38 = (bf16[4,96,1536]{2,1,0:T(8,128)(2,1)S(1)}, bf16[4,96,1536]{2,1,0:T(8,128)(2,1)S(1)}, u32[]{:S(2)}, u32[]{:S(2)}) collective-permute-start(bf16[4,96,1536]{2,1,0:T(8,128)(2,1)S(1)} %pad_maximum_fusion.2), channel_id=1, source_target_pairs={{0,8},{4,12},{8,0},{12,4},{16,24},{20,28},{24,16},{28,20},{1,9},{5... | collective-permute-start | bytes 3538952 | tf_op jit(solution)/shard_map/ppermute | solution.py:531
  266.4 22.5 %collective-permute-start.26 = (bf16[2,96,1536]{2,1,0:T(8,128)(2,1)S(1)}, bf16[2,96,1536]{2,1,0:T(8,128)(2,1)S(1)}, u32[]{:S(2)}, u32[]{:S(2)}) collective-permute-start(bf16[2,96,1536]{2,1,0:T(8,128)(2,1)S(1)} %get-tuple-element.163), channel_id=1, source_target_pairs={{0,8},{4,12},{8,0},{12,4},{16,24},{20,28},{24,16},{28,20},{1,9},{5... | collective-permute-start | bytes 1769480 | tf_op jit(solution)/shard_map/ppermute | solution.py:531
  267.4 21.6 %collective-permute-start.27 = (bf16[2,96,1536]{2,1,0:T(8,128)(2,1)S(1)}, bf16[2,96,1536]{2,1,0:T(8,128)(2,1)S(1)}, u32[]{:S(2)}, u32[]{:S(2)}) collective-permute-start(bf16[2,96,1536]{2,1,0:T(8,128)(2,1)S(1)} %get-tuple-element.164), channel_id=1, source_target_pairs={{0,16},{4,20},{8,24},{12,28},{16,0},{20,4},{24,8},{28,12},{1,17},{... | collective-permute-start | bytes 1769480 | tf_op jit(solution)/shard_map/ppermute | solution.py:531
  276.3 63.8 %collective-permute-start.25 = (bf16[4,4,96,768]{3,2,1,0:T(8,128)(2,1)}, bf16[4,4,96,768]{3,2,1,0:T(8,128)(2,1)}, u32[]{:S(2)}, u32[]{:S(2)}) collective-permute-start(bf16[4,4,96,768]{3,2,1,0:T(8,128)(2,1)} %get-tuple-element.159), channel_id=1, source_target_pairs={{0,4},{4,0},{8,12},{12,8},{16,20},{20,16},{24,28},{28,24},{1,5},{5... | collective-permute-start | bytes 7077896 | tf_op jit(solution)/shard_map/ppermute | solution.py:531
  293.4 40.6 %collective-permute-start.35 = (bf16[4,96,1536]{2,1,0:T(8,128)(2,1)}, bf16[4,96,1536]{2,1,0:T(8,128)(2,1)S(1)}, u32[]{:S(2)}, u32[]{:S(2)}) collective-permute-start(bf16[4,96,1536]{2,1,0:T(8,128)(2,1)} %pad_maximum_fusion.1), channel_id=1, source_target_pairs={{0,16},{4,20},{8,24},{12,28},{16,0},{20,4},{24,8},{28,12},{1,17},{... | collective-permute-start | bytes 3538952 | tf_op jit(solution)/shard_map/ppermute | solution.py:531
  293.9 40.1 %collective-permute-start.34 = (bf16[4,96,1536]{2,1,0:T(8,128)(2,1)}, bf16[4,96,1536]{2,1,0:T(8,128)(2,1)}, u32[]{:S(2)}, u32[]{:S(2)}) collective-permute-start(bf16[4,96,1536]{2,1,0:T(8,128)(2,1)} %pad_maximum_fusion), channel_id=1, source_target_pairs={{0,8},{4,12},{8,0},{12,4},{16,24},{20,28},{24,16},{28,20},{1,9},{5... | collective-permute-start | bytes 3538952 | tf_op jit(solution)/shard_map/ppermute | solution.py:531
  297.5 36.4 %collective-permute-start.40 = (bf16[2,96,1536]{2,1,0:T(8,128)(2,1)}, bf16[2,96,1536]{2,1,0:T(8,128)(2,1)}, u32[]{:S(2)}, u32[]{:S(2)}) collective-permute-start(bf16[2,96,1536]{2,1,0:T(8,128)(2,1)} %slice.403), channel_id=1, source_target_pairs={{0,2},{1,3},{2,0},{3,1},{4,6},{5,7},{6,4},{7,5},{8,10},{9,11},{10,... | collective-permute-start | bytes 1769480 | tf_op jit(solution)/shard_map/ppermute | solution.py:535
  299.7 34.2 %collective-permute-start.42 = (f32[16,768]{1,0:T(8,128)S(1)}, f32[16,768]{1,0:T(8,128)S(1)}, u32[]{:S(2)}, u32[]{:S(2)}) collective-permute-start(f32[16,768]{1,0:T(8,128)S(1)} %constant_dynamic-update-slice_fusion.15), channel_id=1, source_target_pairs={{0,1},{1,0},{2,3},{3,2},{4,5},{5,4},{6,7},{7,6},{8,9},{9,8},{10,11... | collective-permute-start | bytes 147464 | tf_op jit(solution)/shard_map/ppermute | solution.py:535
  343.3 16.0 %collective-permute-start.41 = (bf16[96,1536]{1,0:T(8,128)(2,1)S(1)}, bf16[96,1536]{1,0:T(8,128)(2,1)S(1)}, u32[]{:S(2)}, u32[]{:S(2)}) collective-permute-start(bf16[96,1536]{1,0:T(8,128)(2,1)S(1)} %fusion.24), channel_id=1, source_target_pairs={{0,1},{1,0},{2,3},{3,2},{4,5},{5,4},{6,7},{7,6},{8,9},{9,8},{10,11... | collective-permute-start | bytes 884744 | tf_op jit(solution)/shard_map/ppermute | solution.py:535
  354.8 15.3 %collective-permute-start.31 = (bf16[4,96,768]{2,1,0:T(8,128)(2,1)S(1)}, bf16[4,96,768]{2,1,0:T(8,128)(2,1)}, u32[]{:S(2)}, u32[]{:S(2)}) collective-permute-start(bf16[4,96,768]{2,1,0:T(8,128)(2,1)S(1)} %pad_maximum_fusion.8), channel_id=1, source_target_pairs={{0,16},{4,20},{8,24},{12,28},{16,0},{20,4},{24,8},{28,12},{1,17},{... | collective-permute-start | bytes 1769480 | tf_op jit(solution)/shard_map/ppermute | solution.py:531
  359.0 38.3 %collective-permute-start.36 = (bf16[2,96,1536]{2,1,0:T(8,128)(2,1)S(1)}, bf16[2,96,1536]{2,1,0:T(8,128)(2,1)S(1)}, u32[]{:S(2)}, u32[]{:S(2)}) collective-permute-start(bf16[2,96,1536]{2,1,0:T(8,128)(2,1)S(1)} %slice.404), channel_id=1, source_target_pairs={{0,2},{1,3},{2,0},{3,1},{4,6},{5,7},{6,4},{7,5},{8,10},{9,11},{10,... | collective-permute-start | bytes 1769480 | tf_op jit(solution)/shard_map/ppermute | solution.py:535
  386.5 15.6 %collective-permute-start.32 = (bf16[2,96,768]{2,1,0:T(8,128)(2,1)S(1)}, bf16[2,96,768]{2,1,0:T(8,128)(2,1)S(1)}, u32[]{:S(2)}, u32[]{:S(2)}) collective-permute-start(bf16[2,96,768]{2,1,0:T(8,128)(2,1)S(1)} %slice.405), channel_id=1, source_target_pairs={{0,2},{1,3},{2,0},{3,1},{4,6},{5,7},{6,4},{7,5},{8,10},{9,11},{10,... | collective-permute-start | bytes 884744 | tf_op jit(solution)/shard_map/ppermute | solution.py:535
  (48 other events, 639.3 us)
Sparse Core Ops, SparseCore 0:
  11.7 143.1 all-gather.1
  249.8 134.4 reduce-scatter.1
